TPU v7x, 256 devices: a whole 4x4x8 slice. The times are simulated.
256 devices in a mesh: replica: 16 (over z, core), fsdp: 16 (over y, x).
Axes of the slice: x: 4, y: 4, z: 8, core: 2. Of those that a mesh axis runs over, the one named last changes fastest.
Arguments:
- grad_pair: bfloat16 [16, 2, 1024, 8192], P('replica', None, 'fsdp'), may hold values from -6 to 6
- error_pair: float32 [16, 2, 1024, 8192], P('replica', None, 'fsdp'), may hold values from -4 to 4
- basis_pair: float32 [2, 32, 8192], P(None, None, 'fsdp'), may hold values from -0.0625 to 0.0625
Outputs:
- residual: float32 [16, 2, 1024, 8192], P('replica', None, 'fsdp')
- basis_next: float32 [2, 32, 8192], P(None, None, 'fsdp')
All inputs are finite; a program needn't handle non-finite values.
Results may differ from a plain program's by a relative error of at most 0.0003.
Values sent between devices are 32-bit elements; how exact they have to be, the bound alone decides.
No kernel may reach another device: no remote copies, remote signals or barrier semaphores. Data moves between devices by JAX's collectives and lax.ppermute only.
A program may use at most 64 MiB of HBM per device.

v0:
```python
import jax
import jax.numpy as jnp
from jax import lax
from jax.sharding import PartitionSpec as P


def gram_of(factor):
    return jnp.einsum("mrk,mrl->mkl", factor, factor, precision=lax.Precision.HIGHEST)


def on_device(grad_pair, error_pair, basis_pair):
    high = lax.Precision.HIGHEST
    merged = grad_pair[0].astype(jnp.float32) + error_pair[0]
    basis_whole = lax.all_gather(basis_pair, "fsdp", axis=2, tiled=True)
    local_left = jnp.einsum("mrc,mkc->mrk", merged, basis_whole, precision=high)
    summed_left = lax.psum(local_left, "replica")
    gram = lax.psum(gram_of(summed_left), "fsdp")
    factor_low = jnp.linalg.cholesky(gram)
    orth = lax.linalg.triangular_solve(
        factor_low, summed_left, left_side=False, lower=True, transpose_a=True
    )
    terms = jnp.einsum("mrk,mrc->mkc", orth, merged, precision=high)
    replicas = lax.axis_size("replica")
    right_basis = lax.psum(terms, ("replica", "fsdp")) / replicas
    column_count = basis_pair.shape[2]
    new_shard = lax.dynamic_slice_in_dim(
        right_basis, lax.axis_index("fsdp") * column_count, column_count, 2
    )
    update = jnp.einsum("mrk,mkc->mrc", orth, right_basis, precision=high)
    residual = (merged - update)[None]
    return (residual, new_shard)


def solution(mesh):
    in_specs = (
        P("replica", None, "fsdp", None),
        P("replica", None, "fsdp", None),
        P(None, None, "fsdp"),
    )
    out_specs = (P("replica", None, "fsdp", None), P(None, None, "fsdp"))
    return jax.shard_map(
        on_device, mesh=mesh, in_specs=in_specs, out_specs=out_specs, check_vma=False
    )
```

profile of v0, /device:TPU:1, one launch (start us, length us, event | category | flops | bytes accessed | tf_op | source)
XLA Modules:
  0.0 480.2 jit_solution(4171784187578000691)
XLA Ops:
  7.2 0.0 all-gather.2.cloned.1.call-start
  7.2 0.7 all-gather.2.cloned.1.call-update
  7.9 0.0 all-reduce.2.cloned.1.call-start
  8.0 0.0 copy-start.1
  8.0 55.4 %all-gather.2.cloned.1.call-done = f32[2,32,8192]{2,1,0:T(8,128)} async-done(((f32[2,32,512]{2,1,0:T(8,128)}), f32[2,32,8192]{2,1,0:T(8,128)}) %all-gather.2.cloned.1.call-update) | async-done | bytes 2097168 | tf_op jit(solution)/shard_map/all_gather | solution.py:14
  63.4 7.3 %fusion.3 = f32[2,64,32]{1,2,0:T(8,128)S(1)} fusion(f32[2,32,8192]{2,1,0:T(8,128)} %all-gather.2.cloned.1.call-done, f32[1,2,64,8192]{3,2,1,0:T(8,128)} %param.4, bf16[1,2,64,8192]{3,2,1,0:T(8,128)(2,1)} %param.3), kind=kOutput, calls=%fused_computation.4 | convolution fusion | flops 404750336 | bytes 8404992 | tf_op jit(solution)/shard_map/mrc,mkc->mrk/dot_general | solution.py:15
  70.7 45.5 %psum.21 = f32[2,64,32]{1,2,0:T(8,128)S(1)} all-reduce(f32[2,64,32]{1,2,0:T(8,128)S(1)} %fusion.3), channel_id=1, replica_groups=mesh['replica'=16,'fsdp'=16] {'replica'}, use_global_device_ids=true, to_apply=%region_0.0 | all-reduce | flops 4096 | bytes 32768 | tf_op jit(solution)/shard_map/psum | solution.py:16
  116.2 0.2 fusion.8
  116.3 58.2 %psum.22 = f32[2,32,32]{1,2,0:T(8,128)S(1)} all-reduce(f32[2,32,32]{1,2,0:T(8,128)S(1)} %fusion.8), channel_id=1, replica_groups=mesh['replica'=16,'fsdp'=16] {'fsdp'}, use_global_device_ids=true, to_apply=%region_1.0 | all-reduce | flops 2048 | bytes 16384 | tf_op jit(solution)/shard_map/psum | solution.py:17
  174.6 0.1 copy.9
  174.7 5.9 %custom-call.7 = f32[2,32,32]{2,1,0:T(8,128)S(1)} custom-call(f32[2,32,32]{2,1,0:T(8,128)S(1)} %fusion.7), custom_call_target="Cholesky" | custom-call | tf_op jit(solution)/shard_map/jit(cholesky)/cholesky | solution.py:18
  180.6 0.1 compare_reduce_fusion
  180.7 0.1 select_bitcast_fusion
  180.8 4.9 %custom-call.8 = f32[2,1,32,32]{2,3,1,0:T(8,128)S(1)} custom-call(f32[2,1,32,32]{3,2,1,0:T(8,128)S(1)} %select_bitcast_fusion), custom_call_target="InvertDiagBlocksLowerTriangular" | custom-call | tf_op jit(solution)/shard_map/triangular_solve | solution.py:19
  185.7 0.3 fusion.5
  185.9 0.0 copy-done.1
  185.9 5.8 %fusion.1 = f32[2,32,8192]{2,1,0:T(8,128)} fusion(f32[2,64,32]{1,2,0:T(8,128)S(1)} %fusion.5, f32[1,2,64,8192]{3,2,1,0:T(8,128)} %param.4, bf16[1,2,64,8192]{3,2,1,0:T(8,128)(2,1)S(1)} %copy-done.1), kind=kOutput, calls=%fused_computation.2 | convolution fusion | flops 404750336 | bytes 8404992 | tf_op jit(solution)/shard_map/mrk,mrc->mkc/dot_general | solution.py:22
  191.8 0.0 all-reduce.2.cloned.1.call-update
  191.8 271.2 %all-reduce.2.cloned.1.call-done = f32[2,32,8192]{2,1,0:T(8,128)} async-done(((f32[2,32,8192]{2,1,0:T(8,128)}), f32[2,32,8192]{2,1,0:T(8,128)}) %all-reduce.2.cloned.1.call-update) | async-done | bytes 2097168 | tf_op jit(solution)/shard_map/psum | solution.py:24
  463.0 0.0 copy-start
  463.0 1.9 broadcast_multiply_fusion
  464.9 0.7 constant_dynamic-slice_fusion
  465.6 0.2 copy-done
  465.8 7.6 %fusion = f32[1,2,64,8192]{3,2,1,0:T(8,128)} fusion(f32[2,64,32]{1,2,0:T(8,128)S(1)} %fusion.5, f32[1,2,64,8192]{3,2,1,0:T(8,128)S(1)} %copy-done, bf16[1,2,64,8192]{3,2,1,0:T(8,128)(2,1)S(1)} %copy-done.1, f32[2,32,8192]{2,1,0:T(8,128)} %all-reduce.2.cloned.1.call-done), kind=kOutput, calls=%fused_computation.1 | convolution fusion | flops 406323200 | bytes 12599296 | tf_op jit(solution)/shard_map/mrk,mkc->mrc/dot_general | solution.py:29
  (4 shorter events, 0.1 us)
Async XLA Ops:
  7.2 56.2 %all-gather.2.cloned.1.call-start = ((), (), s32[]{:S(2)}) async-start(), calls=%async_computation | async-start | bytes 2228224 | tf_op jit(solution)/shard_map/all_gather | solution.py:14
  7.9 455.1 %all-reduce.2.cloned.1.call-start = ((), (), s32[]{:S(2)}) async-start(), calls=%async_computation.1 | async-start | bytes 4194304 | tf_op jit(solution)/shard_map/psum | solution.py:24
  8.0 178.0 %copy-start.1 = (bf16[1,2,64,8192]{3,2,1,0:T(8,128)(2,1)S(1)}, bf16[1,2,64,8192]{3,2,1,0:T(8,128)(2,1)}, u32[]{:S(2)}) copy-start(bf16[1,2,64,8192]{3,2,1,0:T(8,128)(2,1)} %param.3) | copy-start | bytes 6291460
  463.0 2.8 copy-start
Sparse Core Ops, SparseCore 0:
  10.4 52.8 all-gather.1
  191.9 271.0 all-reduce.1
where the time goes:
time: 481 us; the launch traced here: 480 us
  waiting for transfers between devices  327 us (68%)
  blocking collectives  104 us (22%)
  matrix products  21.2 us (4%)
  between operations  14.1 us (3%)
  other arithmetic  12.9 us (3%)
    psum x1, waiting for transfers between devices, on_device(): right_basis = lax.psum(terms, ('replica', 'fsdp')) / replicas  271 us
    psum x1, blocking collectives, on_device(): gram = lax.psum(gram_of(summed_left), 'fsdp')  58.2 us
    all_gather x1, waiting for transfers between devices, on_device(): basis_whole = lax.all_gather(basis_pair, 'fsdp', axis=2, tiled=True)  55.4 us
    psum x1, blocking collectives, on_device(): summed_left = lax.psum(local_left, 'replica')  45.5 us
  transfers between devices with their start and end apart: 2, of which 2 were waited for; matrix products, arithmetic and copies ran while one was open for 0% of the time, Pallas kernels for 0%

commit v1 on v0

v1 whole, which is shorter than its diff:
```python
import jax
import jax.numpy as jnp
from jax import lax
from jax.sharding import Mesh, PartitionSpec as P

HIGH = lax.Precision.HIGHEST
F = ("y", "x")


def swap(value):
    return lax.ppermute(value, "core", [(0, 1), (1, 0)])


def spread(value, axes):
    count = lax.axis_size(axes)
    copies = jnp.broadcast_to(value[None], (count,) + value.shape)
    return lax.all_to_all(copies, axes, 0, 0)


def on_device(grad_pair, error_pair, basis_pair):
    core = lax.axis_index("core")
    replicas = lax.axis_size("core") * lax.axis_size("z")
    merged = grad_pair[0].astype(jnp.float32) + error_pair[0]
    rows, width = merged.shape[1:]
    rank, part = basis_pair.shape[1:]
    shards = width // part
    own = lax.dynamic_index_in_dim(merged, core, 0, False)
    other = lax.dynamic_index_in_dim(merged, 1 - core, 0, False)
    pair_sum = own + swap(other)
    own_basis = lax.dynamic_index_in_dim(basis_pair, core, 0, False)
    basis = spread(own_basis, F)
    pieces = pair_sum.reshape(rows, shards, part)
    left = jnp.einsum("rfc,fkc->rk", pieces, basis, precision=HIGH)
    left = jnp.sum(spread(left, "z"), axis=0)
    gram = jnp.einsum("rk,rl->kl", left, left, precision=HIGH)
    terms = jnp.einsum("rk,rfc->fkc", left, pieces, precision=HIGH)
    gram_rows = gram.reshape(rank // 8, 8, rank).transpose(1, 0, 2)
    gram_rows = jnp.pad(gram_rows, ((0, 0), (0, 0), (0, part * 8 // rank - rank)))
    gram_rows = jnp.broadcast_to(gram_rows.reshape(1, 8, part), (shards, 8, part))
    sent = jnp.concatenate([terms, gram_rows], axis=1)
    summed = jnp.sum(lax.all_to_all(sent, F, 0, 0), axis=0)
    gram = summed[rank:].reshape(8, rank // 8, -1)[:, :, :rank]
    gram = gram.transpose(1, 0, 2).reshape(rank, rank)
    chunk = jnp.sum(spread(summed[:rank], "z"), axis=0)
    lower = jnp.linalg.cholesky(gram)
    inverse = lax.linalg.triangular_solve(
        lower, jnp.eye(rank, dtype=jnp.float32), left_side=True, lower=True
    )
    orth = jnp.einsum("rk,lk->rl", left, inverse, precision=HIGH)
    weights = jnp.einsum("rk,kl->rl", orth, inverse, precision=HIGH) / replicas
    shard = jnp.einsum("kl,lc->kc", inverse, chunk, precision=HIGH) / replicas
    whole = spread(chunk, F)
    other_whole = swap(whole)
    other_weights = swap(weights)
    other_shard = swap(shard)

    def leftover(values, factor, right):
        update = jnp.einsum("rk,fkc->rfc", factor, right, precision=HIGH)
        return values - update.reshape(rows, width)

    mine = leftover(own, weights, whole)
    theirs = leftover(other, other_weights, other_whole)

    def ordered(first, second):
        pair = jnp.stack([first, second])
        return jnp.where(core == 0, pair, pair[::-1])

    return (ordered(mine, theirs)[None], ordered(shard, other_shard))


def solution(mesh):
    grid = Mesh(mesh.devices.reshape(8, 2, 4, 4), ("z", "core", "y", "x"))
    replica = ("z", "core")
    in_specs = (
        P(replica, None, F, None),
        P(replica, None, F, None),
        P(None, None, F),
    )
    out_specs = (P(replica, None, F, None), P(None, None, F))
    return jax.shard_map(
        on_device, mesh=grid, in_specs=in_specs, out_specs=out_specs, check_vma=False
    )
```

time: 481 us -> 142 us (0.30)
  waiting for transfers between devices: 327 us -> 36.5 us
  blocking collectives: 104 us -> 36.8 us
  starting transfers between devices: 0.08 us -> 21.5 us
  local copies, waits for them, and re-layouts: 0.99 us -> 15.3 us
  between operations: 14.1 us -> 0.91 us
  matrix products: 21.2 us -> 8.79 us
  other arithmetic: 12.9 us -> 22.1 us
    psum x1 -> x0, waiting for transfers between devices: 271 us -> none  [on_device(): right_basis = lax.psum(terms, ('replica', 'fsdp')) / replicas]
    psum x2 -> x0, blocking collectives: 104 us -> none  [the longest x1 58.2 us: on_device(): gram = lax.psum(gram_of(summed_left), 'fsdp')]
    all_gather x1 -> x0, waiting for transfers between devices: 55.4 us -> none  [on_device(): basis_whole = lax.all_gather(basis_pair, 'fsdp', axis=2, tiled=True)]
    all_to_all x0 -> x2, blocking collectives: none -> 36.8 us  [the longest x1 21.5 us: on_device(): summed = jnp.sum(lax.all_to_all(sent, F, 0, 0), axis=0)]
    all_to_all x0 -> x3, waiting for transfers between devices: none -> 35.4 us  [spread(): return lax.all_to_all(copies, axes, 0, 0)]
    dot_general x4 -> x8, matrix products: 20.9 us -> 8.58 us  [the longest x2 4.9 us: leftover(): update = jnp.einsum('rk,fkc->rfc', factor, right, precision=HIGH)]
    all_to_all x0 -> x3, starting transfers between devices: none -> 12.2 us  [spread(): return lax.all_to_all(copies, axes, 0, 0)]
    ppermute x0 -> x4, starting transfers between devices: none -> 9.3 us  [swap(): return lax.ppermute(value, 'core', [(0, 1), (1, 0)])]
  transfers between devices with their start and end apart: 2 -> 7, of which waited for: 2 -> 4; matrix products, arithmetic and copies ran while one was open for 0% -> 13% of each run, Pallas kernels for 0% -> 0%
where the time goes in v1:
time: 142 us
  blocking collectives  36.8 us (26%)
  waiting for transfers between devices  36.5 us (26%)
  other arithmetic  22.1 us (16%)
  starting transfers between devices  21.5 us (15%)
  local copies, waits for them, and re-layouts  15.3 us (11%)
  matrix products  8.79 us (6%)
    all_to_all x3, waiting for transfers between devices, spread(): return lax.all_to_all(copies, axes, 0, 0)  35.4 us
    all_to_all x1, blocking collectives, on_device(): summed = jnp.sum(lax.all_to_all(sent, F, 0, 0), axis=0)  21.5 us
    all_to_all x1, blocking collectives, spread(): return lax.all_to_all(copies, axes, 0, 0)  15.3 us
    all_to_all x3, starting transfers between devices, spread(): return lax.all_to_all(copies, axes, 0, 0)  12.2 us
    ppermute x4, starting transfers between devices, swap(): return lax.ppermute(value, 'core', [(0, 1), (1, 0)])  9.3 us
    add x1, other arithmetic, on_device(): merged = grad_pair[0].astype(jnp.float32) + error_pair[0]  5.33 us
    dot_general x2, local copies, waits for them, and re-layouts, leftover(): update = jnp.einsum('rk,fkc->rfc', factor, right, precision=HIGH)  5.14 us
    dot_general x2, matrix products, leftover(): update = jnp.einsum('rk,fkc->rfc', factor, right, precision=HIGH)  4.9 us
  transfers between devices with their start and end apart: 7, of which 4 were waited for; matrix products, arithmetic and copies ran while one was open for 13% of the time, Pallas kernels for 0%

profile of v1, /device:TPU:1, one launch (start us, length us, event | category | flops | bytes accessed | tf_op | source)
XLA Modules:
  0.0 141.8 jit_solution(16145703328625186366)
XLA Ops:
  0.6 0.0 copy-start
  0.7 5.3 %convert_add_fusion = f32[1,2,64,8192]{3,2,1,0:T(8,128)} fusion(f32[1,2,64,8192]{3,2,1,0:T(8,128)} %param.4, bf16[1,2,64,8192]{3,2,1,0:T(8,128)(2,1)} %param.3), kind=kLoop, calls=%fused_computation.3 | loop fusion | flops 2097152 | bytes 10485760 | tf_op jit(solution)/shard_map/add | solution.py:23
  6.0 1.7 %dynamic-slice_bitcast_fusion = f32[64,8192]{1,0:T(8,128)S(1)} fusion(f32[1,2,64,8192]{3,2,1,0:T(8,128)} %convert_add_fusion, s32[]{:T(128)S(6)} %select_n.31), kind=kLoop, calls=%fused_computation.13 | loop fusion | bytes 4194308 | tf_op jit(solution)/shard_map/jit(dynamic_index_in_dim)/squeeze | solution.py:28
  7.7 3.3 %collective-permute-start = (f32[64,8192]{1,0:T(8,128)S(1)}, f32[64,8192]{1,0:T(8,128)}, u32[]{:S(2)}, u32[]{:S(2)}) collective-permute-start(f32[64,8192]{1,0:T(8,128)S(1)} %dynamic-slice_bitcast_fusion), channel_id=1, source_target_pairs={{0,16},{16,0},{1,17},{17,1},{2,18},{18,2},{3,19},{19,3},{4,20},{20... | collective-permute-start | bytes 6291464 | tf_op jit(solution)/shard_map/ppermute | solution.py:11
  11.1 1.1 broadcast_in_dim.19
  12.2 5.0 %all-to-all-start = ((f32[16,32,512]{2,1,0:T(8,128)}), f32[16,32,512]{2,1,0:T(8,128)S(1)}, u32[]{:S(2)}, u32[]{:S(2)}) async-start(f32[16,32,512]{2,1,0:T(8,128)} %broadcast_in_dim.19), calls=%async_computation | async-start | bytes 2097152 | tf_op jit(solution)/shard_map/all_to_all | solution.py:17
  17.2 2.4 %bitcast_add_fusion = f32[64,8192]{1,0:T(8,128)S(1)} fusion(f32[64,8192]{1,0:T(8,128)} %collective-permute-done, f32[1,2,64,8192]{3,2,1,0:T(8,128)} %convert_add_fusion, s32[]{:T(128)S(6)} %select_n.30), kind=kLoop, calls=%fused_computation.9 | loop fusion | flops 524288 | bytes 6291460 | tf_op jit(solution)/shard_map/add | solution.py:29
  19.7 14.9 %all-to-all-done = f32[16,32,512]{2,1,0:T(8,128)S(1)} async-done(((f32[16,32,512]{2,1,0:T(8,128)}), f32[16,32,512]{2,1,0:T(8,128)S(1)}, u32[]{:S(2)}, u32[]{:S(2)}) %all-to-all-start) | async-done | bytes 1048608 | tf_op jit(solution)/shard_map/all_to_all | solution.py:17
  34.6 1.7 %fusion.10 = f32[64,32]{0,1:T(8,128)S(1)} fusion(f32[16,32,512]{2,1,0:T(8,128)S(1)} %all-to-all-done, f32[8,16,8,512]{3,2,1,0:T(8,128)S(1)} %bitcast.78), kind=kOutput, calls=%fused_computation.17 | convolution fusion | flops 201326592 | bytes 3153920 | tf_op jit(solution)/shard_map/rfc,fkc->rk/dot_general | solution.py:33
  36.3 0.1 reshape.52
  36.5 15.3 %all_to_all.25 = f32[8,1,2048]{2,1,0:T(1,128)S(1)} all-to-all(f32[8,1,2048]{2,1,0:T(1,128)S(1)} %reshape.52), channel_id=1, replica_groups=mesh['z'=8,'core'=2,'y'=4,'x'=4] {'z'}, dimensions={0} | all-to-all | bytes 131072 | tf_op jit(solution)/shard_map/all_to_all | solution.py:17
  51.8 0.5 broadcast.54
  52.3 0.8 reduce.6
  53.1 0.1 reshape.53
  53.2 0.1 convolution_bitcast_fusion
  53.4 1.2 fusion.7
  54.6 0.1 pad_maximum_fusion.1
  54.8 21.5 %all_to_all.26 = f32[16,40,512]{2,1,0:T(8,128)S(1)} all-to-all(f32[16,40,512]{2,1,0:T(8,128)S(1)} %pad_maximum_fusion.1), channel_id=1, replica_groups=mesh['z'=8,'core'=2,'y'=4,'x'=4] {'y','x'}, dimensions={0} | all-to-all | bytes 2621440 | tf_op jit(solution)/shard_map/all_to_all | solution.py:41
  76.2 0.1 reduce_sum.28
  76.3 0.8 broadcast_in_dim.43
  77.2 3.5 %all-to-all-start.3 = ((f32[8,32,512]{2,1,0:T(8,128)}), f32[8,32,512]{2,1,0:T(8,128)S(1)}, u32[]{:S(2)}, u32[]{:S(2)}) async-start(f32[8,32,512]{2,1,0:T(8,128)} %broadcast_in_dim.43), calls=%async_computation.3 | async-start | bytes 1048576 | tf_op jit(solution)/shard_map/all_to_all | solution.py:17
  80.7 0.1 copy.20
  80.8 14.0 %all-to-all-done.3 = f32[8,32,512]{2,1,0:T(8,128)S(1)} async-done(((f32[8,32,512]{2,1,0:T(8,128)}), f32[8,32,512]{2,1,0:T(8,128)S(1)}, u32[]{:S(2)}, u32[]{:S(2)}) %all-to-all-start.3) | async-done | bytes 524320 | tf_op jit(solution)/shard_map/all_to_all | solution.py:17
  94.8 1.1 broadcast_in_dim.44
  95.9 3.7 %all-to-all-start.4 = ((f32[16,32,512]{2,1,0:T(8,128)}), f32[16,32,512]{2,1,0:T(8,128)S(1)}, u32[]{:S(2)}, u32[]{:S(2)}) async-start(f32[16,32,512]{2,1,0:T(8,128)} %broadcast_in_dim.44), calls=%async_computation.4 | async-start | bytes 2097152 | tf_op jit(solution)/shard_map/all_to_all | solution.py:17
  99.6 2.9 %cholesky.17 = f32[32,32]{1,0:T(8,128)S(1)} custom-call(f32[32,32]{1,0:T(8,128)S(1)} %fusion.21), custom_call_target="Cholesky" | custom-call | tf_op jit(solution)/shard_map/jit(cholesky)/cholesky | solution.py:45
  102.6 0.6 compare_reduce_fusion
  103.2 0.7 fusion.13
  103.9 2.4 %custom-call.6 = f32[1,32,32]{1,2,0:T(8,128)S(1)} custom-call(f32[1,32,32]{2,1,0:T(8,128)S(1)} %fusion.13), custom_call_target="InvertDiagBlocksLowerTriangular" | custom-call | tf_op jit(solution)/shard_map/triangular_solve | solution.py:46
  106.3 0.2 fusion.19
  106.5 0.1 fusion.24
  106.7 6.5 %all-to-all-done.4 = f32[16,32,512]{2,1,0:T(8,128)S(1)} async-done(((f32[16,32,512]{2,1,0:T(8,128)}), f32[16,32,512]{2,1,0:T(8,128)S(1)}, u32[]{:S(2)}, u32[]{:S(2)}) %all-to-all-start.4) | async-done | bytes 1048608 | tf_op jit(solution)/shard_map/all_to_all | solution.py:17
  113.1 5.1 %collective-permute-start.2 = (f32[16,32,512]{2,1,0:T(8,128)S(1)}, f32[16,32,512]{2,1,0:T(8,128)}, u32[]{:S(2)}, u32[]{:S(2)}) collective-permute-start(f32[16,32,512]{2,1,0:T(8,128)S(1)} %all-to-all-done.4), channel_id=1, source_target_pairs={{0,16},{16,0},{1,17},{17,1},{2,18},{18,2},{3,19},{19,3},{4,20},{20... | collective-permute-start | bytes 3145736 | tf_op jit(solution)/shard_map/ppermute | solution.py:11
  118.3 0.2 convolution_multiply_fusion
  118.5 0.1 collective-permute-start.3
  118.6 0.2 convolution_multiply_fusion.1
  118.8 0.8 collective-permute-start.1
  119.5 1.1 collective-permute-done.3
  120.6 0.7 reverse_select_fusion.1
  121.3 1.8 %fusion.17 = f32[64,16,512]{2,0,1:T(8,128)S(1)} fusion(f32[16,32,512]{2,1,0:T(8,128)S(1)} %all-to-all-done.4, f32[64,32]{0,1:T(8,128)S(1)} %convolution_multiply_fusion.1), kind=kOutput, calls=%fused_computation.30 | convolution fusion | flops 201326592 | bytes 3153920 | tf_op jit(solution)/shard_map/rk,fkc->rfc/dot_general | solution.py:58
  123.2 2.6 %copy.21 = f32[64,16,512]{2,1,0:T(8,128)} copy(f32[64,16,512]{2,0,1:T(8,128)S(1)} %fusion.17) | data formatting | bytes 4194304 | tf_op jit(solution)/shard_map/rk,fkc->rfc/dot_general | solution.py:58
  125.7 1.7 %reshape.46 = f32[1,64,8192]{2,1,0:T(8,128)S(1)} reshape(f32[64,16,512]{2,1,0:T(8,128)} %copy.21) | data formatting | bytes 4194304 | tf_op jit(solution)/shard_map/reshape | solution.py:59
  127.5 3.1 %fusion.15 = f32[64,16,512]{2,0,1:T(8,128)S(1)} fusion(f32[16,32,512]{2,1,0:T(8,128)} %collective-permute-done.2, f32[64,32]{0,1:T(8,128)S(1)} %collective-permute-done.1), kind=kOutput, calls=%fused_computation.28 | convolution fusion | flops 201326592 | bytes 3153920 | tf_op jit(solution)/shard_map/rk,fkc->rfc/dot_general | solution.py:58
  130.6 2.6 %copy.22 = f32[64,16,512]{2,1,0:T(8,128)} copy(f32[64,16,512]{2,0,1:T(8,128)S(1)} %fusion.15) | data formatting | bytes 4194304 | tf_op jit(solution)/shard_map/rk,fkc->rfc/dot_general | solution.py:58
  133.2 2.7 %reshape.47 = f32[1,64,8192]{2,1,0:T(8,128)} reshape(f32[64,16,512]{2,1,0:T(8,128)} %copy.22) | data formatting | bytes 4194304 | tf_op jit(solution)/shard_map/reshape | solution.py:59
  135.9 3.3 %bitcast_subtract_fusion.1 = (f32[1,64,8192]{2,1,0:T(8,128)S(1)}, f32[1,64,8192]{2,1,0:T(8,128)S(1)}) fusion(f32[1,64,8192]{2,1,0:T(8,128)S(1)} %reshape.46, f32[1,2,64,8192]{3,2,1,0:T(8,128)} %convert_add_fusion, s32[]{:T(128)S(6)} %select_n.30, f32[1,64,8192]{2,1,0:T(8,128)} %reshape.47, s32[]{:T(128)S(6)} %select_n.31), kind=kLoop, calls=%fused_computation.10 | loop fusion | flops 1048576 | bytes 12582920 | tf_op jit(solution)/shard_map/sub | solution.py:59
  139.2 0.3 pad_maximum_fusion
  139.4 2.4 %fusion = f32[1,2,64,8192]{3,2,1,0:T(8,128)} fusion(f32[2,64,8192]{2,1,0:T(8,128)S(1)} %pad_maximum_fusion, pred[]{:T(512)S(6)} %eq.2), kind=kLoop, calls=%fused_computation.1 | loop fusion | flops 1048576 | bytes 8388609 | tf_op jit(solution)/shard_map/broadcast_in_dim | solution.py:68
  (16 shorter events, 0.2 us)
Async XLA Ops:
  0.6 10.4 %copy-start = (f32[2,32,512]{2,1,0:T(8,128)S(1)}, f32[2,32,512]{2,1,0:T(8,128)}, u32[]{:S(2)}) copy-start(f32[2,32,512]{2,1,0:T(8,128)} %param.5) | copy-start | bytes 393220
  7.7 9.5 %collective-permute-start = (f32[64,8192]{1,0:T(8,128)S(1)}, f32[64,8192]{1,0:T(8,128)}, u32[]{:S(2)}, u32[]{:S(2)}) collective-permute-start(f32[64,8192]{1,0:T(8,128)S(1)} %dynamic-slice_bitcast_fusion), channel_id=1, source_target_pairs={{0,16},{16,0},{1,17},{17,1},{2,18},{18,2},{3,19},{19,3},{4,20},{20... | collective-permute-start | bytes 6291464 | tf_op jit(solution)/shard_map/ppermute | solution.py:11
  12.2 22.4 %all-to-all-start = ((f32[16,32,512]{2,1,0:T(8,128)}), f32[16,32,512]{2,1,0:T(8,128)S(1)}, u32[]{:S(2)}, u32[]{:S(2)}) async-start(f32[16,32,512]{2,1,0:T(8,128)} %broadcast_in_dim.19), calls=%async_computation | async-start | bytes 2097152 | tf_op jit(solution)/shard_map/all_to_all | solution.py:17
  77.2 17.6 %all-to-all-start.3 = ((f32[8,32,512]{2,1,0:T(8,128)}), f32[8,32,512]{2,1,0:T(8,128)S(1)}, u32[]{:S(2)}, u32[]{:S(2)}) async-start(f32[8,32,512]{2,1,0:T(8,128)} %broadcast_in_dim.43), calls=%async_computation.3 | async-start | bytes 1048576 | tf_op jit(solution)/shard_map/all_to_all | solution.py:17
  95.9 17.2 %all-to-all-start.4 = ((f32[16,32,512]{2,1,0:T(8,128)}), f32[16,32,512]{2,1,0:T(8,128)S(1)}, u32[]{:S(2)}, u32[]{:S(2)}) async-start(f32[16,32,512]{2,1,0:T(8,128)} %broadcast_in_dim.44), calls=%async_computation.4 | async-start | bytes 2097152 | tf_op jit(solution)/shard_map/all_to_all | solution.py:17
  113.1 14.4 %collective-permute-start.2 = (f32[16,32,512]{2,1,0:T(8,128)S(1)}, f32[16,32,512]{2,1,0:T(8,128)}, u32[]{:S(2)}, u32[]{:S(2)}) collective-permute-start(f32[16,32,512]{2,1,0:T(8,128)S(1)} %all-to-all-done.4), channel_id=1, source_target_pairs={{0,16},{16,0},{1,17},{17,1},{2,18},{18,2},{3,19},{19,3},{4,20},{20... | collective-permute-start | bytes 3145736 | tf_op jit(solution)/shard_map/ppermute | solution.py:11
  118.5 2.2 %collective-permute-start.3 = (f32[32,512]{1,0:T(8,128)S(1)}, f32[32,512]{1,0:T(8,128)S(1)}, u32[]{:S(2)}, u32[]{:S(2)}) collective-permute-start(f32[32,512]{1,0:T(8,128)S(1)} %convolution_multiply_fusion), channel_id=1, source_target_pairs={{0,16},{16,0},{1,17},{17,1},{2,18},{18,2},{3,19},{19,3},{4,20},{20... | collective-permute-start | bytes 196616 | tf_op jit(solution)/shard_map/ppermute | solution.py:11
  118.8 8.7 %collective-permute-start.1 = (f32[64,32]{0,1:T(8,128)S(1)}, f32[64,32]{0,1:T(8,128)S(1)}, u32[]{:S(2)}, u32[]{:S(2)}) collective-permute-start(f32[64,32]{0,1:T(8,128)S(1)} %convolution_multiply_fusion.1), channel_id=1, source_target_pairs={{0,16},{16,0},{1,17},{17,1},{2,18},{18,2},{3,19},{19,3},{4,20},{20... | collective-permute-start | bytes 24584 | tf_op jit(solution)/shard_map/ppermute | solution.py:11

commit v2 on v1

v2 whole, which is shorter than its diff:
```python
import jax
import jax.numpy as jnp
from jax import lax
from jax.experimental import pallas as pl
from jax.experimental.pallas import tpu as pltpu
from jax.sharding import Mesh, PartitionSpec as P

HIGH = lax.Precision.HIGHEST
F = ("y", "x")


def swap(value):
    return lax.ppermute(value, "core", [(0, 1), (1, 0)])


def spread(value, axes):
    count = lax.axis_size(axes)
    copies = jnp.broadcast_to(value[None], (count,) + value.shape)
    return lax.all_to_all(copies, axes, 0, 0)


def inverse_kernel(gram_ref, out_ref):
    rank = gram_ref.shape[0]
    row_id = lax.broadcasted_iota(jnp.int32, (rank, rank), 0)
    col_id = lax.broadcasted_iota(jnp.int32, (rank, rank), 1)
    eye = jnp.where(row_id == col_id, 1.0, 0.0).astype(jnp.float32)
    state = jnp.concatenate([gram_ref[...], eye], axis=1)
    below = lax.broadcasted_iota(jnp.int32, state.shape, 0)
    for k in range(rank):
        scale = 1.0 / jnp.sqrt(state[k : k + 1, k : k + 1])
        row = state[k : k + 1, :] * scale
        factor = state[:, k : k + 1] * scale
        state = jnp.where(
            below > k, state - factor * row, jnp.where(below == k, row, state)
        )
    out_ref[...] = state[:, rank:]


def inverse_of(gram):
    return pl.pallas_call(
        inverse_kernel,
        out_shape=jax.ShapeDtypeStruct(gram.shape, jnp.float32),
        name="cholesky_inverse",
    )(gram)


def split(value):
    high = value.astype(jnp.bfloat16)
    return high, (value - high.astype(jnp.float32)).astype(jnp.bfloat16)


def residual_kernel(which_ref, grad_ref, error_ref, weights_ref, right_ref, *rest):
    out_ref = rest[-1]
    high, low = split(weights_ref[...])
    weights = jnp.concatenate([high, low, high], axis=1)
    pieces, _, part = right_ref.shape
    for piece in range(pieces):
        columns = pl.ds(piece * part, part)
        high, low = split(right_ref[piece])
        right = jnp.concatenate([high, high, low], axis=0)
        update = jnp.dot(weights, right, preferred_element_type=jnp.float32)
        merged = grad_ref[0, 0, :, columns].astype(jnp.float32) + error_ref[0, 0, :, columns]
        out_ref[0, 0, :, columns] = merged - update


def residual_of(which, grad_pair, error_pair, weights, right, earlier=None):
    steps = 4
    _, _, rows, width = grad_pair.shape
    shards, rank, part = right.shape
    big = pl.BlockSpec((1, 1, rows, width // steps), lambda i, w: (0, w[0], 0, i))
    in_specs = [
        big,
        big,
        pl.BlockSpec((rows, rank), lambda i, w: (0, 0)),
        pl.BlockSpec((shards // steps, rank, part), lambda i, w: (i, 0, 0)),
    ]
    operands = [which, grad_pair, error_pair, weights, right]
    aliases = {}
    if earlier is not None:
        in_specs.append(pl.BlockSpec(memory_space=pl.ANY))
        operands.append(earlier)
        aliases = {5: 0}
    return pl.pallas_call(
        residual_kernel,
        grid_spec=pltpu.PrefetchScalarGridSpec(
            num_scalar_prefetch=1, grid=(steps,), in_specs=in_specs, out_specs=big
        ),
        out_shape=jax.ShapeDtypeStruct(error_pair.shape, jnp.float32),
        input_output_aliases=aliases,
        cost_estimate=pl.CostEstimate(
            flops=6 * rows * rank * width, bytes_accessed=11 * rows * width, transcendentals=0
        ),
        name="residual",
    )(*operands)


def on_device(grad_pair, error_pair, basis_pair):
    core = lax.axis_index("core")
    replicas = lax.axis_size("core") * lax.axis_size("z")
    rows, width = grad_pair.shape[2:]
    rank, part = basis_pair.shape[1:]
    shards = width // part

    def merged(index):
        grad = lax.dynamic_index_in_dim(grad_pair[0], index, 0, False)
        return grad.astype(jnp.float32) + lax.dynamic_index_in_dim(error_pair[0], index, 0, False)

    own_basis = lax.dynamic_index_in_dim(basis_pair, core, 0, False)
    basis = spread(own_basis, F)
    pair_sum = merged(core) + swap(merged(1 - core))
    pieces = pair_sum.reshape(rows, shards, part)
    left = jnp.einsum("fkc,rfc->kr", basis, pieces, precision=HIGH)
    half = rank // 2
    packed = jnp.concatenate([left[:half], left[half:]], axis=1)
    packed = jnp.sum(spread(packed, "z"), axis=0)
    left = jnp.concatenate([packed[:, :rows], packed[:, rows:]], axis=0)
    terms = jnp.einsum("kr,rfc->fkc", left, pieces, precision=HIGH)
    sums = jnp.sum(lax.all_to_all(terms, F, 0, 0), axis=0)
    gram = jnp.einsum("kr,lr->kl", left, left, precision=HIGH)
    gram = jnp.concatenate(jnp.split(gram, 4), axis=1)
    gram = jnp.sum(spread(gram, F), axis=0)
    gram = jnp.concatenate(jnp.split(gram, 4, axis=1), axis=0)
    chunk = jnp.sum(spread(sums, "z"), axis=0)
    inverse = inverse_of(gram)
    orth = jnp.einsum("lk,kr->lr", inverse, left, precision=HIGH)
    weights = jnp.einsum("lr,lk->rk", orth, inverse, precision=HIGH) / replicas
    shard = jnp.einsum("kl,lc->kc", inverse, chunk, precision=HIGH) / replicas
    whole = spread(chunk, F)
    other_whole = swap(whole)
    other_weights = swap(weights)
    other_shard = swap(shard)
    which = core.astype(jnp.int32).reshape(1)
    residual = residual_of(which, grad_pair, error_pair, weights, whole)
    residual = residual_of(
        1 - which, grad_pair, error_pair, other_weights, other_whole, residual
    )
    pair = jnp.stack([shard, other_shard])
    return (residual, jnp.where(core == 0, pair, pair[::-1]))


def solution(mesh):
    grid = Mesh(mesh.devices.reshape(8, 2, 4, 4), ("z", "core", "y", "x"))
    replica = ("z", "core")
    in_specs = (
        P(replica, None, F, None),
        P(replica, None, F, None),
        P(None, None, F),
    )
    out_specs = (P(replica, None, F, None), P(None, None, F))
    return jax.shard_map(
        on_device, mesh=grid, in_specs=in_specs, out_specs=out_specs, check_vma=False
    )
```

time: 142 us -> 141 us (level)
  other arithmetic: 22.1 us -> 6.4 us
  Pallas kernels: 0 us -> 13.7 us
  waiting for transfers between devices: 36.5 us -> 47.9 us
  local copies, waits for them, and re-layouts: 15.3 us -> 5.43 us
  starting transfers between devices: 21.5 us -> 25.7 us
  matrix products: 8.79 us -> 5.87 us
  blocking collectives: 36.8 us -> 34.3 us
    pallas_call x0 -> x3, Pallas kernels: none -> 13.7 us  [the longest x2 9.28 us: residual_of(): pl.pallas_call(residual_kernel, grid_spec=pltpu.PrefetchScalarGridSpec(nu...]
    all_to_all x3 -> x4, waiting for transfers between devices: 35.4 us -> 47.9 us  [spread(): return lax.all_to_all(copies, axes, 0, 0)]
    another operation x7 -> x1, other arithmetic: 6.97 us -> 0.01 us  [on_device(): pair = jnp.stack([shard, other_shard])]
    dot_general x2 -> x0, local copies, waits for them, and re-layouts: 5.14 us -> none  [leftover(): update = jnp.einsum('rk,fkc->rfc', factor, right, precision=HIGH)]
    reshape x5 -> x0, local copies, waits for them, and re-layouts: 4.54 us -> none  [the longest x2 4.46 us: leftover(): return values - update.reshape(rows, width)]
    all_to_all x3 -> x4, starting transfers between devices: 12.2 us -> 15.7 us  [spread(): return lax.all_to_all(copies, axes, 0, 0)]
    dot_general x7 -> x5, matrix products: 8.38 us -> 4.95 us  [the longest x1 1.77 us: on_device(): left = jnp.einsum('fkc,rfc->kr', basis, pieces, precision=HIGH)]
    sub x1 -> x0, other arithmetic: 3.28 us -> none  [leftover(): return values - update.reshape(rows, width)]
  transfers between devices with their start and end apart: 7 -> 8, of which waited for: 4 -> 4; matrix products, arithmetic and copies ran while one was open for 13% -> 6% of each run, Pallas kernels for 0% -> 6%
where the time goes in v2:
time: 141 us; the launch traced here: 140 us
  waiting for transfers between devices  47.9 us (34%)
  blocking collectives  34.3 us (24%)
  starting transfers between devices  25.7 us (18%)
  Pallas kernels  13.7 us (10%)
  other arithmetic  6.4 us (5%)
  matrix products  5.87 us (4%)
  local copies, waits for them, and re-layouts  5.43 us (4%)
    all_to_all x4, waiting for transfers between devices, spread(): return lax.all_to_all(copies, axes, 0, 0)  47.9 us
    all_to_all x1, blocking collectives, on_device(): sums = jnp.sum(lax.all_to_all(terms, F, 0, 0), axis=0)  19 us
    all_to_all x4, starting transfers between devices, spread(): return lax.all_to_all(copies, axes, 0, 0)  15.7 us
    all_to_all x1, blocking collectives, spread(): return lax.all_to_all(copies, axes, 0, 0)  15.3 us
    ppermute x4, starting transfers between devices, swap(): return lax.ppermute(value, 'core', [(0, 1), (1, 0)])  10 us
    pallas_call x2, Pallas kernels, residual_of(): pl.pallas_call(residual_kernel, grid_spec=pltpu.PrefetchScalarGridSpec(nu...  9.28 us
    pallas_call x1, Pallas kernels, inverse_of(): pl.pallas_call(inverse_kernel, out_shape=jax.ShapeDtypeStruct(gram.shape,...  4.46 us
    broadcast_in_dim x6, local copies, waits for them, and re-layouts, spread(): copies = jnp.broadcast_to(value[None], (count,) + value.shape)  3.7 us
  transfers between devices with their start and end apart: 8, of which 4 were waited for; matrix products, arithmetic and copies ran while one was open for 6% of the time, Pallas kernels for 6%

profile of v2, /device:TPU:1, one launch (start us, length us, event | category | flops | bytes accessed | tf_op | source)
XLA Modules:
  0.0 140.2 jit_solution(8043704760827111160)
XLA Ops:
  0.6 0.0 copy-start
  0.6 2.1 %add_bitcast_fusion = f32[64,8192]{1,0:T(8,128)S(1)} fusion(f32[1,2,64,8192]{3,2,1,0:T(8,128)} %error_ref.3, s32[]{:T(128)S(6)} %select_n.21, bf16[1,2,64,8192]{3,2,1,0:T(8,128)(2,1)} %grad_ref.3), kind=kLoop, calls=%fused_computation.5 | loop fusion | flops 1048576 | bytes 5242884 | tf_op jit(solution)/shard_map/add | solution.py:106
  2.7 3.3 %collective-permute-start = (f32[64,8192]{1,0:T(8,128)S(1)}, f32[64,8192]{1,0:T(8,128)}, u32[]{:S(2)}, u32[]{:S(2)}) collective-permute-start(f32[64,8192]{1,0:T(8,128)S(1)} %add_bitcast_fusion), channel_id=1, source_target_pairs={{0,16},{16,0},{1,17},{17,1},{2,18},{18,2},{3,19},{19,3},{4,20},{20... | collective-permute-start | bytes 6291464 | tf_op jit(solution)/shard_map/ppermute | solution.py:13
  6.1 0.0 copy-done
  6.1 1.1 broadcast_in_dim.13
  7.2 5.0 %all-to-all-start = ((f32[16,32,512]{2,1,0:T(8,128)}), f32[16,32,512]{2,1,0:T(8,128)S(1)}, u32[]{:S(2)}, u32[]{:S(2)}) async-start(f32[16,32,512]{2,1,0:T(8,128)} %broadcast_in_dim.13), calls=%async_computation | async-start | bytes 2097152 | tf_op jit(solution)/shard_map/all_to_all | solution.py:19
  12.2 0.0 collective-permute-done
  12.2 2.8 %bitcast_add_fusion = f32[64,8192]{1,0:T(8,128)S(1)} fusion(f32[64,8192]{1,0:T(8,128)} %collective-permute-done, f32[1,2,64,8192]{3,2,1,0:T(8,128)} %error_ref.3, s32[]{:T(128)S(6)} %select_n.20, bf16[1,2,64,8192]{3,2,1,0:T(8,128)(2,1)} %grad_ref.3), kind=kLoop, calls=%fused_computation.4 | loop fusion | flops 1572864 | bytes 7340036 | tf_op jit(solution)/shard_map/add | solution.py:110
  15.0 14.6 %all-to-all-done = f32[16,32,512]{2,1,0:T(8,128)S(1)} async-done(((f32[16,32,512]{2,1,0:T(8,128)}), f32[16,32,512]{2,1,0:T(8,128)S(1)}, u32[]{:S(2)}, u32[]{:S(2)}) %all-to-all-start) | async-done | bytes 1048608 | tf_op jit(solution)/shard_map/all_to_all | solution.py:19
  29.6 1.8 %fusion.9 = f32[32,64]{1,0:T(8,128)S(1)} fusion(f32[16,32,512]{2,1,0:T(8,128)S(1)} %all-to-all-done, f32[8,16,8,512]{3,2,1,0:T(8,128)S(1)} %bitcast.32), kind=kOutput, calls=%fused_computation.11 | convolution fusion | flops 201326592 | bytes 3153920 | tf_op jit(solution)/shard_map/fkc,rfc->kr/dot_general | solution.py:112
  31.3 0.1 pad_maximum_fusion.6
  31.4 15.3 %all_to_all.30 = f32[8,16,128]{2,1,0:T(8,128)S(1)} all-to-all(f32[8,16,128]{2,1,0:T(8,128)S(1)} %broadcast_in_dim.14), channel_id=1, replica_groups=mesh['z'=8,'core'=2,'y'=4,'x'=4] {'z'}, dimensions={0} | all-to-all | bytes 131072 | tf_op jit(solution)/shard_map/all_to_all | solution.py:19
  46.8 0.1 fusion.20
  46.8 1.2 fusion.6
  48.1 19.0 %all_to_all.31 = f32[16,32,512]{2,1,0:T(8,128)S(1)} all-to-all(f32[16,32,512]{2,1,0:T(8,128)S(1)} %fusion.6), channel_id=1, replica_groups=mesh['z'=8,'core'=2,'y'=4,'x'=4] {'y','x'}, dimensions={0} | all-to-all | bytes 2097152 | tf_op jit(solution)/shard_map/all_to_all | solution.py:118
  67.1 0.1 reduce_sum.38
  67.2 0.9 broadcast_in_dim.16
  68.0 3.5 %all-to-all-start.4 = ((f32[8,32,512]{2,1,0:T(8,128)}), f32[8,32,512]{2,1,0:T(8,128)S(1)}, u32[]{:S(2)}, u32[]{:S(2)}) async-start(f32[8,32,512]{2,1,0:T(8,128)} %broadcast_in_dim.16), calls=%async_computation.4 | async-start | bytes 1048576 | tf_op jit(solution)/shard_map/all_to_all | solution.py:19
  71.5 0.1 fusion.14
  71.7 0.1 pad_maximum_fusion.7
  71.8 14.1 %all-to-all-done.4 = f32[8,32,512]{2,1,0:T(8,128)S(1)} async-done(((f32[8,32,512]{2,1,0:T(8,128)}), f32[8,32,512]{2,1,0:T(8,128)S(1)}, u32[]{:S(2)}, u32[]{:S(2)}) %all-to-all-start.4) | async-done | bytes 524320 | tf_op jit(solution)/shard_map/all_to_all | solution.py:19
  85.9 0.6 broadcast_in_dim.15
  86.5 3.5 %all-to-all-start.2 = ((f32[16,8,128]{2,1,0:T(8,128)}), f32[16,8,128]{2,1,0:T(8,128)S(1)}, u32[]{:S(2)}, u32[]{:S(2)}) async-start(f32[16,8,128]{2,1,0:T(8,128)} %broadcast_in_dim.15), calls=%async_computation.2 | async-start | bytes 131072 | tf_op jit(solution)/shard_map/all_to_all | solution.py:19
  90.1 6.4 %all-to-all-done.2 = f32[16,8,128]{2,1,0:T(8,128)S(1)} async-done(((f32[16,8,128]{2,1,0:T(8,128)}), f32[16,8,128]{2,1,0:T(8,128)S(1)}, u32[]{:S(2)}, u32[]{:S(2)}) %all-to-all-start.2) | async-done | bytes 65568 | tf_op jit(solution)/shard_map/all_to_all | solution.py:19
  96.5 1.1 broadcast_in_dim.17
  97.6 3.7 %all-to-all-start.5 = ((f32[16,32,512]{2,1,0:T(8,128)}), f32[16,32,512]{2,1,0:T(8,128)S(1)}, u32[]{:S(2)}, u32[]{:S(2)}) async-start(f32[16,32,512]{2,1,0:T(8,128)} %broadcast_in_dim.17), calls=%async_computation.5 | async-start | bytes 2097152 | tf_op jit(solution)/shard_map/all_to_all | solution.py:19
  101.3 0.1 fusion.21
  101.4 12.8 %all-to-all-done.5.right_ref = f32[16,32,512]{2,1,0:T(8,128)S(1)} async-done(((f32[16,32,512]{2,1,0:T(8,128)}), f32[16,32,512]{2,1,0:T(8,128)S(1)}, u32[]{:S(2)}, u32[]{:S(2)}) %all-to-all-start.5) | async-done | bytes 1048608 | tf_op jit(solution)/shard_map/all_to_all | solution.py:19
  114.1 0.0 copy-start.1
  114.1 6.0 %collective-permute-start.2 = (f32[16,32,512]{2,1,0:T(8,128)S(1)}, f32[16,32,512]{2,1,0:T(8,128)S(1)}, u32[]{:S(2)}, u32[]{:S(2)}) collective-permute-start(f32[16,32,512]{2,1,0:T(8,128)S(1)} %all-to-all-done.5.right_ref), channel_id=1, source_target_pairs={{0,16},{16,0},{1,17},{17,1},{2,18},{18,2},{3,19},{19,3},{4,20},{20... | collective-permute-start | bytes 3145736 | tf_op jit(solution)/shard_map/ppermute | solution.py:13
  120.2 0.6 pad_maximum_fusion.2.gram_ref
  120.8 4.5 %cholesky_inverse.1 = f32[32,32]{1,0:T(8,128)} custom-call(f32[32,32]{1,0:T(8,128)} %pad_maximum_fusion.2.gram_ref), custom_call_target="tpu_custom_call" | custom-call | tf_op jit(solution)/shard_map/cholesky_inverse/pallas_call | solution.py:40
  125.2 0.8 fusion.13
  126.1 0.9 convolution_multiply_fusion
  127.0 0.1 collective-permute-start.3
  127.2 1.0 convolution_multiply_fusion.1.weights_ref
  128.1 0.0 copy-start.3
  128.1 0.5 collective-permute-start.1
  128.7 0.0 collective-permute-done.3
  128.7 0.7 reverse_select_fusion
  129.4 0.0 copy-done.1
  129.4 0.0 copy-done.3
  129.4 4.6 %residual.2.rest_0_ = f32[1,2,64,8192]{3,2,1,0:T(8,128)} custom-call(s32[1]{0:T(128)} %bitcast.which_ref, bf16[1,2,64,8192]{3,2,1,0:T(8,128)(2,1)} %grad_ref.3, f32[1,2,64,8192]{3,2,1,0:T(8,128)} %error_ref.3, f32[64,32]{1,0:T(8,128)} %copy-done.3, f32[16,32,512]{2,1,0:T(8,128)} %copy-done.1), custom_call_target="tpu_custom_call" | custom-call | flops 100663296 | bytes 5767168 | tf_op jit(solution)/shard_map/residual/pallas_call | solution.py:83
  134.0 0.0 collective-permute-done.1.weights_ref
  134.0 0.0 collective-permute-done.2.right_ref
  134.0 0.6 copy-done.4
  134.6 1.0 copy-done.2
  135.6 4.6 %residual.3 = f32[1,2,64,8192]{3,2,1,0:T(8,128)} custom-call(s32[1]{0:T(128)S(6)} %sub.6.which_ref, bf16[1,2,64,8192]{3,2,1,0:T(8,128)(2,1)} %grad_ref.3, f32[1,2,64,8192]{3,2,1,0:T(8,128)} %error_ref.3, f32[64,32]{1,0:T(8,128)} %copy-done.4, f32[16,32,512]{2,1,0:T(8,128)} %copy-done.2, ...), custom_call_target="tpu_custom_call", output_to_operand_aliasing={{}: (5, {})} | custom-call | flops 100663296 | bytes 5767168 | tf_op jit(solution)/shard_map/residual/pallas_call | solution.py:83
  (10 shorter events, 0.1 us)
Async XLA Ops:
  0.6 5.4 %copy-start = (f32[2,32,512]{2,1,0:T(8,128)S(1)}, f32[2,32,512]{2,1,0:T(8,128)}, u32[]{:S(2)}) copy-start(f32[2,32,512]{2,1,0:T(8,128)} %param.5) | copy-start | bytes 393220
  2.7 9.5 %collective-permute-start = (f32[64,8192]{1,0:T(8,128)S(1)}, f32[64,8192]{1,0:T(8,128)}, u32[]{:S(2)}, u32[]{:S(2)}) collective-permute-start(f32[64,8192]{1,0:T(8,128)S(1)} %add_bitcast_fusion), channel_id=1, source_target_pairs={{0,16},{16,0},{1,17},{17,1},{2,18},{18,2},{3,19},{19,3},{4,20},{20... | collective-permute-start | bytes 6291464 | tf_op jit(solution)/shard_map/ppermute | solution.py:13
  7.2 22.4 %all-to-all-start = ((f32[16,32,512]{2,1,0:T(8,128)}), f32[16,32,512]{2,1,0:T(8,128)S(1)}, u32[]{:S(2)}, u32[]{:S(2)}) async-start(f32[16,32,512]{2,1,0:T(8,128)} %broadcast_in_dim.13), calls=%async_computation | async-start | bytes 2097152 | tf_op jit(solution)/shard_map/all_to_all | solution.py:19
  68.0 17.9 %all-to-all-start.4 = ((f32[8,32,512]{2,1,0:T(8,128)}), f32[8,32,512]{2,1,0:T(8,128)S(1)}, u32[]{:S(2)}, u32[]{:S(2)}) async-start(f32[8,32,512]{2,1,0:T(8,128)} %broadcast_in_dim.16), calls=%async_computation.4 | async-start | bytes 1048576 | tf_op jit(solution)/shard_map/all_to_all | solution.py:19
  86.5 10.0 %all-to-all-start.2 = ((f32[16,8,128]{2,1,0:T(8,128)}), f32[16,8,128]{2,1,0:T(8,128)S(1)}, u32[]{:S(2)}, u32[]{:S(2)}) async-start(f32[16,8,128]{2,1,0:T(8,128)} %broadcast_in_dim.15), calls=%async_computation.2 | async-start | bytes 131072 | tf_op jit(solution)/shard_map/all_to_all | solution.py:19
  97.6 16.5 %all-to-all-start.5 = ((f32[16,32,512]{2,1,0:T(8,128)}), f32[16,32,512]{2,1,0:T(8,128)S(1)}, u32[]{:S(2)}, u32[]{:S(2)}) async-start(f32[16,32,512]{2,1,0:T(8,128)} %broadcast_in_dim.17), calls=%async_computation.5 | async-start | bytes 2097152 | tf_op jit(solution)/shard_map/all_to_all | solution.py:19
  114.1 15.2 %copy-start.1 = (f32[16,32,512]{2,1,0:T(8,128)}, f32[16,32,512]{2,1,0:T(8,128)S(1)}, u32[]{:S(2)}) copy-start(f32[16,32,512]{2,1,0:T(8,128)S(1)} %all-to-all-done.5.right_ref) | copy-start | bytes 3145732
  114.1 19.9 %collective-permute-start.2 = (f32[16,32,512]{2,1,0:T(8,128)S(1)}, f32[16,32,512]{2,1,0:T(8,128)S(1)}, u32[]{:S(2)}, u32[]{:S(2)}) collective-permute-start(f32[16,32,512]{2,1,0:T(8,128)S(1)} %all-to-all-done.5.right_ref), channel_id=1, source_target_pairs={{0,16},{16,0},{1,17},{17,1},{2,18},{18,2},{3,19},{19,3},{4,20},{20... | collective-permute-start | bytes 3145736 | tf_op jit(solution)/shard_map/ppermute | solution.py:13
  127.0 1.7 %collective-permute-start.3 = (f32[32,512]{1,0:T(8,128)S(1)}, f32[32,512]{1,0:T(8,128)S(1)}, u32[]{:S(2)}, u32[]{:S(2)}) collective-permute-start(f32[32,512]{1,0:T(8,128)S(1)} %convolution_multiply_fusion), channel_id=1, source_target_pairs={{0,16},{16,0},{1,17},{17,1},{2,18},{18,2},{3,19},{19,3},{4,20},{20... | collective-permute-start | bytes 196616 | tf_op jit(solution)/shard_map/ppermute | solution.py:13
  128.1 1.3 copy-start.3
  128.1 5.9 %collective-permute-start.1 = (f32[64,32]{1,0:T(8,128)S(1)}, f32[64,32]{1,0:T(8,128)S(1)}, u32[]{:S(2)}, u32[]{:S(2)}) collective-permute-start(f32[64,32]{1,0:T(8,128)S(1)} %convolution_multiply_fusion.1.weights_ref), channel_id=1, source_target_pairs={{0,16},{16,0},{1,17},{17,1},{2,18},{18,2},{3,19},{19,3},{4,20},{20... | collective-permute-start | bytes 24584 | tf_op jit(solution)/shard_map/ppermute | solution.py:13
  134.0 0.6 copy-start.4
  134.6 1.0 copy-start.2

commit v3 on v2

v3 whole, which is shorter than its diff:
```python
import functools

import jax
import jax.numpy as jnp
from jax import lax
from jax.experimental import pallas as pl
from jax.experimental.pallas import tpu as pltpu
from jax.sharding import Mesh, PartitionSpec as P

HIGH = lax.Precision.HIGHEST
F = ("y", "x")


def swap(value):
    return lax.ppermute(value, "core", [(0, 1), (1, 0)])


def spread(value, axes):
    count = lax.axis_size(axes)
    copies = jnp.broadcast_to(value[None], (count,) + value.shape)
    return lax.all_to_all(copies, axes, 0, 0)


def params(mib):
    return pltpu.CompilerParams(vmem_limit_bytes=mib << 20)


def tile_grid(rank, part):
    return rank // 8, part // 128


def terms_kernel(packed_ref, values_ref, sent_ref, left_ref):
    _, rows = left_ref.shape
    packed = jnp.sum(packed_ref[...], axis=0)
    left = jnp.concatenate([packed[:, :rows], packed[:, rows:]], axis=0)
    left_ref[...] = left
    shards = sent_ref.shape[0]
    part = values_ref.shape[1] // shards
    down, across = tile_grid(left.shape[0], part)
    gram = lax.dot_general(
        left, left, (((1,), (1,)), ((), ())), precision=HIGH, preferred_element_type=jnp.float32
    )
    gram_tile = jnp.concatenate([gram[8 * i : 8 * i + 8] for i in range(gram.shape[0] // 8)], axis=1)
    for shard in range(shards):
        terms = jnp.dot(
            left,
            values_ref[:, shard * part : (shard + 1) * part],
            precision=HIGH,
            preferred_element_type=jnp.float32,
        )
        for i in range(down):
            for j in range(across):
                sent_ref[shard, i * across + j] = terms[8 * i : 8 * i + 8, 128 * j : 128 * j + 128]
        sent_ref[shard, down * across] = gram_tile


def terms_of(packed, values, rank, shards):
    rows, width = values.shape
    down, across = tile_grid(rank, width // shards)
    return pl.pallas_call(
        terms_kernel,
        out_shape=(
            jax.ShapeDtypeStruct((shards, down * across + 1, 8, 128), jnp.float32),
            jax.ShapeDtypeStruct((rank, rows), jnp.float32),
        ),
        compiler_params=params(16),
        cost_estimate=pl.CostEstimate(
            flops=12 * rows * rank * width, bytes_accessed=6 * rows * width, transcendentals=0
        ),
        name="terms",
    )(packed, values)


def columns_kernel(got_ref, sums_ref, gram_ref):
    total = jnp.sum(got_ref[...], axis=0)
    tiles = total.shape[0] - 1
    gram_ref[...] = total[tiles]
    for z in range(sums_ref.shape[0]):
        sums_ref[z] = total[:tiles]


def columns_of(got, copies):
    tiles = got.shape[1] - 1
    return pl.pallas_call(
        columns_kernel,
        out_shape=(
            jax.ShapeDtypeStruct((copies, tiles, 8, 128), jnp.float32),
            jax.ShapeDtypeStruct((8, 128), jnp.float32),
        ),
        compiler_params=params(16),
        name="columns",
    )(got)


def inverse_kernel(scale_out, gram_ref, left_ref, factors_ref):
    rank, rows = left_ref.shape
    tile = gram_ref[...]
    gram = jnp.concatenate([tile[:, rank * i : rank * i + rank] for i in range(rank // 8)], axis=0)
    row_id = lax.broadcasted_iota(jnp.int32, (rank, rank), 0)
    col_id = lax.broadcasted_iota(jnp.int32, (rank, rank), 1)
    eye = jnp.where(row_id == col_id, 1.0, 0.0).astype(jnp.float32)
    state = jnp.concatenate([gram, eye], axis=1)
    below = lax.broadcasted_iota(jnp.int32, state.shape, 0)
    for k in range(rank):
        scale = 1.0 / jnp.sqrt(state[k : k + 1, k : k + 1])
        row = state[k : k + 1, :] * scale
        factor = state[:, k : k + 1] * scale
        state = jnp.where(
            below > k, state - factor * row, jnp.where(below == k, row, state)
        )
    inverse = state[:, rank:]
    factors_ref[rows:, :] = inverse
    orth = jnp.dot(inverse, left_ref[...], precision=HIGH, preferred_element_type=jnp.float32)
    factors_ref[:rows, :] = scale_out * lax.dot_general(
        orth, inverse, (((0,), (0,)), ((), ())), precision=HIGH, preferred_element_type=jnp.float32
    )


def inverse_of(gram, left, replicas):
    rank, rows = left.shape
    return pl.pallas_call(
        functools.partial(inverse_kernel, 1.0 / replicas),
        out_shape=jax.ShapeDtypeStruct((rows + rank, rank), jnp.float32),
        compiler_params=params(4),
        name="cholesky_inverse",
    )(gram, left)


def shard_kernel(scale, got_ref, factors_ref, later_ref, copies_ref, shard_ref):
    shards, rank, part = copies_ref.shape
    down, across = tile_grid(rank, part)
    total = jnp.sum(got_ref[...], axis=0)
    chunk = jnp.concatenate(
        [
            jnp.concatenate([total[i * across + j] for j in range(across)], axis=1)
            for i in range(down)
        ],
        axis=0,
    )
    for shard in range(shards):
        copies_ref[shard] = chunk
    shard_ref[...] = scale * jnp.dot(
        factors_ref[-rank:, :], chunk, precision=HIGH, preferred_element_type=jnp.float32
    )


def shard_of(got, factors, later, replicas, shards):
    rank = factors.shape[1]
    part = got.shape[1] * 1024 // rank
    return pl.pallas_call(
        functools.partial(shard_kernel, 1.0 / replicas),
        out_shape=(
            jax.ShapeDtypeStruct((shards, rank, part), jnp.float32),
            jax.ShapeDtypeStruct((rank, part), jnp.float32),
        ),
        compiler_params=params(16),
        name="shard",
    )(got, factors, later)


def split(value):
    high = value.astype(jnp.bfloat16)
    return high, (value - high.astype(jnp.float32)).astype(jnp.bfloat16)


def subtract(grad_ref, error_ref, factors_ref, right_ref, out_ref):
    rows = out_ref.shape[2]
    high, low = split(factors_ref[:rows, :])
    weights = jnp.concatenate([high, low, high], axis=1)
    pieces, _, part = right_ref.shape
    for piece in range(pieces):
        columns = pl.ds(piece * part, part)
        high, low = split(right_ref[piece])
        right = jnp.concatenate([high, high, low], axis=0)
        update = jnp.dot(weights, right, preferred_element_type=jnp.float32)
        merged = grad_ref[0, 0, :, columns].astype(jnp.float32) + error_ref[0, 0, :, columns]
        out_ref[0, 0, :, columns] = merged - update


def first_kernel(_, grad_ref, error_ref, factors_ref, right_ref, out_ref):
    subtract(grad_ref, error_ref, factors_ref, right_ref, out_ref)


def second_kernel(
    scale, where_ref, grad_ref, error_ref, factors_ref, right_ref, shard_ref, _, out_ref, basis_ref
):
    subtract(grad_ref, error_ref, factors_ref, right_ref, out_ref)
    pieces, rank, _ = right_ref.shape
    index, place = where_ref[0], where_ref[1]

    @pl.when(place // pieces == pl.program_id(0))
    def _():
        basis_ref[1 - index] = shard_ref[...]
        basis_ref[index] = scale * jnp.dot(
            factors_ref[-rank:, :],
            right_ref[place % pieces],
            precision=HIGH,
            preferred_element_type=jnp.float32,
        )


def residual_of(where, grad_pair, error_pair, factors, right, later=None, replicas=1):
    steps = 4
    _, pair, rows, width = grad_pair.shape
    shards, rank, part = right.shape
    big = pl.BlockSpec((1, 1, rows, width // steps), lambda i, w: (0, w[0], 0, i))
    in_specs = [
        big,
        big,
        pl.BlockSpec((rows + rank, rank), lambda i, w: (0, 0)),
        pl.BlockSpec((shards // steps, rank, part), lambda i, w: (i, 0, 0)),
    ]
    kernel, extra, aliases = first_kernel, (), {}
    out_specs, out_shape = big, jax.ShapeDtypeStruct(error_pair.shape, jnp.float32)
    if later is not None:
        kernel, extra, aliases = functools.partial(second_kernel, 1.0 / replicas), later, {6: 0}
        in_specs += [
            pl.BlockSpec((rank, part), lambda i, w: (0, 0)),
            pl.BlockSpec(memory_space=pl.ANY),
        ]
        out_specs = (big, pl.BlockSpec((pair, rank, part), lambda i, w: (0, 0, 0)))
        out_shape = (out_shape, jax.ShapeDtypeStruct((pair, rank, part), jnp.float32))
    return pl.pallas_call(
        kernel,
        grid_spec=pltpu.PrefetchScalarGridSpec(
            num_scalar_prefetch=1, grid=(steps,), in_specs=in_specs, out_specs=out_specs
        ),
        out_shape=out_shape,
        input_output_aliases=aliases,
        compiler_params=params(16),
        cost_estimate=pl.CostEstimate(
            flops=6 * rows * rank * width, bytes_accessed=11 * rows * width, transcendentals=0
        ),
        name="residual",
    )(where, grad_pair, error_pair, factors, right, *extra)


def on_device(grad_pair, error_pair, basis_pair):
    core = lax.axis_index("core")
    replicas = lax.axis_size("core") * lax.axis_size("z")
    rows, width = grad_pair.shape[2:]
    rank, part = basis_pair.shape[1:]
    shards = width // part

    def merged(index):
        grad = lax.dynamic_index_in_dim(grad_pair[0], index, 0, False)
        return grad.astype(jnp.float32) + lax.dynamic_index_in_dim(error_pair[0], index, 0, False)

    own_basis = lax.dynamic_index_in_dim(basis_pair, core, 0, False)
    basis = spread(own_basis, F)
    pair_sum = merged(core) + swap(merged(1 - core))
    pieces = pair_sum.reshape(rows, shards, part)
    left = jnp.einsum("fkc,rfc->kr", basis, pieces, precision=HIGH)
    half = rank // 2
    packed = jnp.concatenate([left[:half], left[half:]], axis=1)
    sent, left = terms_of(spread(packed, "z"), pair_sum, rank, shards)
    sums, gram = columns_of(lax.all_to_all(sent, F, 0, 0), lax.axis_size("z"))
    factors = inverse_of(gram, left, replicas)
    other_factors = swap(factors)
    copies, shard = shard_of(
        lax.all_to_all(sums, "z", 0, 0), factors, other_factors, replicas, shards
    )
    whole = lax.all_to_all(copies, F, 0, 0)
    other_whole = swap(whole)
    place = lax.axis_index(F)
    residual = residual_of(jnp.stack([core, place]), grad_pair, error_pair, factors, whole)
    return residual_of(
        jnp.stack([1 - core, place]),
        grad_pair,
        error_pair,
        other_factors,
        other_whole,
        (shard, residual),
        replicas,
    )


def solution(mesh):
    grid = Mesh(mesh.devices.reshape(8, 2, 4, 4), ("z", "core", "y", "x"))
    replica = ("z", "core")
    in_specs = (
        P(replica, None, F, None),
        P(replica, None, F, None),
        P(None, None, F),
    )
    out_specs = (P(replica, None, F, None), P(None, None, F))
    return jax.shard_map(
        on_device, mesh=grid, in_specs=in_specs, out_specs=out_specs, check_vma=False
    )
```

time: 141 us -> 118 us (0.84)
  waiting for transfers between devices: 47.9 us -> 22.2 us
  blocking collectives: 34.3 us -> 50.6 us
  starting transfers between devices: 25.7 us -> 20.3 us
  matrix products: 5.87 us -> 1.77 us
  local copies, waits for them, and re-layouts: 5.43 us -> 3.32 us
    all_to_all x4 -> x1, waiting for transfers between devices: 47.9 us -> 14.6 us  [spread(): return lax.all_to_all(copies, axes, 0, 0)]
    all_to_all x1 -> x2, blocking collectives: 19 us -> 35.3 us  [the longest x1 19.6 us: on_device(): sums, gram = columns_of(lax.all_to_all(sent, F, 0, 0), lax.axis_size('z'))]
    all_to_all x4 -> x1, starting transfers between devices: 15.7 us -> 5.02 us  [spread(): return lax.all_to_all(copies, axes, 0, 0)]
    all_to_all x0 -> x1, waiting for transfers between devices: none -> 6.71 us  [on_device(): lax.all_to_all(sums, 'z', 0, 0)]
    dot_general x5 -> x0, matrix products: 4.1 us -> none  [the longest x1 1.24 us: on_device(): terms = jnp.einsum('kr,rfc->fkc', left, pieces, precision=HIGH)]
    all_to_all x0 -> x1, starting transfers between devices: none -> 3.63 us  [on_device(): lax.all_to_all(sums, 'z', 0, 0)]
    broadcast_in_dim x6 -> x3, local copies, waits for them, and re-layouts: 3.7 us -> 1.11 us  [spread(): copies = jnp.broadcast_to(value[None], (count,) + value.shape)]
    ppermute x4 -> x3, starting transfers between devices: 10 us -> 11.7 us  [swap(): return lax.ppermute(value, 'core', [(0, 1), (1, 0)])]
  transfers between devices with their start and end apart: 8 -> 5, of which waited for: 4 -> 3; matrix products, arithmetic and copies ran while one was open for 6% -> 3% of each run, Pallas kernels for 6% -> 6%
where the time goes in v3:
time: 118 us
  blocking collectives  50.6 us (43%)
  waiting for transfers between devices  22.2 us (19%)
  starting transfers between devices  20.3 us (17%)
  Pallas kernels  13.9 us (12%)
  other arithmetic  5.05 us (4%)
  local copies, waits for them, and re-layouts  3.32 us (3%)
  matrix products  1.77 us (2%)
    all_to_all x1, blocking collectives, on_device(): sums, gram = columns_of(lax.all_to_all(sent, F, 0, 0), lax.axis_size('z'))  19.6 us
    all_to_all x1, blocking collectives, on_device(): whole = lax.all_to_all(copies, F, 0, 0)  15.6 us
    all_to_all x1, blocking collectives, spread(): return lax.all_to_all(copies, axes, 0, 0)  15.3 us
    all_to_all x1, waiting for transfers between devices, spread(): return lax.all_to_all(copies, axes, 0, 0)  14.6 us
    ppermute x3, starting transfers between devices, swap(): return lax.ppermute(value, 'core', [(0, 1), (1, 0)])  11.7 us
    pallas_call x2, Pallas kernels, residual_of(): pl.pallas_call(kernel, grid_spec=pltpu.PrefetchScalarGridSpec(num_scalar_...  8.14 us
    all_to_all x1, waiting for transfers between devices, on_device(): lax.all_to_all(sums, 'z', 0, 0)  6.71 us
    all_to_all x1, starting transfers between devices, spread(): return lax.all_to_all(copies, axes, 0, 0)  5.02 us
  transfers between devices with their start and end apart: 5, of which 3 were waited for; matrix products, arithmetic and copies ran while one was open for 3% of the time, Pallas kernels for 6%

profile of v3, /device:TPU:1, one launch (start us, length us, event | category | flops | bytes accessed | tf_op | source)
XLA Modules:
  0.0 117.8 jit_solution(5951249527921434785)
XLA Ops:
  0.6 0.0 copy-start
  0.7 2.1 %add_bitcast_fusion = f32[64,8192]{1,0:T(8,128)S(1)} fusion(f32[1,2,64,8192]{3,2,1,0:T(8,128)} %error_ref.3, s32[]{:T(128)S(6)} %select_n.13, bf16[1,2,64,8192]{3,2,1,0:T(8,128)(2,1)} %grad_ref.3), kind=kLoop, calls=%fused_computation.4 | loop fusion | flops 1048576 | bytes 5242884 | tf_op jit(solution)/shard_map/add | solution.py:247
  2.7 3.3 %collective-permute-start = (f32[64,8192]{1,0:T(8,128)S(1)}, f32[64,8192]{1,0:T(8,128)}, u32[]{:S(2)}, u32[]{:S(2)}) collective-permute-start(f32[64,8192]{1,0:T(8,128)S(1)} %add_bitcast_fusion), channel_id=1, source_target_pairs={{0,16},{16,0},{1,17},{17,1},{2,18},{18,2},{3,19},{19,3},{4,20},{20... | collective-permute-start | bytes 6291464 | tf_op jit(solution)/shard_map/ppermute | solution.py:15
  6.1 0.0 copy-done
  6.1 1.1 broadcast_in_dim.7
  7.2 5.0 %all-to-all-start = ((f32[16,32,512]{2,1,0:T(8,128)}), f32[16,32,512]{2,1,0:T(8,128)S(1)}, u32[]{:S(2)}, u32[]{:S(2)}) async-start(f32[16,32,512]{2,1,0:T(8,128)} %broadcast_in_dim.7), calls=%async_computation | async-start | bytes 2097152 | tf_op jit(solution)/shard_map/all_to_all | solution.py:21
  12.2 0.0 collective-permute-done
  12.2 2.8 %bitcast_add_fusion.values_ref = f32[64,8192]{1,0:T(8,128)S(1)} fusion(f32[64,8192]{1,0:T(8,128)} %collective-permute-done, f32[1,2,64,8192]{3,2,1,0:T(8,128)} %error_ref.3, s32[]{:T(128)S(6)} %select_n.12, bf16[1,2,64,8192]{3,2,1,0:T(8,128)(2,1)} %grad_ref.3), kind=kLoop, calls=%fused_computation.3 | loop fusion | flops 1572864 | bytes 7340036 | tf_op jit(solution)/shard_map/add | solution.py:251
  15.0 14.6 %all-to-all-done = f32[16,32,512]{2,1,0:T(8,128)S(1)} async-done(((f32[16,32,512]{2,1,0:T(8,128)}), f32[16,32,512]{2,1,0:T(8,128)S(1)}, u32[]{:S(2)}, u32[]{:S(2)}) %all-to-all-start) | async-done | bytes 1048608 | tf_op jit(solution)/shard_map/all_to_all | solution.py:21
  29.6 1.8 %fusion.3 = f32[32,64]{1,0:T(8,128)S(1)} fusion(f32[16,32,512]{2,1,0:T(8,128)S(1)} %all-to-all-done, f32[8,16,8,512]{3,2,1,0:T(8,128)S(1)} %bitcast.18), kind=kOutput, calls=%fused_computation.5 | convolution fusion | flops 201326592 | bytes 3153920 | tf_op jit(solution)/shard_map/fkc,rfc->kr/dot_general | solution.py:253
  31.3 0.1 pad_maximum_fusion
  31.4 15.3 %all_to_all.25.packed_ref = f32[8,16,128]{2,1,0:T(8,128)S(1)} all-to-all(f32[8,16,128]{2,1,0:T(8,128)S(1)} %broadcast_in_dim.16), channel_id=1, replica_groups=mesh['z'=8,'core'=2,'y'=4,'x'=4] {'z'}, dimensions={0} | all-to-all | bytes 131072 | tf_op jit(solution)/shard_map/all_to_all | solution.py:21
  46.7 1.1 terms.1
  47.8 19.6 %all_to_all.26.got_ref = f32[16,17,8,128]{3,2,1,0:T(8,128)S(1)} all-to-all(f32[16,17,8,128]{3,2,1,0:T(8,128)S(1)} %get-tuple-element.8), channel_id=1, replica_groups=mesh['z'=8,'core'=2,'y'=4,'x'=4] {'y','x'}, dimensions={0} | all-to-all | bytes 2228224 | tf_op jit(solution)/shard_map/all_to_all | solution.py:257
  67.4 0.9 columns.1
  68.3 0.0 copy-start.2
  68.3 3.6 %all-to-all-start.3 = ((f32[8,16,8,128]{3,2,1,0:T(8,128)}), f32[8,16,8,128]{3,2,1,0:T(8,128)S(1)}, u32[]{:S(2)}, u32[]{:S(2)}) async-start(f32[8,16,8,128]{3,2,1,0:T(8,128)} %get-tuple-element.11), calls=%async_computation.3 | async-start | bytes 1048576 | tf_op jit(solution)/shard_map/all_to_all | solution.py:261
  71.9 3.5 %cholesky_inverse.1.factors_ref = f32[96,32]{1,0:T(8,128)S(1)} custom-call(f32[8,128]{1,0:T(8,128)S(1)} %get-tuple-element.9.gram_ref, f32[32,64]{1,0:T(8,128)S(1)} %get-tuple-element.10.left_ref), custom_call_target="tpu_custom_call" | custom-call | tf_op jit(solution)/shard_map/cholesky_inverse/pallas_call | solution.py:121
  75.5 3.1 %collective-permute-start.1 = (f32[96,32]{1,0:T(8,128)S(1)}, f32[96,32]{1,0:T(8,128)S(1)}, u32[]{:S(2)}, u32[]{:S(2)}) collective-permute-start(f32[96,32]{1,0:T(8,128)S(1)} %cholesky_inverse.1.factors_ref), channel_id=1, source_target_pairs={{0,16},{16,0},{1,17},{17,1},{2,18},{18,2},{3,19},{19,3},{4,20},{20... | collective-permute-start | bytes 36872 | tf_op jit(solution)/shard_map/ppermute | solution.py:15
  78.6 0.9 collective-permute-done.1.later_ref.factors_ref
  79.5 6.7 %all-to-all-done.3.got_ref = f32[8,16,8,128]{3,2,1,0:T(8,128)S(1)} async-done(((f32[8,16,8,128]{3,2,1,0:T(8,128)}), f32[8,16,8,128]{3,2,1,0:T(8,128)S(1)}, u32[]{:S(2)}, u32[]{:S(2)}) %all-to-all-start.3) | async-done | bytes 524320 | tf_op jit(solution)/shard_map/all_to_all | solution.py:261
  86.2 0.3 shard.1
  86.5 15.6 %all_to_all.27.right_ref = f32[16,32,512]{2,1,0:T(8,128)S(1)} all-to-all(f32[16,32,512]{2,1,0:T(8,128)S(1)} %get-tuple-element.12), channel_id=1, replica_groups=mesh['z'=8,'core'=2,'y'=4,'x'=4] {'y','x'}, dimensions={0} | all-to-all | bytes 2097152 | tf_op jit(solution)/shard_map/all_to_all | solution.py:263
  102.1 5.2 %collective-permute-start.2 = (f32[16,32,512]{2,1,0:T(8,128)S(1)}, f32[16,32,512]{2,1,0:T(8,128)}, u32[]{:S(2)}, u32[]{:S(2)}) collective-permute-start(f32[16,32,512]{2,1,0:T(8,128)S(1)} %all_to_all.27.right_ref), channel_id=1, source_target_pairs={{0,16},{16,0},{1,17},{17,1},{2,18},{18,2},{3,19},{19,3},{4,20},{20... | collective-permute-start | bytes 3145736 | tf_op jit(solution)/shard_map/ppermute | solution.py:15
  107.3 0.1 pad_add_fusion.where_ref
  107.4 0.1 pad_add_fusion.1._
  107.5 0.0 copy-done.2
  107.5 0.0 copy-start.1
  107.5 2.2 %copy-done.1 = f32[1,2,64,8192]{3,2,1,0:T(8,128)S(1)} copy-done((f32[1,2,64,8192]{3,2,1,0:T(8,128)S(1)}, f32[1,2,64,8192]{3,2,1,0:T(8,128)}, u32[]{:S(2)}) %copy-start.1) | copy-done | bytes 4194328
  109.7 3.2 %residual.2._ = f32[1,2,64,8192]{3,2,1,0:T(8,128)} custom-call(s32[2]{0:T(128)S(1)} %pad_add_fusion.1._, bf16[1,2,64,8192]{3,2,1,0:T(8,128)(2,1)S(1)} %copy-done.2, f32[1,2,64,8192]{3,2,1,0:T(8,128)S(1)} %copy-done.1, f32[96,32]{1,0:T(8,128)S(1)} %cholesky_inverse.1.factors_ref, f32[16,32,512]{2,1,0:T(8,128)S(1)} %all_to_all.27.right_ref), custom_call_target="tpu_custom_call" | custom-call | flops 100663296 | bytes 5767168 | tf_op jit(solution)/shard_map/residual/pallas_call | solution.py:223
  112.8 0.0 collective-permute-done.2.right_ref
  112.9 5.0 %residual.3 = (f32[1,2,64,8192]{3,2,1,0:T(8,128)}, f32[2,32,512]{2,1,0:T(8,128)}) custom-call(s32[2]{0:T(128)S(1)} %pad_add_fusion.where_ref, bf16[1,2,64,8192]{3,2,1,0:T(8,128)(2,1)S(1)} %copy-done.2, f32[1,2,64,8192]{3,2,1,0:T(8,128)S(1)} %copy-done.1, f32[96,32]{1,0:T(8,128)S(1)} %collective-permute-done.1.later_ref.factors_ref, ...), custom_call_target="tpu_custom_call", output_to_operand_aliasing={{0}: (6, {})} | custom-call | flops 100663296 | bytes 5767168 | tf_op jit(solution)/shard_map/residual/pallas_call | solution.py:223
  (3 shorter events, 0.0 us)
Async XLA Ops:
  0.6 5.4 %copy-start = (f32[2,32,512]{2,1,0:T(8,128)S(1)}, f32[2,32,512]{2,1,0:T(8,128)}, u32[]{:S(2)}) copy-start(f32[2,32,512]{2,1,0:T(8,128)} %param.5) | copy-start | bytes 393220
  2.7 9.5 %collective-permute-start = (f32[64,8192]{1,0:T(8,128)S(1)}, f32[64,8192]{1,0:T(8,128)}, u32[]{:S(2)}, u32[]{:S(2)}) collective-permute-start(f32[64,8192]{1,0:T(8,128)S(1)} %add_bitcast_fusion), channel_id=1, source_target_pairs={{0,16},{16,0},{1,17},{17,1},{2,18},{18,2},{3,19},{19,3},{4,20},{20... | collective-permute-start | bytes 6291464 | tf_op jit(solution)/shard_map/ppermute | solution.py:15
  7.2 22.4 %all-to-all-start = ((f32[16,32,512]{2,1,0:T(8,128)}), f32[16,32,512]{2,1,0:T(8,128)S(1)}, u32[]{:S(2)}, u32[]{:S(2)}) async-start(f32[16,32,512]{2,1,0:T(8,128)} %broadcast_in_dim.7), calls=%async_computation | async-start | bytes 2097152 | tf_op jit(solution)/shard_map/all_to_all | solution.py:21
  68.3 39.2 %copy-start.2 = (bf16[1,2,64,8192]{3,2,1,0:T(8,128)(2,1)S(1)}, bf16[1,2,64,8192]{3,2,1,0:T(8,128)(2,1)}, u32[]{:S(2)}) copy-start(bf16[1,2,64,8192]{3,2,1,0:T(8,128)(2,1)} %grad_ref.3) | copy-start | bytes 6291460
  68.3 17.9 %all-to-all-start.3 = ((f32[8,16,8,128]{3,2,1,0:T(8,128)}), f32[8,16,8,128]{3,2,1,0:T(8,128)S(1)}, u32[]{:S(2)}, u32[]{:S(2)}) async-start(f32[8,16,8,128]{3,2,1,0:T(8,128)} %get-tuple-element.11), calls=%async_computation.3 | async-start | bytes 1048576 | tf_op jit(solution)/shard_map/all_to_all | solution.py:261
  75.5 4.0 %collective-permute-start.1 = (f32[96,32]{1,0:T(8,128)S(1)}, f32[96,32]{1,0:T(8,128)S(1)}, u32[]{:S(2)}, u32[]{:S(2)}) collective-permute-start(f32[96,32]{1,0:T(8,128)S(1)} %cholesky_inverse.1.factors_ref), channel_id=1, source_target_pairs={{0,16},{16,0},{1,17},{17,1},{2,18},{18,2},{3,19},{19,3},{4,20},{20... | collective-permute-start | bytes 36872 | tf_op jit(solution)/shard_map/ppermute | solution.py:15
  102.1 10.7 %collective-permute-start.2 = (f32[16,32,512]{2,1,0:T(8,128)S(1)}, f32[16,32,512]{2,1,0:T(8,128)}, u32[]{:S(2)}, u32[]{:S(2)}) collective-permute-start(f32[16,32,512]{2,1,0:T(8,128)S(1)} %all_to_all.27.right_ref), channel_id=1, source_target_pairs={{0,16},{16,0},{1,17},{17,1},{2,18},{18,2},{3,19},{19,3},{4,20},{20... | collective-permute-start | bytes 3145736 | tf_op jit(solution)/shard_map/ppermute | solution.py:15
  107.5 2.2 %copy-start.1 = (f32[1,2,64,8192]{3,2,1,0:T(8,128)S(1)}, f32[1,2,64,8192]{3,2,1,0:T(8,128)}, u32[]{:S(2)}) copy-start(f32[1,2,64,8192]{3,2,1,0:T(8,128)} %error_ref.3) | copy-start | bytes 12582916

commit v4 on v0

v4 whole, which is shorter than its diff:
```python
import functools

import jax
import jax.numpy as jnp
from jax import lax
from jax.experimental import pallas as pl
from jax.experimental.pallas import tpu as pltpu
from jax.sharding import Mesh, PartitionSpec as P

HIGH = lax.Precision.HIGHEST
F = ("y", "x")
LANES = 128
SMEM = pl.BlockSpec(memory_space=pltpu.SMEM)
VMEM = pl.BlockSpec(memory_space=pltpu.VMEM)
ANY = pl.BlockSpec(memory_space=pl.ANY)


def f32(*shape):
    return jax.ShapeDtypeStruct(shape, jnp.float32)


def call(kernel, name, in_specs, out_shape, operands, mib=16, **more):
    return pl.pallas_call(
        kernel,
        in_specs=in_specs,
        out_shape=out_shape,
        compiler_params=pltpu.CompilerParams(vmem_limit_bytes=mib << 20),
        name=name,
        **more,
    )(*operands)


def swap(value):
    return lax.ppermute(value, "core", [(0, 1), (1, 0)])


def shift(value, step):
    count = lax.axis_size("z")
    return lax.ppermute(value, "z", [(i, (i + step) % count) for i in range(count)])


def kept(place_ref):
    return 3 - 2 * place_ref[3], 2 * place_ref[3]


def given(place_ref):
    return 1 + 2 * place_ref[3], 2 - 2 * place_ref[3]


def quarter(ref, chunk, which):
    start = pl.multiple_of((4 * chunk + which) * LANES, LANES)
    return ref[:, pl.ds(start, LANES)]


def half(ref, chunk, slot):
    start = (2 * chunk + slot) * LANES
    return ref[:, start : start + LANES]


def other_kernel(place_ref, other_ref, give_ref, keep_ref):
    for out_ref, quarters in ((give_ref, given(place_ref)), (keep_ref, kept(place_ref))):
        for chunk in range(other_ref.shape[1] // (4 * LANES)):
            for slot, which in enumerate(quarters):
                start = (2 * chunk + slot) * LANES
                out_ref[:, start : start + LANES] = quarter(other_ref, chunk, which)


def give_kernel(place_ref, own_ref, got_ref, *out_refs):
    for chunk in range(own_ref.shape[1] // (4 * LANES)):
        for slot, (out_ref, which) in enumerate(zip(out_refs, given(place_ref))):
            start = chunk * LANES
            out_ref[:, start : start + LANES] = quarter(own_ref, chunk, which) + half(
                got_ref, chunk, slot
            )


def basis_kernel(place_ref, basis_ref, _, copies_ref):
    columns = [
        basis_ref[place_ref[0], :, pl.ds(pl.multiple_of(which * LANES, LANES), LANES)]
        for which in kept(place_ref)
    ]
    chunk = jnp.concatenate(columns, axis=1)
    for copy in range(copies_ref.shape[0]):
        copies_ref[copy] = chunk


def left_kernel(place_ref, own_ref, got_ref, up_ref, down_ref, basis_ref, copies_ref, values_ref):
    parts = []
    for chunk in range(basis_ref.shape[0]):
        start = chunk * LANES
        sums = [
            quarter(own_ref, chunk, which)
            + half(got_ref, chunk, slot)
            + z_ref[:, start : start + LANES]
            for slot, (which, z_ref) in enumerate(zip(kept(place_ref), (up_ref, down_ref)))
        ]
        values = jnp.concatenate(sums, axis=1)
        values_ref[:, 2 * start : 2 * start + 2 * LANES] = values
        parts.append(
            lax.dot_general(
                basis_ref[chunk],
                values,
                (((1,), (1,)), ((), ())),
                precision=HIGH,
                preferred_element_type=jnp.float32,
            )
        )
    while len(parts) > 1:
        parts = [sum(parts[i : i + 2]) for i in range(0, len(parts), 2)]
    left = parts[0]
    middle = left.shape[0] // 2
    packed = jnp.concatenate([left[:middle], left[middle:]], axis=1)
    for copy in range(copies_ref.shape[0]):
        copies_ref[copy] = packed


def terms_kernel(packed_ref, values_ref, sent_ref, left_ref):
    _, rows = left_ref.shape
    packed = jnp.sum(packed_ref[...], axis=0)
    left = jnp.concatenate([packed[:, :rows], packed[:, rows:]], axis=0)
    left_ref[...] = left
    gram = lax.dot_general(
        left, left, (((1,), (1,)), ((), ())), precision=HIGH, preferred_element_type=jnp.float32
    )
    rank = gram.shape[0]
    gram_tile = jnp.concatenate([gram[8 * i : 8 * i + 8] for i in range(rank // 8)], axis=1)
    for chunk in range(sent_ref.shape[0]):
        start = 2 * chunk * LANES
        terms = jnp.dot(
            left,
            values_ref[:, start : start + 2 * LANES],
            precision=HIGH,
            preferred_element_type=jnp.float32,
        )
        for i in range(rank // 8):
            for j in range(2):
                sent_ref[chunk, 2 * i + j] = terms[8 * i : 8 * i + 8, LANES * j : LANES * j + LANES]
        sent_ref[chunk, rank // 4] = gram_tile


def columns_kernel(got_ref, sums_ref, gram_ref):
    total = jnp.sum(got_ref[...], axis=0)
    tiles = total.shape[0] - 1
    gram_ref[...] = total[tiles]
    for copy in range(sums_ref.shape[0]):
        sums_ref[copy] = total[:tiles]


def factors_kernel(scale, gram_ref, left_ref, factors_ref):
    rank, rows = left_ref.shape
    tile = gram_ref[...]
    gram = jnp.concatenate([tile[:, rank * i : rank * i + rank] for i in range(rank // 8)], axis=0)
    row_id = lax.broadcasted_iota(jnp.int32, (rank, rank), 0)
    col_id = lax.broadcasted_iota(jnp.int32, (rank, rank), 1)
    eye = jnp.where(row_id == col_id, 1.0, 0.0).astype(jnp.float32)
    state = jnp.concatenate([gram, eye], axis=1)
    below = lax.broadcasted_iota(jnp.int32, state.shape, 0)
    for k in range(rank):
        root = 1.0 / jnp.sqrt(state[k : k + 1, k : k + 1])
        row = state[k : k + 1, :] * root
        factor = state[:, k : k + 1] * root
        state = jnp.where(
            below > k, state - factor * row, jnp.where(below == k, row, state)
        )
    inverse = state[:, rank:]
    factors_ref[rows:, :] = inverse
    orth = jnp.dot(inverse, left_ref[...], precision=HIGH, preferred_element_type=jnp.float32)
    factors_ref[:rows, :] = scale * lax.dot_general(
        orth, inverse, (((0,), (0,)), ((), ())), precision=HIGH, preferred_element_type=jnp.float32
    )


def shard_kernel(scale, got_ref, factors_ref, _, copies_ref, shard_ref):
    rank = copies_ref.shape[1]
    got = got_ref[...]
    count = got.shape[0]
    even = sum(got[z] for z in range(0, count, 2))
    odd = sum(got[z] for z in range(1, count, 2))
    rows = []
    for i in range(rank // 8):
        quarters = (even[2 * i + 1], odd[2 * i], odd[2 * i + 1], even[2 * i])
        rows.append(jnp.concatenate(quarters, axis=1))
    chunk = jnp.concatenate(rows, axis=0)
    for copy in range(copies_ref.shape[0]):
        copies_ref[copy] = chunk
    shard_ref[...] = scale * jnp.dot(
        factors_ref[-rank:, :], chunk, precision=HIGH, preferred_element_type=jnp.float32
    )


def split(value):
    high = value.astype(jnp.bfloat16)
    return high, (value - high.astype(jnp.float32)).astype(jnp.bfloat16)


def subtract(index, merged_ref, factors_ref, right_ref, out_ref, buffer, sems):
    rows = merged_ref.shape[0]
    shards, _, part = right_ref.shape
    groups = sems.shape[0]
    high, low = split(factors_ref[:rows, :])
    weights = jnp.concatenate([high, low, high], axis=1)
    copies = []
    for group in range(groups):
        for chunk in range(group * shards // groups, (group + 1) * shards // groups):
            columns = slice(chunk * part, (chunk + 1) * part)
            high, low = split(right_ref[chunk])
            right = jnp.concatenate([high, high, low], axis=0)
            update = jnp.dot(weights, right, preferred_element_type=jnp.float32)
            buffer[:, columns] = merged_ref[:, columns] - update
        width = merged_ref.shape[1] // groups
        columns = pl.ds(group * width, width)
        copy = pltpu.make_async_copy(
            buffer.at[:, columns], out_ref.at[0, index, :, columns], sems.at[group]
        )
        copy.start()
        copies.append(copy)
    return copies


def first_kernel(place_ref, merged_ref, factors_ref, right_ref, out_ref, *scratch):
    for copy in subtract(place_ref[0], merged_ref, factors_ref, right_ref, out_ref, *scratch):
        copy.wait()


def second_kernel(
    scale, place_ref, merged_ref, factors_ref, right_ref, shard_ref, _, out_ref, basis_ref, *scratch
):
    copies = subtract(place_ref[1], merged_ref, factors_ref, right_ref, out_ref, *scratch)
    rank = right_ref.shape[1]
    basis_ref[place_ref[0]] = shard_ref[...]
    basis_ref[place_ref[1]] = scale * jnp.dot(
        factors_ref[-rank:, :],
        right_ref[place_ref[2]],
        precision=HIGH,
        preferred_element_type=jnp.float32,
    )
    for copy in copies:
        copy.wait()


def on_device(grad_pair, error_pair, basis_pair):
    core = lax.axis_index("core")
    zs = lax.axis_size("z")
    scale = 1.0 / (lax.axis_size("core") * zs)
    pair, rows, width = grad_pair.shape[1:]
    rank, part = basis_pair.shape[1:]
    shards = width // part
    place = jnp.stack([core, 1 - core, lax.axis_index(F), lax.axis_index("z") % 2])

    def merged(index):
        grad = lax.dynamic_index_in_dim(grad_pair[0], index, 0, False)
        return grad.astype(jnp.float32) + lax.dynamic_index_in_dim(error_pair[0], index, 0, False)

    by_two, by_four = f32(rows, width // 2), f32(rows, width // 4)

    other = merged(1 - core)
    give, keep = call(other_kernel, "quarters", [SMEM, VMEM], (by_two, by_two), (place, other))
    give, index = lax.optimization_barrier((give, core))
    give, keep = swap(give), swap(keep)
    own = merged(index)
    up, down = call(
        give_kernel, "give", [SMEM, VMEM, VMEM], (by_four, by_four), (place, own, give)
    )
    copies = call(
        basis_kernel, "basis", [SMEM, VMEM, ANY], f32(shards, rank, part // 2),
        (place, basis_pair, up),
    )
    up, down = shift(up, 1), shift(down, -1)
    basis = lax.all_to_all(copies, F, 0, 0)
    copies, values = call(
        left_kernel, "left", [SMEM] + [VMEM] * 5, (f32(zs, rank // 2, 2 * rows), by_two),
        (place, own, keep, up, down, basis),
    )
    sent, left = call(
        terms_kernel, "terms", [VMEM, VMEM], (f32(shards, rank // 4 + 1, 8, LANES), f32(rank, rows)),
        (lax.all_to_all(copies, "z", 0, 0), values),
    )
    sums, gram = call(
        columns_kernel, "columns", [VMEM], (f32(zs, rank // 4, 8, LANES), f32(8, LANES)),
        (lax.all_to_all(sent, F, 0, 0),),
    )
    factors = call(
        functools.partial(factors_kernel, scale), "factors", [VMEM, VMEM],
        f32(rows + rank, rank), (gram, left),
    )
    other_factors = swap(factors)
    copies, shard = call(
        functools.partial(shard_kernel, scale), "shard", [VMEM, VMEM, ANY],
        (f32(shards, rank, part), f32(rank, part)),
        (lax.all_to_all(sums, "z", 0, 0), factors, other_factors),
    )
    whole = lax.all_to_all(copies, F, 0, 0)
    other_whole = swap(whole)
    residual_scratch = [pltpu.VMEM((rows, width), jnp.float32), pltpu.SemaphoreType.DMA((4,))]
    residual_shape = f32(1, pair, rows, width)
    residual = call(
        first_kernel, "residual_own", [SMEM, VMEM, VMEM, VMEM], residual_shape,
        (place, own, factors, whole), out_specs=ANY, scratch_shapes=residual_scratch,
    )
    return call(
        functools.partial(second_kernel, scale), "residual_other",
        [SMEM, VMEM, VMEM, VMEM, VMEM, ANY], (residual_shape, f32(pair, rank, part)),
        (place, other, other_factors, other_whole, shard, residual),
        out_specs=(ANY, VMEM), scratch_shapes=residual_scratch, input_output_aliases={5: 0},
    )


def solution(mesh):
    grid = Mesh(mesh.devices.reshape(8, 2, 4, 4), ("z", "core", "y", "x"))
    replica = ("z", "core")
    in_specs = (
        P(replica, None, F, None),
        P(replica, None, F, None),
        P(None, None, F),
    )
    out_specs = (P(replica, None, F, None), P(None, None, F))
    return jax.shard_map(
        on_device, mesh=grid, in_specs=in_specs, out_specs=out_specs, check_vma=False
    )
```

time: 481 us -> 105 us (0.22)
  waiting for transfers between devices: 327 us -> 13.2 us
  blocking collectives: 104 us -> 38.3 us
  starting transfers between devices: 0.08 us -> 28.8 us
  matrix products: 21.2 us -> 0 us
  Pallas kernels: 0 us -> 18 us
  between operations: 14.1 us -> 0.72 us
  other arithmetic: 12.9 us -> 4.15 us
    psum x1 -> x0, waiting for transfers between devices: 271 us -> none  [on_device(): right_basis = lax.psum(terms, ('replica', 'fsdp')) / replicas]
    psum x2 -> x0, blocking collectives: 104 us -> none  [the longest x1 58.2 us: on_device(): gram = lax.psum(gram_of(summed_left), 'fsdp')]
    all_gather x1 -> x0, waiting for transfers between devices: 55.4 us -> none  [on_device(): basis_whole = lax.all_gather(basis_pair, 'fsdp', axis=2, tiled=True)]
    all_to_all x0 -> x3, blocking collectives: none -> 38.3 us  [the longest x1 15 us: on_device(): whole = lax.all_to_all(copies, F, 0, 0)]
    dot_general x4 -> x0, matrix products: 20.9 us -> none  [the longest x1 7.6 us: on_device(): update = jnp.einsum('mrk,mkc->mrc', orth, right_basis, precision=high)]
    ppermute x0 -> x6, starting transfers between devices: none -> 18.7 us  [the longest x4 14.8 us: swap(): return lax.ppermute(value, 'core', [(0, 1), (1, 0)])]
    pallas_call x0 -> x10, Pallas kernels: none -> 18 us  [call(): pl.pallas_call(kernel, in_specs=in_specs, out_shape=out_shape, compiler_p...]
    another operation x7 -> x1, other arithmetic: 11 us -> 0.08 us  [on_device(): jnp.stack([core, 1 - core, lax.axis_index(F), lax.axis_index('z') % 2])]
  transfers between devices with their start and end apart: 2 -> 8, of which waited for: 2 -> 5; matrix products, arithmetic and copies ran while one was open for 0% -> 2% of each run, Pallas kernels for 0% -> 8%
where the time goes in v4:
time: 105 us
  blocking collectives  38.3 us (36%)
  starting transfers between devices  28.8 us (27%)
  Pallas kernels  18 us (17%)
  waiting for transfers between devices  13.2 us (13%)
  other arithmetic  4.15 us (4%)
  local copies, waits for them, and re-layouts  1.35 us (1%)
    pallas_call x10, Pallas kernels, call(): pl.pallas_call(kernel, in_specs=in_specs, out_shape=out_shape, compiler_p...  18 us
    all_to_all x1, blocking collectives, on_device(): whole = lax.all_to_all(copies, F, 0, 0)  15 us
    ppermute x4, starting transfers between devices, swap(): return lax.ppermute(value, 'core', [(0, 1), (1, 0)])  14.8 us
    all_to_all x1, blocking collectives, on_device(): lax.all_to_all(sent, F, 0, 0)  12.3 us
    all_to_all x1, blocking collectives, on_device(): lax.all_to_all(copies, 'z', 0, 0)  11 us
    all_to_all x1, waiting for transfers between devices, on_device(): basis = lax.all_to_all(copies, F, 0, 0)  10.5 us
    all_to_all x1, starting transfers between devices, on_device(): basis = lax.all_to_all(copies, F, 0, 0)  6.75 us
    add x2, other arithmetic, merged(): grad.astype(jnp.float32)  4.07 us
  transfers between devices with their start and end apart: 8, of which 5 were waited for; matrix products, arithmetic and copies ran while one was open for 2% of the time, Pallas kernels for 8%

profile of v4, /device:TPU:1, one launch (start us, length us, event | category | flops | bytes accessed | tf_op | source)
XLA Modules:
  0.0 104.6 jit_solution(7386975628595903458)
XLA Ops:
  0.6 2.0 %add_bitcast_fusion.1.other_ref.merged_ref = f32[64,8192]{1,0:T(8,128)S(1)} fusion(f32[1,2,64,8192]{3,2,1,0:T(8,128)} %param.4, s32[]{:T(128)S(6)} %select_n.18, bf16[1,2,64,8192]{3,2,1,0:T(8,128)(2,1)} %param.3), kind=kLoop, calls=%fused_computation.1 | loop fusion | flops 1048576 | bytes 5242884 | tf_op jit(solution)/shard_map/add | solution.py:252
  2.7 0.1 pad_add_fusion.place_ref
  2.8 2.2 %quarters.1 = (f32[64,4096]{1,0:T(8,128)}, f32[64,4096]{1,0:T(8,128)}) custom-call(s32[4]{0:T(128)S(1)} %pad_add_fusion.place_ref, f32[64,8192]{1,0:T(8,128)S(1)} %add_bitcast_fusion.1.other_ref.merged_ref), custom_call_target="tpu_custom_call" | custom-call | tf_op jit(solution)/shard_map/quarters/pallas_call | solution.py:23
  4.9 0.0 copy-start
  4.9 1.3 %copy-done = f32[64,8192]{1,0:T(8,128)} copy-done((f32[64,8192]{1,0:T(8,128)}, f32[64,8192]{1,0:T(8,128)S(1)}, u32[]{:S(2)}) %copy-start) | copy-done | bytes 2097176
  6.3 3.2 %collective-permute-start.1 = (f32[64,4096]{1,0:T(8,128)}, f32[64,4096]{1,0:T(8,128)S(1)}, u32[]{:S(2)}, u32[]{:S(2)}) collective-permute-start(f32[64,4096]{1,0:T(8,128)} %get-tuple-element.19), channel_id=1, source_target_pairs={{0,16},{16,0},{1,17},{17,1},{2,18},{18,2},{3,19},{19,3},{4,20},{20... | collective-permute-start | bytes 3145736 | tf_op jit(solution)/shard_map/ppermute | solution.py:34
  9.5 0.0 collective-permute-start
  9.5 2.0 %add_bitcast_fusion.own_ref.merged_ref = f32[64,8192]{1,0:T(8,128)S(1)} fusion(f32[1,2,64,8192]{3,2,1,0:T(8,128)} %param.4, s32[]{:T(128)S(6)} %select_n.19, bf16[1,2,64,8192]{3,2,1,0:T(8,128)(2,1)} %param.3), kind=kLoop, calls=%fused_computation | loop fusion | flops 1048576 | bytes 5242884 | tf_op jit(solution)/shard_map/add | solution.py:252
  11.6 0.0 copy-start.2
  11.6 1.6 %collective-permute-done.1.got_ref = f32[64,4096]{1,0:T(8,128)S(1)} collective-permute-done((f32[64,4096]{1,0:T(8,128)}, f32[64,4096]{1,0:T(8,128)S(1)}, u32[]{:S(2)}, u32[]{:S(2)}) %collective-permute-start.1) | collective-permute-done | bytes 1048608 | tf_op jit(solution)/shard_map/ppermute | solution.py:34
  13.1 1.7 %give.1 = (f32[64,2048]{1,0:T(8,128)}, f32[64,2048]{1,0:T(8,128)}) custom-call(s32[4]{0:T(128)S(1)} %pad_add_fusion.place_ref, f32[64,8192]{1,0:T(8,128)S(1)} %add_bitcast_fusion.own_ref.merged_ref, f32[64,4096]{1,0:T(8,128)S(1)} %collective-permute-done.1.got_ref), custom_call_target="tpu_custom_call" | custom-call | tf_op jit(solution)/shard_map/give/pallas_call | solution.py:23
  14.9 3.8 %collective-permute-start.3 = (f32[64,2048]{1,0:T(8,128)}, f32[64,2048]{1,0:T(8,128)S(1)}, u32[]{:S(2)}, u32[]{:S(2)}) collective-permute-start(f32[64,2048]{1,0:T(8,128)} %get-tuple-element.21), channel_id=1, source_target_pairs={{0,224},{32,0},{64,32},{96,64},{128,96},{160,128},{192,160},{224,1... | collective-permute-start | bytes 1572872 | tf_op jit(solution)/shard_map/ppermute | solution.py:39
  18.7 0.0 collective-permute-start.2
  18.7 0.0 copy-done.2
  18.7 1.4 %basis.1 = f32[16,32,256]{2,1,0:T(8,128)} custom-call(s32[4]{0:T(128)S(1)} %pad_add_fusion.place_ref, f32[2,32,512]{2,1,0:T(8,128)S(1)} %copy-done.2, f32[64,2048]{1,0:T(8,128)} %get-tuple-element.20._), custom_call_target="tpu_custom_call" | custom-call | tf_op jit(solution)/shard_map/basis/pallas_call | solution.py:23
  20.1 6.8 %all-to-all-start = ((f32[16,32,256]{2,1,0:T(8,128)}), f32[16,32,256]{2,1,0:T(8,128)S(1)}, u32[]{:S(2)}, u32[]{:S(2)}) async-start(f32[16,32,256]{2,1,0:T(8,128)} %basis.1), calls=%async_computation | async-start | bytes 1048576 | tf_op jit(solution)/shard_map/all_to_all | solution.py:269
  26.9 0.0 collective-permute-done.got_ref
  26.9 10.5 %all-to-all-done.basis_ref = f32[16,32,256]{2,1,0:T(8,128)S(1)} async-done(((f32[16,32,256]{2,1,0:T(8,128)}), f32[16,32,256]{2,1,0:T(8,128)S(1)}, u32[]{:S(2)}, u32[]{:S(2)}) %all-to-all-start) | async-done | bytes 524320 | tf_op jit(solution)/shard_map/all_to_all | solution.py:269
  37.4 0.0 collective-permute-done.3.down_ref
  37.4 0.0 collective-permute-done.2.up_ref
  37.4 2.5 %left.1 = (f32[8,16,128]{2,1,0:T(8,128)S(1)}, f32[64,4096]{1,0:T(8,128)S(1)}) custom-call(s32[4]{0:T(128)S(1)} %pad_add_fusion.place_ref, f32[64,8192]{1,0:T(8,128)S(1)} %add_bitcast_fusion.own_ref.merged_ref, f32[64,4096]{1,0:T(8,128)} %collective-permute-done.got_ref, f32[64,2048]{1,0:T(8,128)} %collective-permute-done.2.up_ref, ...), custom_call_target="tpu_custom_call" | custom-call | tf_op jit(solution)/shard_map/left/pallas_call | solution.py:23
  39.9 11.0 %all_to_all.25.packed_ref = f32[8,16,128]{2,1,0:T(8,128)S(1)} all-to-all(f32[8,16,128]{2,1,0:T(8,128)S(1)} %get-tuple-element.22), channel_id=1, replica_groups=mesh['z'=8,'core'=2,'y'=4,'x'=4] {'z'}, dimensions={0} | all-to-all | bytes 131072 | tf_op jit(solution)/shard_map/all_to_all | solution.py:276
  50.9 0.6 terms.1
  51.5 12.3 %all_to_all.26.got_ref = f32[16,9,8,128]{3,2,1,0:T(8,128)S(1)} all-to-all(f32[16,9,8,128]{3,2,1,0:T(8,128)S(1)} %get-tuple-element.24), channel_id=1, replica_groups=mesh['z'=8,'core'=2,'y'=4,'x'=4] {'y','x'}, dimensions={0} | all-to-all | bytes 1179648 | tf_op jit(solution)/shard_map/all_to_all | solution.py:280
  63.9 0.7 columns.1
  64.6 3.4 %all-to-all-start.3 = ((f32[8,8,8,128]{3,2,1,0:T(8,128)}), f32[8,8,8,128]{3,2,1,0:T(8,128)S(1)}, u32[]{:S(2)}, u32[]{:S(2)}) async-start(f32[8,8,8,128]{3,2,1,0:T(8,128)} %get-tuple-element.27), calls=%async_computation.3 | async-start | bytes 524288 | tf_op jit(solution)/shard_map/all_to_all | solution.py:290
  68.0 3.5 %factors.1.factors_ref = f32[96,32]{1,0:T(8,128)S(1)} custom-call(f32[8,128]{1,0:T(8,128)S(1)} %get-tuple-element.25.gram_ref, f32[32,64]{1,0:T(8,128)S(1)} %get-tuple-element.26.left_ref), custom_call_target="tpu_custom_call" | custom-call | tf_op jit(solution)/shard_map/factors/pallas_call | solution.py:23
  71.6 4.7 %collective-permute-start.4 = (f32[96,32]{1,0:T(8,128)S(1)}, f32[96,32]{1,0:T(8,128)S(1)}, u32[]{:S(2)}, u32[]{:S(2)}) collective-permute-start(f32[96,32]{1,0:T(8,128)S(1)} %factors.1.factors_ref), channel_id=1, source_target_pairs={{0,16},{16,0},{1,17},{17,1},{2,18},{18,2},{3,19},{19,3},{4,20},{20... | collective-permute-start | bytes 36872 | tf_op jit(solution)/shard_map/ppermute | solution.py:34
  76.3 0.9 collective-permute-done.4._.factors_ref
  77.2 0.2 all-to-all-done.3.got_ref
  77.4 0.3 shard.1
  77.7 15.0 %all_to_all.27.right_ref = f32[16,32,512]{2,1,0:T(8,128)S(1)} all-to-all(f32[16,32,512]{2,1,0:T(8,128)S(1)} %get-tuple-element.28), channel_id=1, replica_groups=mesh['z'=8,'core'=2,'y'=4,'x'=4] {'y','x'}, dimensions={0} | all-to-all | bytes 2097152 | tf_op jit(solution)/shard_map/all_to_all | solution.py:292
  92.6 0.0 copy-start.1
  92.6 6.8 %collective-permute-start.5 = (f32[16,32,512]{2,1,0:T(8,128)S(1)}, f32[16,32,512]{2,1,0:T(8,128)S(1)}, u32[]{:S(2)}, u32[]{:S(2)}) collective-permute-start(f32[16,32,512]{2,1,0:T(8,128)S(1)} %all_to_all.27.right_ref), channel_id=1, source_target_pairs={{0,16},{16,0},{1,17},{17,1},{2,18},{18,2},{3,19},{19,3},{4,20},{20... | collective-permute-start | bytes 3145736 | tf_op jit(solution)/shard_map/ppermute | solution.py:34
  99.5 2.2 %residual_own.1._ = f32[1,2,64,8192]{3,2,1,0:T(8,128)} custom-call(s32[4]{0:T(128)S(1)} %pad_add_fusion.place_ref, f32[64,8192]{1,0:T(8,128)S(1)} %add_bitcast_fusion.own_ref.merged_ref, f32[96,32]{1,0:T(8,128)S(1)} %factors.1.factors_ref, f32[16,32,512]{2,1,0:T(8,128)S(1)} %all_to_all.27.right_ref), custom_call_target="tpu_custom_call" | custom-call | tf_op jit(solution)/shard_map/residual_own/pallas_call | solution.py:23
  101.7 0.1 collective-permute-done.5.right_ref
  101.8 0.0 copy-done.1
  101.8 2.8 %residual_other.1 = (f32[1,2,64,8192]{3,2,1,0:T(8,128)}, f32[2,32,512]{2,1,0:T(8,128)}) custom-call(s32[4]{0:T(128)S(1)} %pad_add_fusion.place_ref, f32[64,8192]{1,0:T(8,128)S(1)} %copy-done.1, f32[96,32]{1,0:T(8,128)S(1)} %collective-permute-done.4._.factors_ref, ...), custom_call_target="tpu_custom_call", output_to_operand_aliasing={{0}: (5, {})} | custom-call | tf_op jit(solution)/shard_map/residual_other/pallas_call | solution.py:23
Async XLA Ops:
  4.9 1.3 %copy-start = (f32[64,8192]{1,0:T(8,128)}, f32[64,8192]{1,0:T(8,128)S(1)}, u32[]{:S(2)}) copy-start(f32[64,8192]{1,0:T(8,128)S(1)} %add_bitcast_fusion.1.other_ref.merged_ref) | copy-start | bytes 6291460
  6.3 6.9 %collective-permute-start.1 = (f32[64,4096]{1,0:T(8,128)}, f32[64,4096]{1,0:T(8,128)S(1)}, u32[]{:S(2)}, u32[]{:S(2)}) collective-permute-start(f32[64,4096]{1,0:T(8,128)} %get-tuple-element.19), channel_id=1, source_target_pairs={{0,16},{16,0},{1,17},{17,1},{2,18},{18,2},{3,19},{19,3},{4,20},{20... | collective-permute-start | bytes 3145736 | tf_op jit(solution)/shard_map/ppermute | solution.py:34
  9.5 17.4 %collective-permute-start = (f32[64,4096]{1,0:T(8,128)}, f32[64,4096]{1,0:T(8,128)}, u32[]{:S(2)}, u32[]{:S(2)}) collective-permute-start(f32[64,4096]{1,0:T(8,128)} %get-tuple-element.18), channel_id=1, source_target_pairs={{0,16},{16,0},{1,17},{17,1},{2,18},{18,2},{3,19},{19,3},{4,20},{20... | collective-permute-start | bytes 3145736 | tf_op jit(solution)/shard_map/ppermute | solution.py:34
  11.6 7.1 %copy-start.2 = (f32[2,32,512]{2,1,0:T(8,128)S(1)}, f32[2,32,512]{2,1,0:T(8,128)}, u32[]{:S(2)}) copy-start(f32[2,32,512]{2,1,0:T(8,128)} %basis_ref.1) | copy-start | bytes 393220
  14.9 22.5 %collective-permute-start.3 = (f32[64,2048]{1,0:T(8,128)}, f32[64,2048]{1,0:T(8,128)S(1)}, u32[]{:S(2)}, u32[]{:S(2)}) collective-permute-start(f32[64,2048]{1,0:T(8,128)} %get-tuple-element.21), channel_id=1, source_target_pairs={{0,224},{32,0},{64,32},{96,64},{128,96},{160,128},{192,160},{224,1... | collective-permute-start | bytes 1572872 | tf_op jit(solution)/shard_map/ppermute | solution.py:39
  18.7 18.7 %collective-permute-start.2 = (f32[64,2048]{1,0:T(8,128)}, f32[64,2048]{1,0:T(8,128)}, u32[]{:S(2)}, u32[]{:S(2)}) collective-permute-start(f32[64,2048]{1,0:T(8,128)} %get-tuple-element.20._), channel_id=1, source_target_pairs={{0,32},{32,64},{64,96},{96,128},{128,160},{160,192},{192,224},{224... | collective-permute-start | bytes 1572872 | tf_op jit(solution)/shard_map/ppermute | solution.py:39
  20.1 17.2 %all-to-all-start = ((f32[16,32,256]{2,1,0:T(8,128)}), f32[16,32,256]{2,1,0:T(8,128)S(1)}, u32[]{:S(2)}, u32[]{:S(2)}) async-start(f32[16,32,256]{2,1,0:T(8,128)} %basis.1), calls=%async_computation | async-start | bytes 1048576 | tf_op jit(solution)/shard_map/all_to_all | solution.py:269
  64.6 12.8 %all-to-all-start.3 = ((f32[8,8,8,128]{3,2,1,0:T(8,128)}), f32[8,8,8,128]{3,2,1,0:T(8,128)S(1)}, u32[]{:S(2)}, u32[]{:S(2)}) async-start(f32[8,8,8,128]{3,2,1,0:T(8,128)} %get-tuple-element.27), calls=%async_computation.3 | async-start | bytes 524288 | tf_op jit(solution)/shard_map/all_to_all | solution.py:290
  71.6 5.6 %collective-permute-start.4 = (f32[96,32]{1,0:T(8,128)S(1)}, f32[96,32]{1,0:T(8,128)S(1)}, u32[]{:S(2)}, u32[]{:S(2)}) collective-permute-start(f32[96,32]{1,0:T(8,128)S(1)} %factors.1.factors_ref), channel_id=1, source_target_pairs={{0,16},{16,0},{1,17},{17,1},{2,18},{18,2},{3,19},{19,3},{4,20},{20... | collective-permute-start | bytes 36872 | tf_op jit(solution)/shard_map/ppermute | solution.py:34
  92.6 9.1 %copy-start.1 = (f32[64,8192]{1,0:T(8,128)S(1)}, f32[64,8192]{1,0:T(8,128)}, u32[]{:S(2)}) copy-start(f32[64,8192]{1,0:T(8,128)} %copy-done) | copy-start | bytes 6291460
  92.6 9.1 %collective-permute-start.5 = (f32[16,32,512]{2,1,0:T(8,128)S(1)}, f32[16,32,512]{2,1,0:T(8,128)S(1)}, u32[]{:S(2)}, u32[]{:S(2)}) collective-permute-start(f32[16,32,512]{2,1,0:T(8,128)S(1)} %all_to_all.27.right_ref), channel_id=1, source_target_pairs={{0,16},{16,0},{1,17},{17,1},{2,18},{18,2},{3,19},{19,3},{4,20},{20... | collective-permute-start | bytes 3145736 | tf_op jit(solution)/shard_map/ppermute | solution.py:34

commit v5 on v4

--- a/solution.py
+++ b/solution.py
@@ -57,12 +57,49 @@
     return ref[:, start : start + LANES]
 
 
-def other_kernel(place_ref, other_ref, give_ref, keep_ref):
+def merge(index, grad_ref, error_ref, out_ref, grad_buf, error_buf, sems):
+    groups = sems.shape[1]
+    width = out_ref.shape[1] // groups
+    copies = []
+    for group in range(groups):
+        columns = pl.ds(group * width, width)
+        pair = (
+            pltpu.make_async_copy(
+                grad_ref.at[0, index, :, columns], grad_buf.at[:, columns], sems.at[0, group]
+            ),
+            pltpu.make_async_copy(
+                error_ref.at[0, index, :, columns], error_buf.at[:, columns], sems.at[1, group]
+            ),
+        )
+        for copy in pair:
+            copy.start()
+        copies.append(pair)
+    for group, pair in enumerate(copies):
+        columns = pl.ds(group * width, width)
+        for copy in pair:
+            copy.wait()
+        out_ref[:, columns] = grad_buf[:, columns].astype(jnp.float32) + error_buf[:, columns]
+
+
+def merge_scratch(rows, width, groups=4):
+    return [
+        pltpu.VMEM((rows, width), jnp.bfloat16),
+        pltpu.VMEM((rows, width), jnp.float32),
+        pltpu.SemaphoreType.DMA((2, groups)),
+    ]
+
+
+def other_kernel(place_ref, grad_ref, error_ref, other_ref, give_ref, keep_ref, *scratch):
+    merge(place_ref[1], grad_ref, error_ref, other_ref, *scratch)
     for out_ref, quarters in ((give_ref, given(place_ref)), (keep_ref, kept(place_ref))):
         for chunk in range(other_ref.shape[1] // (4 * LANES)):
             for slot, which in enumerate(quarters):
                 start = (2 * chunk + slot) * LANES
                 out_ref[:, start : start + LANES] = quarter(other_ref, chunk, which)
+
+
+def own_kernel(place_ref, grad_ref, error_ref, own_ref, *scratch):
+    merge(place_ref[0], grad_ref, error_ref, own_ref, *scratch)
 
 
 def give_kernel(place_ref, own_ref, got_ref, *out_refs):
@@ -247,17 +284,21 @@
     shards = width // part
     place = jnp.stack([core, 1 - core, lax.axis_index(F), lax.axis_index("z") % 2])
 
-    def merged(index):
-        grad = lax.dynamic_index_in_dim(grad_pair[0], index, 0, False)
-        return grad.astype(jnp.float32) + lax.dynamic_index_in_dim(error_pair[0], index, 0, False)
-
+    inputs = [
+        pltpu.with_memory_space_constraint(array, pltpu.HBM) for array in (grad_pair, error_pair)
+    ]
+    merging = dict(scratch_shapes=merge_scratch(rows, width))
     by_two, by_four = f32(rows, width // 2), f32(rows, width // 4)
 
-    other = merged(1 - core)
-    give, keep = call(other_kernel, "quarters", [SMEM, VMEM], (by_two, by_two), (place, other))
-    give, index = lax.optimization_barrier((give, core))
+    other, give, keep = call(
+        other_kernel, "merge_other", [SMEM, ANY, ANY], (f32(rows, width), by_two, by_two),
+        (place, *inputs), out_specs=(VMEM, VMEM, VMEM), **merging,
+    )
     give, keep = swap(give), swap(keep)
-    own = merged(index)
+    own = call(
+        own_kernel, "merge_own", [SMEM, ANY, ANY], f32(rows, width),
+        (place, *inputs), out_specs=VMEM, **merging,
+    )
     up, down = call(
         give_kernel, "give", [SMEM, VMEM, VMEM], (by_four, by_four), (place, own, give)
     )

time: 105 us -> 102 us (0.971)
  other arithmetic: 4.15 us -> 0.08 us
  Pallas kernels: 18 us -> 22 us
  waiting for transfers between devices: 13.2 us -> 11.7 us
  local copies, waits for them, and re-layouts: 1.35 us -> 0.01 us
    add x2 -> x0, other arithmetic: 4.07 us -> none  [merged(): grad.astype(jnp.float32)]
    pallas_call x10 -> x11, Pallas kernels: 18 us -> 22 us  [call(): pl.pallas_call(kernel, in_specs=in_specs, out_shape=out_shape, compiler_p...]
    ppermute x4, waiting for transfers between devices: 2.58 us -> 1.03 us  [swap(): return lax.ppermute(value, 'core', [(0, 1), (1, 0)])]
    unnamed x6, local copies, waits for them, and re-layouts: 1.35 us -> 0.01 us
  transfers between devices with their start and end apart: 8 -> 8, of which waited for: 5 -> 4; matrix products, arithmetic and copies ran while one was open for 2% -> 0% of each run, Pallas kernels for 8% -> 11%
where the time goes in v5:
time: 102 us
  blocking collectives  38.3 us (38%)
  starting transfers between devices  29.1 us (29%)
  Pallas kernels  22 us (22%)
  waiting for transfers between devices  11.7 us (11%)
    pallas_call x11, Pallas kernels, call(): pl.pallas_call(kernel, in_specs=in_specs, out_shape=out_shape, compiler_p...  22 us
    ppermute x4, starting transfers between devices, swap(): return lax.ppermute(value, 'core', [(0, 1), (1, 0)])  15 us
    all_to_all x1, blocking collectives, on_device(): whole = lax.all_to_all(copies, F, 0, 0)  15 us
    all_to_all x1, blocking collectives, on_device(): lax.all_to_all(sent, F, 0, 0)  12.3 us
    all_to_all x1, blocking collectives, on_device(): lax.all_to_all(copies, 'z', 0, 0)  11 us
    all_to_all x1, waiting for transfers between devices, on_device(): basis = lax.all_to_all(copies, F, 0, 0)  10.5 us
    all_to_all x1, starting transfers between devices, on_device(): basis = lax.all_to_all(copies, F, 0, 0)  6.75 us
    ppermute x2, starting transfers between devices, shift(): lax.ppermute(value, 'z', [(i, (i + step) % count) for i in range(count)])  3.86 us
  transfers between devices with their start and end apart: 8, of which 4 were waited for; matrix products, arithmetic and copies ran while one was open for 0% of the time, Pallas kernels for 11%

profile of v5, /device:TPU:1, one launch (start us, length us, event | category | flops | bytes accessed | tf_op | source)
XLA Modules:
  0.0 101.9 jit_solution(2685161842478145316)
XLA Ops:
  0.6 0.1 pad_add_fusion.place_ref
  0.7 3.8 %merge_other.1 = (f32[64,8192]{1,0:T(8,128)S(1)}, f32[64,4096]{1,0:T(8,128)S(1)}, f32[64,4096]{1,0:T(8,128)}) custom-call(s32[4]{0:T(128)S(1)} %pad_add_fusion.place_ref, bf16[1,2,64,8192]{3,2,1,0:T(8,128)(2,1)} %grad_ref.3, f32[1,2,64,8192]{3,2,1,0:T(8,128)} %error_ref.3), custom_call_target="tpu_custom_call" | custom-call | tf_op jit(solution)/shard_map/merge_other/pallas_call | solution.py:23
  4.5 0.0 copy-start
  4.5 3.3 %collective-permute-start.1 = (f32[64,4096]{1,0:T(8,128)S(1)}, f32[64,4096]{1,0:T(8,128)S(1)}, u32[]{:S(2)}, u32[]{:S(2)}) collective-permute-start(f32[64,4096]{1,0:T(8,128)S(1)} %get-tuple-element.17), channel_id=1, source_target_pairs={{0,16},{16,0},{1,17},{17,1},{2,18},{18,2},{3,19},{19,3},{4,20},{20... | collective-permute-start | bytes 3145736 | tf_op jit(solution)/shard_map/ppermute | solution.py:34
  7.8 0.0 copy-start.2
  7.8 0.1 collective-permute-start
  7.9 2.5 %merge_own.1.own_ref.merged_ref = f32[64,8192]{1,0:T(8,128)S(1)} custom-call(s32[4]{0:T(128)S(1)} %pad_add_fusion.place_ref, bf16[1,2,64,8192]{3,2,1,0:T(8,128)(2,1)} %grad_ref.3, f32[1,2,64,8192]{3,2,1,0:T(8,128)} %error_ref.3), custom_call_target="tpu_custom_call" | custom-call | tf_op jit(solution)/shard_map/merge_own/pallas_call | solution.py:23
  10.4 0.0 copy-done
  10.5 0.0 collective-permute-done.1.got_ref
  10.5 1.7 %give.1 = (f32[64,2048]{1,0:T(8,128)}, f32[64,2048]{1,0:T(8,128)}) custom-call(s32[4]{0:T(128)S(1)} %pad_add_fusion.place_ref, f32[64,8192]{1,0:T(8,128)S(1)} %merge_own.1.own_ref.merged_ref, f32[64,4096]{1,0:T(8,128)S(1)} %collective-permute-done.1.got_ref), custom_call_target="tpu_custom_call" | custom-call | tf_op jit(solution)/shard_map/give/pallas_call | solution.py:23
  12.2 3.9 %collective-permute-start.3 = (f32[64,2048]{1,0:T(8,128)}, f32[64,2048]{1,0:T(8,128)S(1)}, u32[]{:S(2)}, u32[]{:S(2)}) collective-permute-start(f32[64,2048]{1,0:T(8,128)} %get-tuple-element.19), channel_id=1, source_target_pairs={{0,224},{32,0},{64,32},{96,64},{128,96},{160,128},{192,160},{224,1... | collective-permute-start | bytes 1572872 | tf_op jit(solution)/shard_map/ppermute | solution.py:39
  16.1 0.0 collective-permute-start.2
  16.1 0.0 copy-done.2
  16.1 1.4 %basis.1 = f32[16,32,256]{2,1,0:T(8,128)} custom-call(s32[4]{0:T(128)S(1)} %pad_add_fusion.place_ref, f32[2,32,512]{2,1,0:T(8,128)S(1)} %copy-done.2, f32[64,2048]{1,0:T(8,128)} %get-tuple-element.18._), custom_call_target="tpu_custom_call" | custom-call | tf_op jit(solution)/shard_map/basis/pallas_call | solution.py:23
  17.5 6.8 %all-to-all-start = ((f32[16,32,256]{2,1,0:T(8,128)}), f32[16,32,256]{2,1,0:T(8,128)S(1)}, u32[]{:S(2)}, u32[]{:S(2)}) async-start(f32[16,32,256]{2,1,0:T(8,128)} %basis.1), calls=%async_computation | async-start | bytes 1048576 | tf_op jit(solution)/shard_map/all_to_all | solution.py:310
  24.2 0.0 collective-permute-done.got_ref
  24.2 10.5 %all-to-all-done.basis_ref = f32[16,32,256]{2,1,0:T(8,128)S(1)} async-done(((f32[16,32,256]{2,1,0:T(8,128)}), f32[16,32,256]{2,1,0:T(8,128)S(1)}, u32[]{:S(2)}, u32[]{:S(2)}) %all-to-all-start) | async-done | bytes 524320 | tf_op jit(solution)/shard_map/all_to_all | solution.py:310
  34.7 0.0 collective-permute-done.3.down_ref
  34.7 0.0 collective-permute-done.2.up_ref
  34.7 2.5 %left.1 = (f32[8,16,128]{2,1,0:T(8,128)S(1)}, f32[64,4096]{1,0:T(8,128)S(1)}) custom-call(s32[4]{0:T(128)S(1)} %pad_add_fusion.place_ref, f32[64,8192]{1,0:T(8,128)S(1)} %merge_own.1.own_ref.merged_ref, f32[64,4096]{1,0:T(8,128)} %collective-permute-done.got_ref, f32[64,2048]{1,0:T(8,128)} %collective-permute-done.2.up_ref, ...), custom_call_target="tpu_custom_call" | custom-call | tf_op jit(solution)/shard_map/left/pallas_call | solution.py:23
  37.2 11.0 %all_to_all.25.packed_ref = f32[8,16,128]{2,1,0:T(8,128)S(1)} all-to-all(f32[8,16,128]{2,1,0:T(8,128)S(1)} %get-tuple-element.20), channel_id=1, replica_groups=mesh['z'=8,'core'=2,'y'=4,'x'=4] {'z'}, dimensions={0} | all-to-all | bytes 131072 | tf_op jit(solution)/shard_map/all_to_all | solution.py:317
  48.2 0.6 terms.1
  48.8 12.3 %all_to_all.26.got_ref = f32[16,9,8,128]{3,2,1,0:T(8,128)S(1)} all-to-all(f32[16,9,8,128]{3,2,1,0:T(8,128)S(1)} %get-tuple-element.22), channel_id=1, replica_groups=mesh['z'=8,'core'=2,'y'=4,'x'=4] {'y','x'}, dimensions={0} | all-to-all | bytes 1179648 | tf_op jit(solution)/shard_map/all_to_all | solution.py:321
  61.2 0.7 columns.1
  61.9 3.4 %all-to-all-start.3 = ((f32[8,8,8,128]{3,2,1,0:T(8,128)}), f32[8,8,8,128]{3,2,1,0:T(8,128)S(1)}, u32[]{:S(2)}, u32[]{:S(2)}) async-start(f32[8,8,8,128]{3,2,1,0:T(8,128)} %get-tuple-element.25), calls=%async_computation.3 | async-start | bytes 524288 | tf_op jit(solution)/shard_map/all_to_all | solution.py:331
  65.3 3.5 %factors.1.factors_ref = f32[96,32]{1,0:T(8,128)S(1)} custom-call(f32[8,128]{1,0:T(8,128)S(1)} %get-tuple-element.23.gram_ref, f32[32,64]{1,0:T(8,128)S(1)} %get-tuple-element.24.left_ref), custom_call_target="tpu_custom_call" | custom-call | tf_op jit(solution)/shard_map/factors/pallas_call | solution.py:23
  68.9 4.7 %collective-permute-start.4 = (f32[96,32]{1,0:T(8,128)S(1)}, f32[96,32]{1,0:T(8,128)S(1)}, u32[]{:S(2)}, u32[]{:S(2)}) collective-permute-start(f32[96,32]{1,0:T(8,128)S(1)} %factors.1.factors_ref), channel_id=1, source_target_pairs={{0,16},{16,0},{1,17},{17,1},{2,18},{18,2},{3,19},{19,3},{4,20},{20... | collective-permute-start | bytes 36872 | tf_op jit(solution)/shard_map/ppermute | solution.py:34
  73.6 0.9 collective-permute-done.4._.factors_ref
  74.5 0.2 all-to-all-done.3.got_ref
  74.7 0.3 shard.1
  75.0 15.0 %all_to_all.27.right_ref = f32[16,32,512]{2,1,0:T(8,128)S(1)} all-to-all(f32[16,32,512]{2,1,0:T(8,128)S(1)} %get-tuple-element.26), channel_id=1, replica_groups=mesh['z'=8,'core'=2,'y'=4,'x'=4] {'y','x'}, dimensions={0} | all-to-all | bytes 2097152 | tf_op jit(solution)/shard_map/all_to_all | solution.py:333
  89.9 0.0 copy-start.1
  89.9 6.8 %collective-permute-start.5 = (f32[16,32,512]{2,1,0:T(8,128)S(1)}, f32[16,32,512]{2,1,0:T(8,128)S(1)}, u32[]{:S(2)}, u32[]{:S(2)}) collective-permute-start(f32[16,32,512]{2,1,0:T(8,128)S(1)} %all_to_all.27.right_ref), channel_id=1, source_target_pairs={{0,16},{16,0},{1,17},{17,1},{2,18},{18,2},{3,19},{19,3},{4,20},{20... | collective-permute-start | bytes 3145736 | tf_op jit(solution)/shard_map/ppermute | solution.py:34
  96.8 2.2 %residual_own.1._ = f32[1,2,64,8192]{3,2,1,0:T(8,128)} custom-call(s32[4]{0:T(128)S(1)} %pad_add_fusion.place_ref, f32[64,8192]{1,0:T(8,128)S(1)} %merge_own.1.own_ref.merged_ref, f32[96,32]{1,0:T(8,128)S(1)} %factors.1.factors_ref, f32[16,32,512]{2,1,0:T(8,128)S(1)} %all_to_all.27.right_ref), custom_call_target="tpu_custom_call" | custom-call | tf_op jit(solution)/shard_map/residual_own/pallas_call | solution.py:23
  99.0 0.1 collective-permute-done.5.right_ref
  99.1 0.0 copy-done.1
  99.1 2.8 %residual_other.1 = (f32[1,2,64,8192]{3,2,1,0:T(8,128)}, f32[2,32,512]{2,1,0:T(8,128)}) custom-call(s32[4]{0:T(128)S(1)} %pad_add_fusion.place_ref, f32[64,8192]{1,0:T(8,128)S(1)} %copy-done.1, f32[96,32]{1,0:T(8,128)S(1)} %collective-permute-done.4._.factors_ref, ...), custom_call_target="tpu_custom_call", output_to_operand_aliasing={{0}: (5, {})} | custom-call | tf_op jit(solution)/shard_map/residual_other/pallas_call | solution.py:23
Async XLA Ops:
  4.5 6.0 %copy-start = (f32[64,8192]{1,0:T(8,128)}, f32[64,8192]{1,0:T(8,128)S(1)}, u32[]{:S(2)}) copy-start(f32[64,8192]{1,0:T(8,128)S(1)} %get-tuple-element.15.merged_ref) | copy-start | bytes 6291460
  4.5 6.0 %collective-permute-start.1 = (f32[64,4096]{1,0:T(8,128)S(1)}, f32[64,4096]{1,0:T(8,128)S(1)}, u32[]{:S(2)}, u32[]{:S(2)}) collective-permute-start(f32[64,4096]{1,0:T(8,128)S(1)} %get-tuple-element.17), channel_id=1, source_target_pairs={{0,16},{16,0},{1,17},{17,1},{2,18},{18,2},{3,19},{19,3},{4,20},{20... | collective-permute-start | bytes 3145736 | tf_op jit(solution)/shard_map/ppermute | solution.py:34
  7.8 8.2 %copy-start.2 = (f32[2,32,512]{2,1,0:T(8,128)S(1)}, f32[2,32,512]{2,1,0:T(8,128)}, u32[]{:S(2)}) copy-start(f32[2,32,512]{2,1,0:T(8,128)} %basis_ref.1) | copy-start | bytes 393220
  7.8 16.4 %collective-permute-start = (f32[64,4096]{1,0:T(8,128)}, f32[64,4096]{1,0:T(8,128)}, u32[]{:S(2)}, u32[]{:S(2)}) collective-permute-start(f32[64,4096]{1,0:T(8,128)} %get-tuple-element.16), channel_id=1, source_target_pairs={{0,16},{16,0},{1,17},{17,1},{2,18},{18,2},{3,19},{19,3},{4,20},{20... | collective-permute-start | bytes 3145736 | tf_op jit(solution)/shard_map/ppermute | solution.py:34
  12.2 22.5 %collective-permute-start.3 = (f32[64,2048]{1,0:T(8,128)}, f32[64,2048]{1,0:T(8,128)S(1)}, u32[]{:S(2)}, u32[]{:S(2)}) collective-permute-start(f32[64,2048]{1,0:T(8,128)} %get-tuple-element.19), channel_id=1, source_target_pairs={{0,224},{32,0},{64,32},{96,64},{128,96},{160,128},{192,160},{224,1... | collective-permute-start | bytes 1572872 | tf_op jit(solution)/shard_map/ppermute | solution.py:39
  16.1 18.7 %collective-permute-start.2 = (f32[64,2048]{1,0:T(8,128)}, f32[64,2048]{1,0:T(8,128)}, u32[]{:S(2)}, u32[]{:S(2)}) collective-permute-start(f32[64,2048]{1,0:T(8,128)} %get-tuple-element.18._), channel_id=1, source_target_pairs={{0,32},{32,64},{64,96},{96,128},{128,160},{160,192},{192,224},{224... | collective-permute-start | bytes 1572872 | tf_op jit(solution)/shard_map/ppermute | solution.py:39
  17.5 17.2 %all-to-all-start = ((f32[16,32,256]{2,1,0:T(8,128)}), f32[16,32,256]{2,1,0:T(8,128)S(1)}, u32[]{:S(2)}, u32[]{:S(2)}) async-start(f32[16,32,256]{2,1,0:T(8,128)} %basis.1), calls=%async_computation | async-start | bytes 1048576 | tf_op jit(solution)/shard_map/all_to_all | solution.py:310
  61.9 12.8 %all-to-all-start.3 = ((f32[8,8,8,128]{3,2,1,0:T(8,128)}), f32[8,8,8,128]{3,2,1,0:T(8,128)S(1)}, u32[]{:S(2)}, u32[]{:S(2)}) async-start(f32[8,8,8,128]{3,2,1,0:T(8,128)} %get-tuple-element.25), calls=%async_computation.3 | async-start | bytes 524288 | tf_op jit(solution)/shard_map/all_to_all | solution.py:331
  68.9 5.6 %collective-permute-start.4 = (f32[96,32]{1,0:T(8,128)S(1)}, f32[96,32]{1,0:T(8,128)S(1)}, u32[]{:S(2)}, u32[]{:S(2)}) collective-permute-start(f32[96,32]{1,0:T(8,128)S(1)} %factors.1.factors_ref), channel_id=1, source_target_pairs={{0,16},{16,0},{1,17},{17,1},{2,18},{18,2},{3,19},{19,3},{4,20},{20... | collective-permute-start | bytes 36872 | tf_op jit(solution)/shard_map/ppermute | solution.py:34
  89.9 9.1 %copy-start.1 = (f32[64,8192]{1,0:T(8,128)S(1)}, f32[64,8192]{1,0:T(8,128)}, u32[]{:S(2)}) copy-start(f32[64,8192]{1,0:T(8,128)} %copy-done) | copy-start | bytes 6291460
  89.9 9.1 %collective-permute-start.5 = (f32[16,32,512]{2,1,0:T(8,128)S(1)}, f32[16,32,512]{2,1,0:T(8,128)S(1)}, u32[]{:S(2)}, u32[]{:S(2)}) collective-permute-start(f32[16,32,512]{2,1,0:T(8,128)S(1)} %all_to_all.27.right_ref), channel_id=1, source_target_pairs={{0,16},{16,0},{1,17},{17,1},{2,18},{18,2},{3,19},{19,3},{4,20},{20... | collective-permute-start | bytes 3145736 | tf_op jit(solution)/shard_map/ppermute | solution.py:34

commit v6 on v5

--- a/solution.py
+++ b/solution.py
@@ -57,7 +57,7 @@
     return ref[:, start : start + LANES]
 
 
-def merge(index, grad_ref, error_ref, out_ref, grad_buf, error_buf, sems):
+def merge(index, each, grad_ref, error_ref, out_ref, grad_buf, error_buf, sems):
     groups = sems.shape[1]
     width = out_ref.shape[1] // groups
     copies = []
@@ -79,6 +79,7 @@
         for copy in pair:
             copy.wait()
         out_ref[:, columns] = grad_buf[:, columns].astype(jnp.float32) + error_buf[:, columns]
+        each(range(group * width // (4 * LANES), (group + 1) * width // (4 * LANES)))
 
 
 def merge_scratch(rows, width, groups=4):
@@ -90,16 +91,18 @@
 
 
 def other_kernel(place_ref, grad_ref, error_ref, other_ref, give_ref, keep_ref, *scratch):
-    merge(place_ref[1], grad_ref, error_ref, other_ref, *scratch)
-    for out_ref, quarters in ((give_ref, given(place_ref)), (keep_ref, kept(place_ref))):
-        for chunk in range(other_ref.shape[1] // (4 * LANES)):
-            for slot, which in enumerate(quarters):
-                start = (2 * chunk + slot) * LANES
-                out_ref[:, start : start + LANES] = quarter(other_ref, chunk, which)
+    def sort(chunks):
+        for out_ref, quarters in ((give_ref, given(place_ref)), (keep_ref, kept(place_ref))):
+            for chunk in chunks:
+                for slot, which in enumerate(quarters):
+                    start = (2 * chunk + slot) * LANES
+                    out_ref[:, start : start + LANES] = quarter(other_ref, chunk, which)
+
+    merge(place_ref[1], sort, grad_ref, error_ref, other_ref, *scratch)
 
 
 def own_kernel(place_ref, grad_ref, error_ref, own_ref, *scratch):
-    merge(place_ref[0], grad_ref, error_ref, own_ref, *scratch)
+    merge(place_ref[0], lambda chunks: None, grad_ref, error_ref, own_ref, *scratch)
 
 
 def give_kernel(place_ref, own_ref, got_ref, *out_refs):
@@ -111,7 +114,8 @@
             )
 
 
-def basis_kernel(place_ref, basis_ref, _, copies_ref):
+def basis_kernel(place_ref, basis_ref, *rest):
+    copies_ref = rest[-1]
     columns = [
         basis_ref[place_ref[0], :, pl.ds(pl.multiple_of(which * LANES, LANES), LANES)]
         for which in kept(place_ref)
@@ -303,8 +307,8 @@
         give_kernel, "give", [SMEM, VMEM, VMEM], (by_four, by_four), (place, own, give)
     )
     copies = call(
-        basis_kernel, "basis", [SMEM, VMEM, ANY], f32(shards, rank, part // 2),
-        (place, basis_pair, up),
+        basis_kernel, "basis", [SMEM, VMEM, ANY, ANY], f32(shards, rank, part // 2),
+        (place, basis_pair, up, keep),
     )
     up, down = shift(up, 1), shift(down, -1)
     basis = lax.all_to_all(copies, F, 0, 0)

time: 102 us -> 98.4 us (0.965)
  blocking collectives: 38.3 us -> 55.3 us
  waiting for transfers between devices: 11.7 us -> 1.16 us
  starting transfers between devices: 29.1 us -> 22.4 us
  Pallas kernels: 22 us -> 18.3 us
    all_to_all x0 -> x1, blocking collectives: none -> 17.1 us  [on_device(): basis = lax.all_to_all(copies, F, 0, 0)]
    all_to_all x1 -> x0, waiting for transfers between devices: 10.5 us -> none  [on_device(): basis = lax.all_to_all(copies, F, 0, 0)]
    all_to_all x1 -> x0, starting transfers between devices: 6.75 us -> none  [on_device(): basis = lax.all_to_all(copies, F, 0, 0)]
    pallas_call x11, Pallas kernels: 22 us -> 18.3 us  [call(): pl.pallas_call(kernel, in_specs=in_specs, out_shape=out_shape, compiler_p...]
  transfers between devices with their start and end apart: 8 -> 7, of which waited for: 4 -> 3; matrix products, arithmetic and copies ran while one was open for 0% -> 0% of each run, Pallas kernels for 11% -> 10%
where the time goes in v6:
time: 98.4 us; the launch traced here: 98 us
  blocking collectives  55.3 us (56%)
  starting transfers between devices  22.4 us (23%)
  Pallas kernels  18.3 us (19%)
  waiting for transfers between devices  1.16 us (1%)
    pallas_call x11, Pallas kernels, call(): pl.pallas_call(kernel, in_specs=in_specs, out_shape=out_shape, compiler_p...  18.3 us
    all_to_all x1, blocking collectives, on_device(): basis = lax.all_to_all(copies, F, 0, 0)  17.1 us
    ppermute x4, starting transfers between devices, swap(): return lax.ppermute(value, 'core', [(0, 1), (1, 0)])  15.1 us
    all_to_all x1, blocking collectives, on_device(): whole = lax.all_to_all(copies, F, 0, 0)  15 us
    all_to_all x1, blocking collectives, on_device(): lax.all_to_all(sent, F, 0, 0)  12.3 us
    all_to_all x1, blocking collectives, on_device(): lax.all_to_all(copies, 'z', 0, 0)  10.9 us
    ppermute x2, starting transfers between devices, shift(): lax.ppermute(value, 'z', [(i, (i + step) % count) for i in range(count)])  3.93 us
    all_to_all x1, starting transfers between devices, on_device(): lax.all_to_all(sums, 'z', 0, 0)  3.41 us
  transfers between devices with their start and end apart: 7, of which 3 were waited for; matrix products, arithmetic and copies ran while one was open for 0% of the time, Pallas kernels for 10%

profile of v6, /device:TPU:1, one launch (start us, length us, event | category | flops | bytes accessed | tf_op | source)
XLA Modules:
  0.0 98.0 jit_solution(18072066800287707245)
XLA Ops:
  0.6 0.1 pad_add_fusion.place_ref
  0.7 2.6 %merge_other.1 = (f32[64,8192]{1,0:T(8,128)S(1)}, f32[64,4096]{1,0:T(8,128)S(1)}, f32[64,4096]{1,0:T(8,128)S(1)}) custom-call(s32[4]{0:T(128)S(1)} %pad_add_fusion.place_ref, bf16[1,2,64,8192]{3,2,1,0:T(8,128)(2,1)} %grad_ref.3, f32[1,2,64,8192]{3,2,1,0:T(8,128)} %error_ref.3), custom_call_target="tpu_custom_call" | custom-call | tf_op jit(solution)/shard_map/merge_other/pallas_call | solution.py:23
  3.3 0.0 copy-start
  3.3 3.3 %collective-permute-start.1 = (f32[64,4096]{1,0:T(8,128)S(1)}, f32[64,4096]{1,0:T(8,128)S(1)}, u32[]{:S(2)}, u32[]{:S(2)}) collective-permute-start(f32[64,4096]{1,0:T(8,128)S(1)} %get-tuple-element.17), channel_id=1, source_target_pairs={{0,16},{16,0},{1,17},{17,1},{2,18},{18,2},{3,19},{19,3},{4,20},{20... | collective-permute-start | bytes 3145736 | tf_op jit(solution)/shard_map/ppermute | solution.py:34
  6.7 0.0 copy-start.2
  6.7 0.1 collective-permute-start
  6.8 2.5 %merge_own.1.own_ref.merged_ref = f32[64,8192]{1,0:T(8,128)S(1)} custom-call(s32[4]{0:T(128)S(1)} %pad_add_fusion.place_ref, bf16[1,2,64,8192]{3,2,1,0:T(8,128)(2,1)} %grad_ref.3, f32[1,2,64,8192]{3,2,1,0:T(8,128)} %error_ref.3), custom_call_target="tpu_custom_call" | custom-call | tf_op jit(solution)/shard_map/merge_own/pallas_call | solution.py:23
  9.3 0.0 copy-done
  9.3 0.0 collective-permute-done.1.got_ref
  9.3 0.7 give.1
  10.0 3.9 %collective-permute-start.3 = (f32[64,2048]{1,0:T(8,128)S(1)}, f32[64,2048]{1,0:T(8,128)S(1)}, u32[]{:S(2)}, u32[]{:S(2)}) collective-permute-start(f32[64,2048]{1,0:T(8,128)S(1)} %get-tuple-element.19), channel_id=1, source_target_pairs={{0,224},{32,0},{64,32},{96,64},{128,96},{160,128},{192,160},{224,1... | collective-permute-start | bytes 1572872 | tf_op jit(solution)/shard_map/ppermute | solution.py:39
  14.0 0.0 collective-permute-start.2
  14.0 0.0 collective-permute-done.rest_1_.got_ref
  14.0 0.0 copy-done.2
  14.0 0.6 basis.1
  14.6 17.1 %all_to_all.25.basis_ref = f32[16,32,256]{2,1,0:T(8,128)S(1)} all-to-all(f32[16,32,256]{2,1,0:T(8,128)S(1)} %basis.1), channel_id=1, replica_groups=mesh['z'=8,'core'=2,'y'=4,'x'=4] {'y','x'}, dimensions={0} | all-to-all | bytes 1048576 | tf_op jit(solution)/shard_map/all_to_all | solution.py:314
  31.6 0.0 collective-permute-done.3.down_ref
  31.6 0.0 collective-permute-done.2.up_ref
  31.6 1.7 %left.1 = (f32[8,16,128]{2,1,0:T(8,128)S(1)}, f32[64,4096]{1,0:T(8,128)S(1)}) custom-call(s32[4]{0:T(128)S(1)} %pad_add_fusion.place_ref, f32[64,8192]{1,0:T(8,128)S(1)} %merge_own.1.own_ref.merged_ref, f32[64,4096]{1,0:T(8,128)S(1)} %collective-permute-done.rest_1_.got_ref, f32[64,2048]{1,0:T(8,128)S(1)} %collective-permute-done.2.up_ref, ...), custom_call_target="tpu_custom_call" | custom-call | tf_op jit(solution)/shard_map/left/pallas_call | solution.py:23
  33.3 10.9 %all_to_all.26.packed_ref = f32[8,16,128]{2,1,0:T(8,128)S(1)} all-to-all(f32[8,16,128]{2,1,0:T(8,128)S(1)} %get-tuple-element.20), channel_id=1, replica_groups=mesh['z'=8,'core'=2,'y'=4,'x'=4] {'z'}, dimensions={0} | all-to-all | bytes 131072 | tf_op jit(solution)/shard_map/all_to_all | solution.py:321
  44.3 0.6 terms.1
  44.9 12.3 %all_to_all.27.got_ref = f32[16,9,8,128]{3,2,1,0:T(8,128)S(1)} all-to-all(f32[16,9,8,128]{3,2,1,0:T(8,128)S(1)} %get-tuple-element.22), channel_id=1, replica_groups=mesh['z'=8,'core'=2,'y'=4,'x'=4] {'y','x'}, dimensions={0} | all-to-all | bytes 1179648 | tf_op jit(solution)/shard_map/all_to_all | solution.py:325
  57.3 0.7 columns.1
  58.0 3.4 %all-to-all-start.3 = ((f32[8,8,8,128]{3,2,1,0:T(8,128)}), f32[8,8,8,128]{3,2,1,0:T(8,128)S(1)}, u32[]{:S(2)}, u32[]{:S(2)}) async-start(f32[8,8,8,128]{3,2,1,0:T(8,128)} %get-tuple-element.25), calls=%async_computation.3 | async-start | bytes 524288 | tf_op jit(solution)/shard_map/all_to_all | solution.py:335
  61.4 3.5 %factors.1.factors_ref = f32[96,32]{1,0:T(8,128)S(1)} custom-call(f32[8,128]{1,0:T(8,128)S(1)} %get-tuple-element.23.gram_ref, f32[32,64]{1,0:T(8,128)S(1)} %get-tuple-element.24.left_ref), custom_call_target="tpu_custom_call" | custom-call | tf_op jit(solution)/shard_map/factors/pallas_call | solution.py:23
  65.0 4.8 %collective-permute-start.4 = (f32[96,32]{1,0:T(8,128)S(1)}, f32[96,32]{1,0:T(8,128)S(1)}, u32[]{:S(2)}, u32[]{:S(2)}) collective-permute-start(f32[96,32]{1,0:T(8,128)S(1)} %factors.1.factors_ref), channel_id=1, source_target_pairs={{0,16},{16,0},{1,17},{17,1},{2,18},{18,2},{3,19},{19,3},{4,20},{20... | collective-permute-start | bytes 36872 | tf_op jit(solution)/shard_map/ppermute | solution.py:34
  69.7 0.9 collective-permute-done.4._.factors_ref
  70.6 0.2 all-to-all-done.3.got_ref
  70.8 0.3 shard.1
  71.1 15.0 %all_to_all.28.right_ref = f32[16,32,512]{2,1,0:T(8,128)S(1)} all-to-all(f32[16,32,512]{2,1,0:T(8,128)S(1)} %get-tuple-element.26), channel_id=1, replica_groups=mesh['z'=8,'core'=2,'y'=4,'x'=4] {'y','x'}, dimensions={0} | all-to-all | bytes 2097152 | tf_op jit(solution)/shard_map/all_to_all | solution.py:337
  86.1 0.0 copy-start.1
  86.1 6.9 %collective-permute-start.5 = (f32[16,32,512]{2,1,0:T(8,128)S(1)}, f32[16,32,512]{2,1,0:T(8,128)S(1)}, u32[]{:S(2)}, u32[]{:S(2)}) collective-permute-start(f32[16,32,512]{2,1,0:T(8,128)S(1)} %all_to_all.28.right_ref), channel_id=1, source_target_pairs={{0,16},{16,0},{1,17},{17,1},{2,18},{18,2},{3,19},{19,3},{4,20},{20... | collective-permute-start | bytes 3145736 | tf_op jit(solution)/shard_map/ppermute | solution.py:34
  92.9 2.2 %residual_own.1._ = f32[1,2,64,8192]{3,2,1,0:T(8,128)} custom-call(s32[4]{0:T(128)S(1)} %pad_add_fusion.place_ref, f32[64,8192]{1,0:T(8,128)S(1)} %merge_own.1.own_ref.merged_ref, f32[96,32]{1,0:T(8,128)S(1)} %factors.1.factors_ref, f32[16,32,512]{2,1,0:T(8,128)S(1)} %all_to_all.28.right_ref), custom_call_target="tpu_custom_call" | custom-call | tf_op jit(solution)/shard_map/residual_own/pallas_call | solution.py:23
  95.1 0.1 collective-permute-done.5.right_ref
  95.2 0.0 copy-done.1
  95.2 2.8 %residual_other.1 = (f32[1,2,64,8192]{3,2,1,0:T(8,128)}, f32[2,32,512]{2,1,0:T(8,128)}) custom-call(s32[4]{0:T(128)S(1)} %pad_add_fusion.place_ref, f32[64,8192]{1,0:T(8,128)S(1)} %copy-done.1, f32[96,32]{1,0:T(8,128)S(1)} %collective-permute-done.4._.factors_ref, ...), custom_call_target="tpu_custom_call", output_to_operand_aliasing={{0}: (5, {})} | custom-call | tf_op jit(solution)/shard_map/residual_other/pallas_call | solution.py:23
Async XLA Ops:
  3.3 6.0 %copy-start = (f32[64,8192]{1,0:T(8,128)}, f32[64,8192]{1,0:T(8,128)S(1)}, u32[]{:S(2)}) copy-start(f32[64,8192]{1,0:T(8,128)S(1)} %get-tuple-element.15.merged_ref) | copy-start | bytes 6291460
  3.3 6.0 %collective-permute-start.1 = (f32[64,4096]{1,0:T(8,128)S(1)}, f32[64,4096]{1,0:T(8,128)S(1)}, u32[]{:S(2)}, u32[]{:S(2)}) collective-permute-start(f32[64,4096]{1,0:T(8,128)S(1)} %get-tuple-element.17), channel_id=1, source_target_pairs={{0,16},{16,0},{1,17},{17,1},{2,18},{18,2},{3,19},{19,3},{4,20},{20... | collective-permute-start | bytes 3145736 | tf_op jit(solution)/shard_map/ppermute | solution.py:34
  6.7 7.3 %copy-start.2 = (f32[2,32,512]{2,1,0:T(8,128)S(1)}, f32[2,32,512]{2,1,0:T(8,128)}, u32[]{:S(2)}) copy-start(f32[2,32,512]{2,1,0:T(8,128)} %basis_ref.1) | copy-start | bytes 393220
  6.7 7.3 %collective-permute-start = (f32[64,4096]{1,0:T(8,128)S(1)}, f32[64,4096]{1,0:T(8,128)S(1)}, u32[]{:S(2)}, u32[]{:S(2)}) collective-permute-start(f32[64,4096]{1,0:T(8,128)S(1)} %get-tuple-element.16), channel_id=1, source_target_pairs={{0,16},{16,0},{1,17},{17,1},{2,18},{18,2},{3,19},{19,3},{4,20},{20... | collective-permute-start | bytes 3145736 | tf_op jit(solution)/shard_map/ppermute | solution.py:34
  10.0 21.6 %collective-permute-start.3 = (f32[64,2048]{1,0:T(8,128)S(1)}, f32[64,2048]{1,0:T(8,128)S(1)}, u32[]{:S(2)}, u32[]{:S(2)}) collective-permute-start(f32[64,2048]{1,0:T(8,128)S(1)} %get-tuple-element.19), channel_id=1, source_target_pairs={{0,224},{32,0},{64,32},{96,64},{128,96},{160,128},{192,160},{224,1... | collective-permute-start | bytes 1572872 | tf_op jit(solution)/shard_map/ppermute | solution.py:39
  14.0 17.7 %collective-permute-start.2 = (f32[64,2048]{1,0:T(8,128)S(1)}, f32[64,2048]{1,0:T(8,128)S(1)}, u32[]{:S(2)}, u32[]{:S(2)}) collective-permute-start(f32[64,2048]{1,0:T(8,128)S(1)} %get-tuple-element.18.rest_0_), channel_id=1, source_target_pairs={{0,32},{32,64},{64,96},{96,128},{128,160},{160,192},{192,224},{224... | collective-permute-start | bytes 1572872 | tf_op jit(solution)/shard_map/ppermute | solution.py:39
  58.0 12.8 %all-to-all-start.3 = ((f32[8,8,8,128]{3,2,1,0:T(8,128)}), f32[8,8,8,128]{3,2,1,0:T(8,128)S(1)}, u32[]{:S(2)}, u32[]{:S(2)}) async-start(f32[8,8,8,128]{3,2,1,0:T(8,128)} %get-tuple-element.25), calls=%async_computation.3 | async-start | bytes 524288 | tf_op jit(solution)/shard_map/all_to_all | solution.py:335
  65.0 5.6 %collective-permute-start.4 = (f32[96,32]{1,0:T(8,128)S(1)}, f32[96,32]{1,0:T(8,128)S(1)}, u32[]{:S(2)}, u32[]{:S(2)}) collective-permute-start(f32[96,32]{1,0:T(8,128)S(1)} %factors.1.factors_ref), channel_id=1, source_target_pairs={{0,16},{16,0},{1,17},{17,1},{2,18},{18,2},{3,19},{19,3},{4,20},{20... | collective-permute-start | bytes 36872 | tf_op jit(solution)/shard_map/ppermute | solution.py:34
  86.1 9.1 %copy-start.1 = (f32[64,8192]{1,0:T(8,128)S(1)}, f32[64,8192]{1,0:T(8,128)}, u32[]{:S(2)}) copy-start(f32[64,8192]{1,0:T(8,128)} %copy-done) | copy-start | bytes 6291460
  86.1 9.1 %collective-permute-start.5 = (f32[16,32,512]{2,1,0:T(8,128)S(1)}, f32[16,32,512]{2,1,0:T(8,128)S(1)}, u32[]{:S(2)}, u32[]{:S(2)}) collective-permute-start(f32[16,32,512]{2,1,0:T(8,128)S(1)} %all_to_all.28.right_ref), channel_id=1, source_target_pairs={{0,16},{16,0},{1,17},{17,1},{2,18},{18,2},{3,19},{19,3},{4,20},{20... | collective-permute-start | bytes 3145736 | tf_op jit(solution)/shard_map/ppermute | solution.py:34

commit v7 on v6

--- a/solution.py
+++ b/solution.py
@@ -37,6 +37,21 @@
 def shift(value, step):
     count = lax.axis_size("z")
     return lax.ppermute(value, "z", [(i, (i + step) % count) for i in range(count)])
+
+
+def split(value):
+    high = value.astype(jnp.bfloat16)
+    return high, (value - high.astype(jnp.float32)).astype(jnp.bfloat16)
+
+
+def stack_left(value, axis):
+    high, low = split(value)
+    return jnp.concatenate([high, low, high], axis=axis)
+
+
+def stack_right(value, axis):
+    high, low = split(value)
+    return jnp.concatenate([high, high, low], axis=axis)
 
 
 def kept(place_ref):
@@ -139,10 +154,9 @@
         values_ref[:, 2 * start : 2 * start + 2 * LANES] = values
         parts.append(
             lax.dot_general(
-                basis_ref[chunk],
-                values,
+                stack_left(basis_ref[chunk], 1),
+                stack_right(values, 1),
                 (((1,), (1,)), ((), ())),
-                precision=HIGH,
                 preferred_element_type=jnp.float32,
             )
         )
@@ -165,12 +179,12 @@
     )
     rank = gram.shape[0]
     gram_tile = jnp.concatenate([gram[8 * i : 8 * i + 8] for i in range(rank // 8)], axis=1)
+    stacked = stack_left(left, 1)
     for chunk in range(sent_ref.shape[0]):
         start = 2 * chunk * LANES
         terms = jnp.dot(
-            left,
-            values_ref[:, start : start + 2 * LANES],
-            precision=HIGH,
+            stacked,
+            stack_right(values_ref[:, start : start + 2 * LANES], 0),
             preferred_element_type=jnp.float32,
         )
         for i in range(rank // 8):
@@ -229,52 +243,49 @@
     )
 
 
-def split(value):
-    high = value.astype(jnp.bfloat16)
-    return high, (value - high.astype(jnp.float32)).astype(jnp.bfloat16)
-
-
-def subtract(index, merged_ref, factors_ref, right_ref, out_ref, buffer, sems):
-    rows = merged_ref.shape[0]
-    shards, _, part = right_ref.shape
-    groups = sems.shape[0]
-    high, low = split(factors_ref[:rows, :])
-    weights = jnp.concatenate([high, low, high], axis=1)
-    copies = []
-    for group in range(groups):
-        for chunk in range(group * shards // groups, (group + 1) * shards // groups):
-            columns = slice(chunk * part, (chunk + 1) * part)
-            high, low = split(right_ref[chunk])
-            right = jnp.concatenate([high, high, low], axis=0)
-            update = jnp.dot(weights, right, preferred_element_type=jnp.float32)
-            buffer[:, columns] = merged_ref[:, columns] - update
-        width = merged_ref.shape[1] // groups
-        columns = pl.ds(group * width, width)
-        copy = pltpu.make_async_copy(
-            buffer.at[:, columns], out_ref.at[0, index, :, columns], sems.at[group]
-        )
-        copy.start()
-        copies.append(copy)
-    return copies
-
-
-def first_kernel(place_ref, merged_ref, factors_ref, right_ref, out_ref, *scratch):
-    for copy in subtract(place_ref[0], merged_ref, factors_ref, right_ref, out_ref, *scratch):
-        copy.wait()
-
-
-def second_kernel(
-    scale, place_ref, merged_ref, factors_ref, right_ref, shard_ref, _, out_ref, basis_ref, *scratch
+def subtract(merged_ref, factors_ref, right_ref, chunks, out_ref):
+    weights = stack_left(factors_ref[: merged_ref.shape[0], :], 1)
+    part = right_ref.shape[2]
+    for chunk in chunks:
+        columns = slice(chunk * part, (chunk + 1) * part)
+        update = jnp.dot(
+            weights, stack_right(right_ref[chunk], 0), preferred_element_type=jnp.float32
+        )
+        out_ref[:, columns] = merged_ref[:, columns] - update
+
+
+def own_residual_kernel(merged_ref, factors_ref, right_ref, out_ref):
+    subtract(merged_ref, factors_ref, right_ref, range(right_ref.shape[0]), out_ref)
+
+
+def other_residual_kernel(
+    scale, place_ref, merged_ref, factors_ref, right_ref, shard_ref, own_ref,
+    out_ref, basis_ref, buffer, basis_buffer, sems, basis_sem,
 ):
-    copies = subtract(place_ref[1], merged_ref, factors_ref, right_ref, out_ref, *scratch)
-    rank = right_ref.shape[1]
-    basis_ref[place_ref[0]] = shard_ref[...]
-    basis_ref[place_ref[1]] = scale * jnp.dot(
+    own_copy = pltpu.make_async_copy(own_ref, out_ref.at[0, place_ref[0]], sems.at[0])
+    own_copy.start()
+    shards, rank, _ = right_ref.shape
+    basis_buffer[place_ref[0]] = shard_ref[...]
+    basis_buffer[place_ref[1]] = scale * jnp.dot(
         factors_ref[-rank:, :],
         right_ref[place_ref[2]],
         precision=HIGH,
         preferred_element_type=jnp.float32,
     )
+    basis_copy = pltpu.make_async_copy(basis_buffer, basis_ref, basis_sem)
+    basis_copy.start()
+    copies = [own_copy, basis_copy]
+    groups = sems.shape[0] - 1
+    width = merged_ref.shape[1] // groups
+    for group in range(groups):
+        chunks = range(group * shards // groups, (group + 1) * shards // groups)
+        subtract(merged_ref, factors_ref, right_ref, chunks, buffer)
+        columns = pl.ds(group * width, width)
+        copy = pltpu.make_async_copy(
+            buffer.at[:, columns], out_ref.at[0, place_ref[1], :, columns], sems.at[1 + group]
+        )
+        copy.start()
+        copies.append(copy)
     for copy in copies:
         copy.wait()
 
@@ -336,17 +347,20 @@
     )
     whole = lax.all_to_all(copies, F, 0, 0)
     other_whole = swap(whole)
-    residual_scratch = [pltpu.VMEM((rows, width), jnp.float32), pltpu.SemaphoreType.DMA((4,))]
-    residual_shape = f32(1, pair, rows, width)
-    residual = call(
-        first_kernel, "residual_own", [SMEM, VMEM, VMEM, VMEM], residual_shape,
-        (place, own, factors, whole), out_specs=ANY, scratch_shapes=residual_scratch,
+    own_residual = call(
+        own_residual_kernel, "residual_own", [VMEM] * 3, f32(rows, width), (own, factors, whole)
     )
     return call(
-        functools.partial(second_kernel, scale), "residual_other",
-        [SMEM, VMEM, VMEM, VMEM, VMEM, ANY], (residual_shape, f32(pair, rank, part)),
-        (place, other, other_factors, other_whole, shard, residual),
-        out_specs=(ANY, VMEM), scratch_shapes=residual_scratch, input_output_aliases={5: 0},
+        functools.partial(other_residual_kernel, scale), "residual_other", [SMEM] + [VMEM] * 5,
+        (f32(1, pair, rows, width), f32(pair, rank, part)),
+        (place, other, other_factors, other_whole, shard, own_residual),
+        out_specs=(ANY, ANY),
+        scratch_shapes=[
+            pltpu.VMEM((rows, width), jnp.float32),
+            pltpu.VMEM((pair, rank, part), jnp.float32),
+            pltpu.SemaphoreType.DMA((5,)),
+            pltpu.SemaphoreType.DMA,
+        ],
     )
 
 

time: 98.4 us -> 97.8 us (level)
  Pallas kernels: 18.3 us -> 16 us
  waiting for transfers between devices: 1.16 us -> 2.84 us
    pallas_call x11, Pallas kernels: 18.3 us -> 16 us  [call(): pl.pallas_call(kernel, in_specs=in_specs, out_shape=out_shape, compiler_p...]
    ppermute x4, waiting for transfers between devices: 1 us -> 2.68 us  [swap(): return lax.ppermute(value, 'core', [(0, 1), (1, 0)])]
  transfers between devices with their start and end apart: 7 -> 7, of which waited for: 3 -> 3; matrix products, arithmetic and copies ran while one was open for 0% -> 0% of each run, Pallas kernels for 10% -> 8%
where the time goes in v7:
time: 97.8 us; the launch traced here: 97.4 us
  blocking collectives  55.3 us (57%)
  starting transfers between devices  22.4 us (23%)
  Pallas kernels  16 us (16%)
  waiting for transfers between devices  2.84 us (3%)
    all_to_all x1, blocking collectives, on_device(): basis = lax.all_to_all(copies, F, 0, 0)  17.1 us
    pallas_call x11, Pallas kernels, call(): pl.pallas_call(kernel, in_specs=in_specs, out_shape=out_shape, compiler_p...  16 us
    ppermute x4, starting transfers between devices, swap(): return lax.ppermute(value, 'core', [(0, 1), (1, 0)])  15.1 us
    all_to_all x1, blocking collectives, on_device(): whole = lax.all_to_all(copies, F, 0, 0)  15 us
    all_to_all x1, blocking collectives, on_device(): lax.all_to_all(sent, F, 0, 0)  12.3 us
    all_to_all x1, blocking collectives, on_device(): lax.all_to_all(copies, 'z', 0, 0)  10.9 us
    ppermute x2, starting transfers between devices, shift(): lax.ppermute(value, 'z', [(i, (i + step) % count) for i in range(count)])  3.93 us
    all_to_all x1, starting transfers between devices, on_device(): lax.all_to_all(sums, 'z', 0, 0)  3.41 us
  transfers between devices with their start and end apart: 7, of which 3 were waited for; matrix products, arithmetic and copies ran while one was open for 0% of the time, Pallas kernels for 8%

profile of v7, /device:TPU:1, one launch (start us, length us, event | category | flops | bytes accessed | tf_op | source)
XLA Modules:
  0.0 97.4 jit_solution(2409427829338378124)
XLA Ops:
  0.6 0.1 pad_add_fusion.place_ref
  0.7 2.6 %merge_other.1 = (f32[64,8192]{1,0:T(8,128)S(1)}, f32[64,4096]{1,0:T(8,128)S(1)}, f32[64,4096]{1,0:T(8,128)S(1)}) custom-call(s32[4]{0:T(128)S(1)} %pad_add_fusion.place_ref, bf16[1,2,64,8192]{3,2,1,0:T(8,128)(2,1)} %grad_ref.3, f32[1,2,64,8192]{3,2,1,0:T(8,128)} %error_ref.3), custom_call_target="tpu_custom_call" | custom-call | tf_op jit(solution)/shard_map/merge_other/pallas_call | solution.py:23
  3.3 0.0 copy-start
  3.3 3.3 %collective-permute-start.1 = (f32[64,4096]{1,0:T(8,128)S(1)}, f32[64,4096]{1,0:T(8,128)S(1)}, u32[]{:S(2)}, u32[]{:S(2)}) collective-permute-start(f32[64,4096]{1,0:T(8,128)S(1)} %get-tuple-element.17), channel_id=1, source_target_pairs={{0,16},{16,0},{1,17},{17,1},{2,18},{18,2},{3,19},{19,3},{4,20},{20... | collective-permute-start | bytes 3145736 | tf_op jit(solution)/shard_map/ppermute | solution.py:34
  6.7 0.1 collective-permute-start
  6.8 2.5 %merge_own.1.own_ref.merged_ref = f32[64,8192]{1,0:T(8,128)S(1)} custom-call(s32[4]{0:T(128)S(1)} %pad_add_fusion.place_ref, bf16[1,2,64,8192]{3,2,1,0:T(8,128)(2,1)} %grad_ref.3, f32[1,2,64,8192]{3,2,1,0:T(8,128)} %error_ref.3), custom_call_target="tpu_custom_call" | custom-call | tf_op jit(solution)/shard_map/merge_own/pallas_call | solution.py:23
  9.3 0.0 copy-done
  9.3 0.0 copy-start.2
  9.3 0.0 collective-permute-done.1.got_ref
  9.3 0.7 give.1
  10.0 3.9 %collective-permute-start.3 = (f32[64,2048]{1,0:T(8,128)S(1)}, f32[64,2048]{1,0:T(8,128)S(1)}, u32[]{:S(2)}, u32[]{:S(2)}) collective-permute-start(f32[64,2048]{1,0:T(8,128)S(1)} %get-tuple-element.19), channel_id=1, source_target_pairs={{0,224},{32,0},{64,32},{96,64},{128,96},{160,128},{192,160},{224,1... | collective-permute-start | bytes 1572872 | tf_op jit(solution)/shard_map/ppermute | solution.py:39
  14.0 0.0 collective-permute-start.2
  14.0 0.0 collective-permute-done.rest_1_.got_ref
  14.0 0.0 copy-done.2
  14.0 0.6 basis.1
  14.6 17.1 %all_to_all.25.basis_ref = f32[16,32,256]{2,1,0:T(8,128)S(1)} all-to-all(f32[16,32,256]{2,1,0:T(8,128)S(1)} %basis.1), channel_id=1, replica_groups=mesh['z'=8,'core'=2,'y'=4,'x'=4] {'y','x'}, dimensions={0} | all-to-all | bytes 1048576 | tf_op jit(solution)/shard_map/all_to_all | solution.py:325
  31.7 0.0 collective-permute-done.3.down_ref
  31.7 0.0 collective-permute-done.2.up_ref
  31.7 1.4 %left.1 = (f32[8,16,128]{2,1,0:T(8,128)S(1)}, f32[64,4096]{1,0:T(8,128)S(1)}) custom-call(s32[4]{0:T(128)S(1)} %pad_add_fusion.place_ref, f32[64,8192]{1,0:T(8,128)S(1)} %merge_own.1.own_ref.merged_ref, f32[64,4096]{1,0:T(8,128)S(1)} %collective-permute-done.rest_1_.got_ref, f32[64,2048]{1,0:T(8,128)S(1)} %collective-permute-done.2.up_ref, ...), custom_call_target="tpu_custom_call" | custom-call | tf_op jit(solution)/shard_map/left/pallas_call | solution.py:23
  33.1 10.9 %all_to_all.26.packed_ref = f32[8,16,128]{2,1,0:T(8,128)S(1)} all-to-all(f32[8,16,128]{2,1,0:T(8,128)S(1)} %get-tuple-element.20), channel_id=1, replica_groups=mesh['z'=8,'core'=2,'y'=4,'x'=4] {'z'}, dimensions={0} | all-to-all | bytes 131072 | tf_op jit(solution)/shard_map/all_to_all | solution.py:332
  44.0 0.5 terms.1
  44.5 12.3 %all_to_all.27.got_ref = f32[16,9,8,128]{3,2,1,0:T(8,128)S(1)} all-to-all(f32[16,9,8,128]{3,2,1,0:T(8,128)S(1)} %get-tuple-element.22), channel_id=1, replica_groups=mesh['z'=8,'core'=2,'y'=4,'x'=4] {'y','x'}, dimensions={0} | all-to-all | bytes 1179648 | tf_op jit(solution)/shard_map/all_to_all | solution.py:336
  56.8 0.7 columns.1
  57.6 3.4 %all-to-all-start.3 = ((f32[8,8,8,128]{3,2,1,0:T(8,128)}), f32[8,8,8,128]{3,2,1,0:T(8,128)S(1)}, u32[]{:S(2)}, u32[]{:S(2)}) async-start(f32[8,8,8,128]{3,2,1,0:T(8,128)} %get-tuple-element.25), calls=%async_computation.3 | async-start | bytes 524288 | tf_op jit(solution)/shard_map/all_to_all | solution.py:346
  61.0 3.5 %factors.1.factors_ref = f32[96,32]{1,0:T(8,128)S(1)} custom-call(f32[8,128]{1,0:T(8,128)S(1)} %get-tuple-element.23.gram_ref, f32[32,64]{1,0:T(8,128)S(1)} %get-tuple-element.24.left_ref), custom_call_target="tpu_custom_call" | custom-call | tf_op jit(solution)/shard_map/factors/pallas_call | solution.py:23
  64.5 4.8 %collective-permute-start.4 = (f32[96,32]{1,0:T(8,128)S(1)}, f32[96,32]{1,0:T(8,128)S(1)}, u32[]{:S(2)}, u32[]{:S(2)}) collective-permute-start(f32[96,32]{1,0:T(8,128)S(1)} %factors.1.factors_ref), channel_id=1, source_target_pairs={{0,16},{16,0},{1,17},{17,1},{2,18},{18,2},{3,19},{19,3},{4,20},{20... | collective-permute-start | bytes 36872 | tf_op jit(solution)/shard_map/ppermute | solution.py:34
  69.3 0.9 collective-permute-done.4._.factors_ref
  70.2 0.1 all-to-all-done.3.got_ref
  70.3 0.3 shard.1
  70.6 15.0 %all_to_all.28.right_ref = f32[16,32,512]{2,1,0:T(8,128)S(1)} all-to-all(f32[16,32,512]{2,1,0:T(8,128)S(1)} %get-tuple-element.26), channel_id=1, replica_groups=mesh['z'=8,'core'=2,'y'=4,'x'=4] {'y','x'}, dimensions={0} | all-to-all | bytes 2097152 | tf_op jit(solution)/shard_map/all_to_all | solution.py:348
  85.6 0.0 copy-start.1
  85.6 6.9 %collective-permute-start.5 = (f32[16,32,512]{2,1,0:T(8,128)S(1)}, f32[16,32,512]{2,1,0:T(8,128)S(1)}, u32[]{:S(2)}, u32[]{:S(2)}) collective-permute-start(f32[16,32,512]{2,1,0:T(8,128)S(1)} %all_to_all.28.right_ref), channel_id=1, source_target_pairs={{0,16},{16,0},{1,17},{17,1},{2,18},{18,2},{3,19},{19,3},{4,20},{20... | collective-permute-start | bytes 3145736 | tf_op jit(solution)/shard_map/ppermute | solution.py:34
  92.5 0.5 residual_own.1.own_ref
  93.0 1.8 %collective-permute-done.5.right_ref = f32[16,32,512]{2,1,0:T(8,128)S(1)} collective-permute-done((f32[16,32,512]{2,1,0:T(8,128)S(1)}, f32[16,32,512]{2,1,0:T(8,128)S(1)}, u32[]{:S(2)}, u32[]{:S(2)}) %collective-permute-start.5) | collective-permute-done | bytes 1048608 | tf_op jit(solution)/shard_map/ppermute | solution.py:34
  94.8 0.0 copy-done.1
  94.8 2.6 %residual_other.1 = (f32[1,2,64,8192]{3,2,1,0:T(8,128)}, f32[2,32,512]{2,1,0:T(8,128)}) custom-call(s32[4]{0:T(128)S(1)} %pad_add_fusion.place_ref, f32[64,8192]{1,0:T(8,128)S(1)} %copy-done.1, f32[96,32]{1,0:T(8,128)S(1)} %collective-permute-done.4._.factors_ref, f32[16,32,512]{2,1,0:T(8,128)S(1)} %collective-permute-done.5.right_ref, ...), custom_call_target="tpu_custom_call" | custom-call | tf_op jit(solution)/shard_map/residual_other/pallas_call | solution.py:23
Async XLA Ops:
  3.3 5.9 %copy-start = (f32[64,8192]{1,0:T(8,128)}, f32[64,8192]{1,0:T(8,128)S(1)}, u32[]{:S(2)}) copy-start(f32[64,8192]{1,0:T(8,128)S(1)} %get-tuple-element.15.merged_ref) | copy-start | bytes 6291460
  3.3 6.0 %collective-permute-start.1 = (f32[64,4096]{1,0:T(8,128)S(1)}, f32[64,4096]{1,0:T(8,128)S(1)}, u32[]{:S(2)}, u32[]{:S(2)}) collective-permute-start(f32[64,4096]{1,0:T(8,128)S(1)} %get-tuple-element.17), channel_id=1, source_target_pairs={{0,16},{16,0},{1,17},{17,1},{2,18},{18,2},{3,19},{19,3},{4,20},{20... | collective-permute-start | bytes 3145736 | tf_op jit(solution)/shard_map/ppermute | solution.py:34
  6.7 7.3 %collective-permute-start = (f32[64,4096]{1,0:T(8,128)S(1)}, f32[64,4096]{1,0:T(8,128)S(1)}, u32[]{:S(2)}, u32[]{:S(2)}) collective-permute-start(f32[64,4096]{1,0:T(8,128)S(1)} %get-tuple-element.16), channel_id=1, source_target_pairs={{0,16},{16,0},{1,17},{17,1},{2,18},{18,2},{3,19},{19,3},{4,20},{20... | collective-permute-start | bytes 3145736 | tf_op jit(solution)/shard_map/ppermute | solution.py:34
  9.3 4.7 %copy-start.2 = (f32[2,32,512]{2,1,0:T(8,128)S(1)}, f32[2,32,512]{2,1,0:T(8,128)}, u32[]{:S(2)}) copy-start(f32[2,32,512]{2,1,0:T(8,128)} %basis_ref.1) | copy-start | bytes 393220
  10.0 21.6 %collective-permute-start.3 = (f32[64,2048]{1,0:T(8,128)S(1)}, f32[64,2048]{1,0:T(8,128)S(1)}, u32[]{:S(2)}, u32[]{:S(2)}) collective-permute-start(f32[64,2048]{1,0:T(8,128)S(1)} %get-tuple-element.19), channel_id=1, source_target_pairs={{0,224},{32,0},{64,32},{96,64},{128,96},{160,128},{192,160},{224,1... | collective-permute-start | bytes 1572872 | tf_op jit(solution)/shard_map/ppermute | solution.py:39
  14.0 17.7 %collective-permute-start.2 = (f32[64,2048]{1,0:T(8,128)S(1)}, f32[64,2048]{1,0:T(8,128)S(1)}, u32[]{:S(2)}, u32[]{:S(2)}) collective-permute-start(f32[64,2048]{1,0:T(8,128)S(1)} %get-tuple-element.18.rest_0_), channel_id=1, source_target_pairs={{0,32},{32,64},{64,96},{96,128},{128,160},{160,192},{192,224},{224... | collective-permute-start | bytes 1572872 | tf_op jit(solution)/shard_map/ppermute | solution.py:39
  57.6 12.8 %all-to-all-start.3 = ((f32[8,8,8,128]{3,2,1,0:T(8,128)}), f32[8,8,8,128]{3,2,1,0:T(8,128)S(1)}, u32[]{:S(2)}, u32[]{:S(2)}) async-start(f32[8,8,8,128]{3,2,1,0:T(8,128)} %get-tuple-element.25), calls=%async_computation.3 | async-start | bytes 524288 | tf_op jit(solution)/shard_map/all_to_all | solution.py:346
  64.5 5.7 %collective-permute-start.4 = (f32[96,32]{1,0:T(8,128)S(1)}, f32[96,32]{1,0:T(8,128)S(1)}, u32[]{:S(2)}, u32[]{:S(2)}) collective-permute-start(f32[96,32]{1,0:T(8,128)S(1)} %factors.1.factors_ref), channel_id=1, source_target_pairs={{0,16},{16,0},{1,17},{17,1},{2,18},{18,2},{3,19},{19,3},{4,20},{20... | collective-permute-start | bytes 36872 | tf_op jit(solution)/shard_map/ppermute | solution.py:34
  85.6 9.2 %copy-start.1 = (f32[64,8192]{1,0:T(8,128)S(1)}, f32[64,8192]{1,0:T(8,128)}, u32[]{:S(2)}) copy-start(f32[64,8192]{1,0:T(8,128)} %copy-done) | copy-start | bytes 6291460
  85.6 9.2 %collective-permute-start.5 = (f32[16,32,512]{2,1,0:T(8,128)S(1)}, f32[16,32,512]{2,1,0:T(8,128)S(1)}, u32[]{:S(2)}, u32[]{:S(2)}) collective-permute-start(f32[16,32,512]{2,1,0:T(8,128)S(1)} %all_to_all.28.right_ref), channel_id=1, source_target_pairs={{0,16},{16,0},{1,17},{17,1},{2,18},{18,2},{3,19},{19,3},{4,20},{20... | collective-permute-start | bytes 3145736 | tf_op jit(solution)/shard_map/ppermute | solution.py:34

commit v8 on v7

--- a/solution.py
+++ b/solution.py
@@ -1,7 +1,9 @@
 import functools
+import math
 
 import jax
 import jax.numpy as jnp
+import numpy as np
 from jax import lax
 from jax.experimental import pallas as pl
 from jax.experimental.pallas import tpu as pltpu
@@ -32,6 +34,16 @@
 
 def swap(value):
     return lax.ppermute(value, "core", [(0, 1), (1, 0)])
+
+
+def turned(axes):
+    sizes = [lax.axis_size(axis) for axis in axes]
+    order = np.arange(math.prod(sizes)).reshape(sizes)
+    return tuple(int(i) for i in np.roll(order, [size // 2 for size in sizes], range(len(sizes))).ravel())
+
+
+def exchange(pieces, axes):
+    return lax.all_to_all(pieces, axes, 0, 0, axis_index_groups=[list(turned(axes))])
 
 
 def shift(value, step):
@@ -140,7 +152,7 @@
         copies_ref[copy] = chunk
 
 
-def left_kernel(place_ref, own_ref, got_ref, up_ref, down_ref, basis_ref, copies_ref, values_ref):
+def left_kernel(turn, place_ref, own_ref, got_ref, up_ref, down_ref, basis_ref, copies_ref, values_ref):
     parts = []
     for chunk in range(basis_ref.shape[0]):
         start = chunk * LANES
@@ -154,7 +166,7 @@
         values_ref[:, 2 * start : 2 * start + 2 * LANES] = values
         parts.append(
             lax.dot_general(
-                stack_left(basis_ref[chunk], 1),
+                stack_left(basis_ref[turn[chunk]], 1),
                 stack_right(values, 1),
                 (((1,), (1,)), ((), ())),
                 preferred_element_type=jnp.float32,
@@ -169,7 +181,7 @@
         copies_ref[copy] = packed
 
 
-def terms_kernel(packed_ref, values_ref, sent_ref, left_ref):
+def terms_kernel(turn, packed_ref, values_ref, sent_ref, left_ref):
     _, rows = left_ref.shape
     packed = jnp.sum(packed_ref[...], axis=0)
     left = jnp.concatenate([packed[:, :rows], packed[:, rows:]], axis=0)
@@ -189,8 +201,8 @@
         )
         for i in range(rank // 8):
             for j in range(2):
-                sent_ref[chunk, 2 * i + j] = terms[8 * i : 8 * i + 8, LANES * j : LANES * j + LANES]
-        sent_ref[chunk, rank // 4] = gram_tile
+                sent_ref[turn[chunk], 2 * i + j] = terms[8 * i : 8 * i + 8, LANES * j : LANES * j + LANES]
+        sent_ref[turn[chunk], rank // 4] = gram_tile
 
 
 def columns_kernel(got_ref, sums_ref, gram_ref):
@@ -225,7 +237,7 @@
     )
 
 
-def shard_kernel(scale, got_ref, factors_ref, _, copies_ref, shard_ref):
+def shard_kernel(scale, got_ref, factors_ref, copies_ref, shard_ref):
     rank = copies_ref.shape[1]
     got = got_ref[...]
     count = got.shape[0]
@@ -243,28 +255,47 @@
     )
 
 
-def subtract(merged_ref, factors_ref, right_ref, chunks, out_ref):
+def subtract(turn, merged_ref, factors_ref, right_ref, chunks, out_ref):
     weights = stack_left(factors_ref[: merged_ref.shape[0], :], 1)
     part = right_ref.shape[2]
     for chunk in chunks:
         columns = slice(chunk * part, (chunk + 1) * part)
         update = jnp.dot(
-            weights, stack_right(right_ref[chunk], 0), preferred_element_type=jnp.float32
+            weights, stack_right(right_ref[turn[chunk]], 0), preferred_element_type=jnp.float32
         )
         out_ref[:, columns] = merged_ref[:, columns] - update
 
 
-def own_residual_kernel(merged_ref, factors_ref, right_ref, out_ref):
-    subtract(merged_ref, factors_ref, right_ref, range(right_ref.shape[0]), out_ref)
+def subtract_out(turn, index, merged_ref, factors_ref, right_ref, out_ref, buffer, sems):
+    shards, groups = right_ref.shape[0], sems.shape[0]
+    width = merged_ref.shape[1] // groups
+    copies = []
+    for group in range(groups):
+        chunks = range(group * shards // groups, (group + 1) * shards // groups)
+        subtract(turn, merged_ref, factors_ref, right_ref, chunks, buffer)
+        columns = pl.ds(group * width, width)
+        copy = pltpu.make_async_copy(
+            buffer.at[:, columns], out_ref.at[0, index, :, columns], sems.at[group]
+        )
+        copy.start()
+        copies.append(copy)
+    return copies
+
+
+def own_residual_kernel(turn, place_ref, merged_ref, factors_ref, right_ref, out_ref, *scratch):
+    copies = subtract_out(turn, place_ref[0], merged_ref, factors_ref, right_ref, out_ref, *scratch)
+    for copy in copies:
+        copy.wait()
 
 
 def other_residual_kernel(
-    scale, place_ref, merged_ref, factors_ref, right_ref, shard_ref, own_ref,
-    out_ref, basis_ref, buffer, basis_buffer, sems, basis_sem,
+    turn, scale, place_ref, merged_ref, factors_ref, right_ref, shard_ref, _,
+    out_ref, basis_ref, buffer, sems, basis_buffer, basis_sem,
 ):
-    own_copy = pltpu.make_async_copy(own_ref, out_ref.at[0, place_ref[0]], sems.at[0])
-    own_copy.start()
-    shards, rank, _ = right_ref.shape
+    copies = subtract_out(
+        turn, place_ref[1], merged_ref, factors_ref, right_ref, out_ref, buffer, sems
+    )
+    rank = right_ref.shape[1]
     basis_buffer[place_ref[0]] = shard_ref[...]
     basis_buffer[place_ref[1]] = scale * jnp.dot(
         factors_ref[-rank:, :],
@@ -274,19 +305,7 @@
     )
     basis_copy = pltpu.make_async_copy(basis_buffer, basis_ref, basis_sem)
     basis_copy.start()
-    copies = [own_copy, basis_copy]
-    groups = sems.shape[0] - 1
-    width = merged_ref.shape[1] // groups
-    for group in range(groups):
-        chunks = range(group * shards // groups, (group + 1) * shards // groups)
-        subtract(merged_ref, factors_ref, right_ref, chunks, buffer)
-        columns = pl.ds(group * width, width)
-        copy = pltpu.make_async_copy(
-            buffer.at[:, columns], out_ref.at[0, place_ref[1], :, columns], sems.at[1 + group]
-        )
-        copy.start()
-        copies.append(copy)
-    for copy in copies:
+    for copy in copies + [basis_copy]:
         copy.wait()
 
 
@@ -297,7 +316,9 @@
     pair, rows, width = grad_pair.shape[1:]
     rank, part = basis_pair.shape[1:]
     shards = width // part
-    place = jnp.stack([core, 1 - core, lax.axis_index(F), lax.axis_index("z") % 2])
+    turn = turned(F)
+    position = sum(jnp.where(lax.axis_index(F) == i, turn[i], 0) for i in range(shards))
+    place = jnp.stack([core, 1 - core, position, lax.axis_index("z") % 2])
 
     inputs = [
         pltpu.with_memory_space_constraint(array, pltpu.HBM) for array in (grad_pair, error_pair)
@@ -322,45 +343,45 @@
         (place, basis_pair, up, keep),
     )
     up, down = shift(up, 1), shift(down, -1)
-    basis = lax.all_to_all(copies, F, 0, 0)
+    basis = exchange(copies, F)
     copies, values = call(
-        left_kernel, "left", [SMEM] + [VMEM] * 5, (f32(zs, rank // 2, 2 * rows), by_two),
+        functools.partial(left_kernel, turn), "left", [SMEM] + [VMEM] * 5, (f32(zs, rank // 2, 2 * rows), by_two),
         (place, own, keep, up, down, basis),
     )
     sent, left = call(
-        terms_kernel, "terms", [VMEM, VMEM], (f32(shards, rank // 4 + 1, 8, LANES), f32(rank, rows)),
-        (lax.all_to_all(copies, "z", 0, 0), values),
+        functools.partial(terms_kernel, turn), "terms", [VMEM, VMEM], (f32(shards, rank // 4 + 1, 8, LANES), f32(rank, rows)),
+        (exchange(copies, ("z",)), values),
     )
     sums, gram = call(
         columns_kernel, "columns", [VMEM], (f32(zs, rank // 4, 8, LANES), f32(8, LANES)),
-        (lax.all_to_all(sent, F, 0, 0),),
+        (exchange(sent, F),),
     )
     factors = call(
         functools.partial(factors_kernel, scale), "factors", [VMEM, VMEM],
         f32(rows + rank, rank), (gram, left),
     )
-    other_factors = swap(factors)
     copies, shard = call(
-        functools.partial(shard_kernel, scale), "shard", [VMEM, VMEM, ANY],
+        functools.partial(shard_kernel, scale), "shard", [VMEM, VMEM],
         (f32(shards, rank, part), f32(rank, part)),
-        (lax.all_to_all(sums, "z", 0, 0), factors, other_factors),
-    )
-    whole = lax.all_to_all(copies, F, 0, 0)
-    other_whole = swap(whole)
-    own_residual = call(
-        own_residual_kernel, "residual_own", [VMEM] * 3, f32(rows, width), (own, factors, whole)
+        (exchange(sums, ("z",)), factors),
+    )
+    whole = exchange(copies, F)
+    whole, factors = lax.optimization_barrier((whole, factors))
+    other_whole, other_factors = swap(whole), swap(factors)
+    residual_scratch = [pltpu.VMEM((rows, width), jnp.float32), pltpu.SemaphoreType.DMA((4,))]
+    residual_shape = f32(1, pair, rows, width)
+    residual = call(
+        functools.partial(own_residual_kernel, turn), "residual_own", [SMEM, VMEM, VMEM, VMEM], residual_shape,
+        (place, own, factors, whole), out_specs=ANY, scratch_shapes=residual_scratch,
     )
     return call(
-        functools.partial(other_residual_kernel, scale), "residual_other", [SMEM] + [VMEM] * 5,
-        (f32(1, pair, rows, width), f32(pair, rank, part)),
-        (place, other, other_factors, other_whole, shard, own_residual),
+        functools.partial(other_residual_kernel, turn, scale), "residual_other",
+        [SMEM, VMEM, VMEM, VMEM, VMEM, ANY], (residual_shape, f32(pair, rank, part)),
+        (place, other, other_factors, other_whole, shard, residual),
         out_specs=(ANY, ANY),
-        scratch_shapes=[
-            pltpu.VMEM((rows, width), jnp.float32),
-            pltpu.VMEM((pair, rank, part), jnp.float32),
-            pltpu.SemaphoreType.DMA((5,)),
-            pltpu.SemaphoreType.DMA,
-        ],
+        scratch_shapes=residual_scratch
+        + [pltpu.VMEM((pair, rank, part), jnp.float32), pltpu.SemaphoreType.DMA],
+        input_output_aliases={5: 0},
     )
 
 

time: 97.8 us -> 91.7 us (0.938)
  starting transfers between devices: 22.4 us -> 17.9 us
  waiting for transfers between devices: 2.84 us -> 0.9 us
  Pallas kernels: 16 us -> 17.2 us
    ppermute x4, starting transfers between devices: 15.1 us -> 7.27 us  [swap(): return lax.ppermute(value, 'core', [(0, 1), (1, 0)])]
    all_to_all x1, starting transfers between devices: 3.41 us -> 6.65 us  [exchange(): lax.all_to_all(pieces, axes, 0, 0, axis_index_groups=[list(turned(axes))])]
    ppermute x4, waiting for transfers between devices: 2.68 us -> 0.19 us  [swap(): return lax.ppermute(value, 'core', [(0, 1), (1, 0)])]
    pallas_call x11, Pallas kernels: 16 us -> 17.2 us  [call(): pl.pallas_call(kernel, in_specs=in_specs, out_shape=out_shape, compiler_p...]
  transfers between devices with their start and end apart: 7 -> 7, of which waited for: 3 -> 2; matrix products, arithmetic and copies ran while one was open for 0% -> 0% of each run, Pallas kernels for 8% -> 10%
where the time goes in v8:
time: 91.7 us; the launch traced here: 91.4 us
  blocking collectives  54.5 us (59%)
  starting transfers between devices  17.9 us (20%)
  Pallas kernels  17.2 us (19%)
    all_to_all x4, blocking collectives, exchange(): lax.all_to_all(pieces, axes, 0, 0, axis_index_groups=[list(turned(axes))])  54.5 us
    pallas_call x11, Pallas kernels, call(): pl.pallas_call(kernel, in_specs=in_specs, out_shape=out_shape, compiler_p...  17.2 us
    ppermute x4, starting transfers between devices, swap(): return lax.ppermute(value, 'core', [(0, 1), (1, 0)])  7.27 us
    all_to_all x1, starting transfers between devices, exchange(): lax.all_to_all(pieces, axes, 0, 0, axis_index_groups=[list(turned(axes))])  6.65 us
    ppermute x2, starting transfers between devices, shift(): lax.ppermute(value, 'z', [(i, (i + step) % count) for i in range(count)])  3.93 us
  transfers between devices with their start and end apart: 7, of which 2 were waited for; matrix products, arithmetic and copies ran while one was open for 0% of the time, Pallas kernels for 10%

profile of v8, /device:TPU:1, one launch (start us, length us, event | category | flops | bytes accessed | tf_op | source)
XLA Modules:
  0.0 91.4 jit_solution(12650742103430506718)
XLA Ops:
  0.7 0.1 pad_add_fusion.place_ref
  0.8 2.6 %merge_other.1 = (f32[64,8192]{1,0:T(8,128)S(1)}, f32[64,4096]{1,0:T(8,128)S(1)}, f32[64,4096]{1,0:T(8,128)S(1)}) custom-call(s32[4]{0:T(128)S(1)} %pad_add_fusion.place_ref, bf16[1,2,64,8192]{3,2,1,0:T(8,128)(2,1)} %grad_ref.3, f32[1,2,64,8192]{3,2,1,0:T(8,128)} %error_ref.3), custom_call_target="tpu_custom_call" | custom-call | tf_op jit(solution)/shard_map/merge_other/pallas_call | solution.py:25
  3.4 0.0 copy-start
  3.4 3.3 %collective-permute-start.1 = (f32[64,4096]{1,0:T(8,128)S(1)}, f32[64,4096]{1,0:T(8,128)S(1)}, u32[]{:S(2)}, u32[]{:S(2)}) collective-permute-start(f32[64,4096]{1,0:T(8,128)S(1)} %get-tuple-element.19), channel_id=1, source_target_pairs={{0,16},{16,0},{1,17},{17,1},{2,18},{18,2},{3,19},{19,3},{4,20},{20... | collective-permute-start | bytes 3145736 | tf_op jit(solution)/shard_map/ppermute | solution.py:36
  6.7 0.0 copy-start.2
  6.7 0.1 collective-permute-start
  6.8 2.5 %merge_own.1.own_ref.merged_ref = f32[64,8192]{1,0:T(8,128)S(1)} custom-call(s32[4]{0:T(128)S(1)} %pad_add_fusion.place_ref, bf16[1,2,64,8192]{3,2,1,0:T(8,128)(2,1)} %grad_ref.3, f32[1,2,64,8192]{3,2,1,0:T(8,128)} %error_ref.3), custom_call_target="tpu_custom_call" | custom-call | tf_op jit(solution)/shard_map/merge_own/pallas_call | solution.py:25
  9.3 0.0 copy-done
  9.3 0.0 collective-permute-done.1.got_ref
  9.4 0.7 give.1
  10.1 3.9 %collective-permute-start.3 = (f32[64,2048]{1,0:T(8,128)S(1)}, f32[64,2048]{1,0:T(8,128)S(1)}, u32[]{:S(2)}, u32[]{:S(2)}) collective-permute-start(f32[64,2048]{1,0:T(8,128)S(1)} %get-tuple-element.21), channel_id=1, source_target_pairs={{0,224},{32,0},{64,32},{96,64},{128,96},{160,128},{192,160},{224,1... | collective-permute-start | bytes 1572872 | tf_op jit(solution)/shard_map/ppermute | solution.py:51
  14.0 0.0 collective-permute-start.2
  14.0 0.0 collective-permute-done.rest_1_.got_ref
  14.0 0.0 copy-done.2
  14.0 0.6 basis.1
  14.6 15.3 %all_to_all.25.basis_ref = f32[16,32,256]{2,1,0:T(8,128)S(1)} all-to-all(f32[16,32,256]{2,1,0:T(8,128)S(1)} %basis.1), channel_id=1, replica_groups={{10,11,8,9,14,15,12,13,2,3,0,1,6,7,4,5},{26,27,24,25,30,31,28,29,18,19,..., dimensions={0} | all-to-all | bytes 1048576 | tf_op jit(solution)/shard_map/all_to_all | solution.py:46
  30.0 0.0 collective-permute-done.3.down_ref
  30.0 0.0 collective-permute-done.2.up_ref
  30.0 1.4 %left.1 = (f32[8,16,128]{2,1,0:T(8,128)S(1)}, f32[64,4096]{1,0:T(8,128)S(1)}) custom-call(s32[4]{0:T(128)S(1)} %pad_add_fusion.place_ref, f32[64,8192]{1,0:T(8,128)S(1)} %merge_own.1.own_ref.merged_ref, f32[64,4096]{1,0:T(8,128)S(1)} %collective-permute-done.rest_1_.got_ref, f32[64,2048]{1,0:T(8,128)S(1)} %collective-permute-done.2.up_ref, ...), custom_call_target="tpu_custom_call" | custom-call | tf_op jit(solution)/shard_map/left/pallas_call | solution.py:25
  31.4 9.1 %all_to_all.26.packed_ref = f32[8,16,128]{2,1,0:T(8,128)S(1)} all-to-all(f32[8,16,128]{2,1,0:T(8,128)S(1)} %get-tuple-element.22), channel_id=1, replica_groups={{128,160,192,224,0,32,64,96},{129,161,193,225,1,33,65,97},{130,162,194,..., dimensions={0} | all-to-all | bytes 131072 | tf_op jit(solution)/shard_map/all_to_all | solution.py:46
  40.5 0.5 terms.1
  41.0 13.6 %all_to_all.27.got_ref = f32[16,9,8,128]{3,2,1,0:T(8,128)S(1)} all-to-all(f32[16,9,8,128]{3,2,1,0:T(8,128)S(1)} %get-tuple-element.24), channel_id=1, replica_groups={{10,11,8,9,14,15,12,13,2,3,0,1,6,7,4,5},{26,27,24,25,30,31,28,29,18,19,..., dimensions={0} | all-to-all | bytes 1179648 | tf_op jit(solution)/shard_map/all_to_all | solution.py:46
  54.6 0.7 columns.1
  55.4 6.6 %all-to-all-start.3 = ((f32[8,8,8,128]{3,2,1,0:T(8,128)}), f32[8,8,8,128]{3,2,1,0:T(8,128)S(1)}, u32[]{:S(2)}, u32[]{:S(2)}) async-start(f32[8,8,8,128]{3,2,1,0:T(8,128)} %get-tuple-element.25), calls=%async_computation.3 | async-start | bytes 524288 | tf_op jit(solution)/shard_map/all_to_all | solution.py:46
  62.0 3.5 %factors.1.factors_ref = f32[96,32]{1,0:T(8,128)S(1)} custom-call(f32[8,128]{1,0:T(8,128)S(1)} %get-tuple-element.26.gram_ref, f32[32,64]{1,0:T(8,128)S(1)} %get-tuple-element.27.left_ref), custom_call_target="tpu_custom_call" | custom-call | tf_op jit(solution)/shard_map/factors/pallas_call | solution.py:25
  65.6 0.7 all-to-all-done.3.got_ref
  66.3 0.3 shard.1
  66.5 16.4 %all_to_all.28.right_ref = f32[16,32,512]{2,1,0:T(8,128)S(1)} all-to-all(f32[16,32,512]{2,1,0:T(8,128)S(1)} %get-tuple-element.28), channel_id=1, replica_groups={{10,11,8,9,14,15,12,13,2,3,0,1,6,7,4,5},{26,27,24,25,30,31,28,29,18,19,..., dimensions={0} | all-to-all | bytes 2097152 | tf_op jit(solution)/shard_map/all_to_all | solution.py:46
  82.9 0.0 copy-start.1
  83.0 3.8 %collective-permute-start.5 = (f32[16,32,512]{2,1,0:T(8,128)S(1)}, f32[16,32,512]{2,1,0:T(8,128)S(1)}, u32[]{:S(2)}, u32[]{:S(2)}) collective-permute-start(f32[16,32,512]{2,1,0:T(8,128)S(1)} %all_to_all.28.right_ref), channel_id=1, source_target_pairs={{0,16},{16,0},{1,17},{17,1},{2,18},{18,2},{3,19},{19,3},{4,20},{20... | collective-permute-start | bytes 3145736 | tf_op jit(solution)/shard_map/ppermute | solution.py:36
  86.8 0.0 collective-permute-start.4
  86.8 2.2 %residual_own.1._ = f32[1,2,64,8192]{3,2,1,0:T(8,128)} custom-call(s32[4]{0:T(128)S(1)} %pad_add_fusion.place_ref, f32[64,8192]{1,0:T(8,128)S(1)} %merge_own.1.own_ref.merged_ref, f32[96,32]{1,0:T(8,128)S(1)} %factors.1.factors_ref, f32[16,32,512]{2,1,0:T(8,128)S(1)} %all_to_all.28.right_ref), custom_call_target="tpu_custom_call" | custom-call | tf_op jit(solution)/shard_map/residual_own/pallas_call | solution.py:25
  89.0 0.2 collective-permute-done.4.factors_ref
  89.1 0.0 collective-permute-done.5.right_ref
  89.1 0.0 copy-done.1
  89.1 2.2 %residual_other.1 = (f32[1,2,64,8192]{3,2,1,0:T(8,128)}, f32[2,32,512]{2,1,0:T(8,128)}) custom-call(s32[4]{0:T(128)S(1)} %pad_add_fusion.place_ref, f32[64,8192]{1,0:T(8,128)S(1)} %copy-done.1, f32[96,32]{1,0:T(8,128)S(1)} %collective-permute-done.4.factors_ref, ...), custom_call_target="tpu_custom_call", output_to_operand_aliasing={{0}: (5, {})} | custom-call | tf_op jit(solution)/shard_map/residual_other/pallas_call | solution.py:25
Async XLA Ops:
  3.4 6.0 %copy-start = (f32[64,8192]{1,0:T(8,128)}, f32[64,8192]{1,0:T(8,128)S(1)}, u32[]{:S(2)}) copy-start(f32[64,8192]{1,0:T(8,128)S(1)} %get-tuple-element.17.merged_ref) | copy-start | bytes 6291460
  3.4 6.0 %collective-permute-start.1 = (f32[64,4096]{1,0:T(8,128)S(1)}, f32[64,4096]{1,0:T(8,128)S(1)}, u32[]{:S(2)}, u32[]{:S(2)}) collective-permute-start(f32[64,4096]{1,0:T(8,128)S(1)} %get-tuple-element.19), channel_id=1, source_target_pairs={{0,16},{16,0},{1,17},{17,1},{2,18},{18,2},{3,19},{19,3},{4,20},{20... | collective-permute-start | bytes 3145736 | tf_op jit(solution)/shard_map/ppermute | solution.py:36
  6.7 7.3 %copy-start.2 = (f32[2,32,512]{2,1,0:T(8,128)S(1)}, f32[2,32,512]{2,1,0:T(8,128)}, u32[]{:S(2)}) copy-start(f32[2,32,512]{2,1,0:T(8,128)} %basis_ref.1) | copy-start | bytes 393220
  6.7 7.3 %collective-permute-start = (f32[64,4096]{1,0:T(8,128)S(1)}, f32[64,4096]{1,0:T(8,128)S(1)}, u32[]{:S(2)}, u32[]{:S(2)}) collective-permute-start(f32[64,4096]{1,0:T(8,128)S(1)} %get-tuple-element.18), channel_id=1, source_target_pairs={{0,16},{16,0},{1,17},{17,1},{2,18},{18,2},{3,19},{19,3},{4,20},{20... | collective-permute-start | bytes 3145736 | tf_op jit(solution)/shard_map/ppermute | solution.py:36
  10.1 19.9 %collective-permute-start.3 = (f32[64,2048]{1,0:T(8,128)S(1)}, f32[64,2048]{1,0:T(8,128)S(1)}, u32[]{:S(2)}, u32[]{:S(2)}) collective-permute-start(f32[64,2048]{1,0:T(8,128)S(1)} %get-tuple-element.21), channel_id=1, source_target_pairs={{0,224},{32,0},{64,32},{96,64},{128,96},{160,128},{192,160},{224,1... | collective-permute-start | bytes 1572872 | tf_op jit(solution)/shard_map/ppermute | solution.py:51
  14.0 16.0 %collective-permute-start.2 = (f32[64,2048]{1,0:T(8,128)S(1)}, f32[64,2048]{1,0:T(8,128)S(1)}, u32[]{:S(2)}, u32[]{:S(2)}) collective-permute-start(f32[64,2048]{1,0:T(8,128)S(1)} %get-tuple-element.20.rest_0_), channel_id=1, source_target_pairs={{0,32},{32,64},{64,96},{96,128},{128,160},{160,192},{192,224},{224... | collective-permute-start | bytes 1572872 | tf_op jit(solution)/shard_map/ppermute | solution.py:51
  55.4 10.9 %all-to-all-start.3 = ((f32[8,8,8,128]{3,2,1,0:T(8,128)}), f32[8,8,8,128]{3,2,1,0:T(8,128)S(1)}, u32[]{:S(2)}, u32[]{:S(2)}) async-start(f32[8,8,8,128]{3,2,1,0:T(8,128)} %get-tuple-element.25), calls=%async_computation.3 | async-start | bytes 524288 | tf_op jit(solution)/shard_map/all_to_all | solution.py:46
  82.9 6.2 %copy-start.1 = (f32[64,8192]{1,0:T(8,128)S(1)}, f32[64,8192]{1,0:T(8,128)}, u32[]{:S(2)}) copy-start(f32[64,8192]{1,0:T(8,128)} %copy-done) | copy-start | bytes 6291460
  83.0 6.2 %collective-permute-start.5 = (f32[16,32,512]{2,1,0:T(8,128)S(1)}, f32[16,32,512]{2,1,0:T(8,128)S(1)}, u32[]{:S(2)}, u32[]{:S(2)}) collective-permute-start(f32[16,32,512]{2,1,0:T(8,128)S(1)} %all_to_all.28.right_ref), channel_id=1, source_target_pairs={{0,16},{16,0},{1,17},{17,1},{2,18},{18,2},{3,19},{19,3},{4,20},{20... | collective-permute-start | bytes 3145736 | tf_op jit(solution)/shard_map/ppermute | solution.py:36
  86.8 2.4 %collective-permute-start.4 = (f32[96,32]{1,0:T(8,128)S(1)}, f32[96,32]{1,0:T(8,128)S(1)}, u32[]{:S(2)}, u32[]{:S(2)}) collective-permute-start(f32[96,32]{1,0:T(8,128)S(1)} %factors.1.factors_ref), channel_id=1, source_target_pairs={{0,16},{16,0},{1,17},{17,1},{2,18},{18,2},{3,19},{19,3},{4,20},{20... | collective-permute-start | bytes 36872 | tf_op jit(solution)/shard_map/ppermute | solution.py:36

commit v9 on v8

--- a/solution.py
+++ b/solution.py
@@ -36,14 +36,18 @@
     return lax.ppermute(value, "core", [(0, 1), (1, 0)])
 
 
-def turned(axes):
+def order_of(axes):
     sizes = [lax.axis_size(axis) for axis in axes]
     order = np.arange(math.prod(sizes)).reshape(sizes)
-    return tuple(int(i) for i in np.roll(order, [size // 2 for size in sizes], range(len(sizes))).ravel())
+    if len(sizes) == 1:
+        order = np.roll(order, -2 * (3 * sizes[0] // 8))
+    else:
+        order = np.roll(order, [size // 2 for size in sizes], range(len(sizes))).T
+    return [int(i) for i in order.ravel()]
 
 
 def exchange(pieces, axes):
-    return lax.all_to_all(pieces, axes, 0, 0, axis_index_groups=[list(turned(axes))])
+    return lax.all_to_all(pieces, axes, 0, 0, axis_index_groups=[order_of(axes)])
 
 
 def shift(value, step):
@@ -316,7 +320,7 @@
     pair, rows, width = grad_pair.shape[1:]
     rank, part = basis_pair.shape[1:]
     shards = width // part
-    turn = turned(F)
+    turn = [order_of(F).index(i) for i in range(shards)]
     position = sum(jnp.where(lax.axis_index(F) == i, turn[i], 0) for i in range(shards))
     place = jnp.stack([core, 1 - core, position, lax.axis_index("z") % 2])
 

time: 91.7 us -> 90.1 us (0.983)
  blocking collectives: 54.5 us -> 49.2 us
  starting transfers between devices: 17.9 us -> 21.1 us
    all_to_all x4, blocking collectives: 54.5 us -> 49.2 us  [exchange(): lax.all_to_all(pieces, axes, 0, 0, axis_index_groups=[order_of(axes)])]
    ppermute x4, starting transfers between devices: 7.27 us -> 10.4 us  [swap(): return lax.ppermute(value, 'core', [(0, 1), (1, 0)])]
  transfers between devices with their start and end apart: 7 -> 7, of which waited for: 2 -> 2; matrix products, arithmetic and copies ran while one was open for 0% -> 0% of each run, Pallas kernels for 10% -> 11%
where the time goes in v9:
time: 90.1 us; the launch traced here: 89.7 us
  blocking collectives  49.2 us (55%)
  starting transfers between devices  21.1 us (23%)
  Pallas kernels  17.2 us (19%)
  waiting for transfers between devices  1.32 us (1%)
    all_to_all x4, blocking collectives, exchange(): lax.all_to_all(pieces, axes, 0, 0, axis_index_groups=[order_of(axes)])  49.2 us
    pallas_call x11, Pallas kernels, call(): pl.pallas_call(kernel, in_specs=in_specs, out_shape=out_shape, compiler_p...  17.2 us
    ppermute x4, starting transfers between devices, swap(): return lax.ppermute(value, 'core', [(0, 1), (1, 0)])  10.4 us
    all_to_all x1, starting transfers between devices, exchange(): lax.all_to_all(pieces, axes, 0, 0, axis_index_groups=[order_of(axes)])  6.7 us
    ppermute x2, starting transfers between devices, shift(): lax.ppermute(value, 'z', [(i, (i + step) % count) for i in range(count)])  3.93 us
  transfers between devices with their start and end apart: 7, of which 2 were waited for; matrix products, arithmetic and copies ran while one was open for 0% of the time, Pallas kernels for 11%

profile of v9, /device:TPU:1, one launch (start us, length us, event | category | flops | bytes accessed | tf_op | source)
XLA Modules:
  0.0 89.7 jit_solution(4702641549965789635)
XLA Ops:
  0.7 0.1 pad_add_fusion.place_ref
  0.8 2.6 %merge_other.1 = (f32[64,8192]{1,0:T(8,128)S(1)}, f32[64,4096]{1,0:T(8,128)S(1)}, f32[64,4096]{1,0:T(8,128)S(1)}) custom-call(s32[4]{0:T(128)S(1)} %pad_add_fusion.place_ref, bf16[1,2,64,8192]{3,2,1,0:T(8,128)(2,1)} %grad_ref.3, f32[1,2,64,8192]{3,2,1,0:T(8,128)} %error_ref.3), custom_call_target="tpu_custom_call" | custom-call | tf_op jit(solution)/shard_map/merge_other/pallas_call | solution.py:25
  3.4 0.0 copy-start
  3.4 3.3 %collective-permute-start.1 = (f32[64,4096]{1,0:T(8,128)S(1)}, f32[64,4096]{1,0:T(8,128)S(1)}, u32[]{:S(2)}, u32[]{:S(2)}) collective-permute-start(f32[64,4096]{1,0:T(8,128)S(1)} %get-tuple-element.19), channel_id=1, source_target_pairs={{0,16},{16,0},{1,17},{17,1},{2,18},{18,2},{3,19},{19,3},{4,20},{20... | collective-permute-start | bytes 3145736 | tf_op jit(solution)/shard_map/ppermute | solution.py:36
  6.7 0.0 copy-start.2
  6.7 0.1 collective-permute-start
  6.8 2.5 %merge_own.1.own_ref.merged_ref = f32[64,8192]{1,0:T(8,128)S(1)} custom-call(s32[4]{0:T(128)S(1)} %pad_add_fusion.place_ref, bf16[1,2,64,8192]{3,2,1,0:T(8,128)(2,1)} %grad_ref.3, f32[1,2,64,8192]{3,2,1,0:T(8,128)} %error_ref.3), custom_call_target="tpu_custom_call" | custom-call | tf_op jit(solution)/shard_map/merge_own/pallas_call | solution.py:25
  9.3 0.0 copy-done
  9.3 0.0 collective-permute-done.1.got_ref
  9.4 0.7 give.1
  10.1 3.9 %collective-permute-start.3 = (f32[64,2048]{1,0:T(8,128)S(1)}, f32[64,2048]{1,0:T(8,128)S(1)}, u32[]{:S(2)}, u32[]{:S(2)}) collective-permute-start(f32[64,2048]{1,0:T(8,128)S(1)} %get-tuple-element.21), channel_id=1, source_target_pairs={{0,224},{32,0},{64,32},{96,64},{128,96},{160,128},{192,160},{224,1... | collective-permute-start | bytes 1572872 | tf_op jit(solution)/shard_map/ppermute | solution.py:55
  14.0 0.0 collective-permute-start.2
  14.0 0.0 collective-permute-done.rest_1_.got_ref
  14.0 0.0 copy-done.2
  14.0 0.6 basis.1
  14.6 14.0 %all_to_all.25.basis_ref = f32[16,32,256]{2,1,0:T(8,128)S(1)} all-to-all(f32[16,32,256]{2,1,0:T(8,128)S(1)} %basis.1), channel_id=1, replica_groups={{10,14,2,6,11,15,3,7,8,12,0,4,9,13,1,5},{26,30,18,22,27,31,19,23,24,28,..., dimensions={0} | all-to-all | bytes 1048576 | tf_op jit(solution)/shard_map/all_to_all | solution.py:50
  28.6 0.0 collective-permute-done.3.down_ref
  28.6 0.0 collective-permute-done.2.up_ref
  28.6 1.4 %left.1 = (f32[8,16,128]{2,1,0:T(8,128)S(1)}, f32[64,4096]{1,0:T(8,128)S(1)}) custom-call(s32[4]{0:T(128)S(1)} %pad_add_fusion.place_ref, f32[64,8192]{1,0:T(8,128)S(1)} %merge_own.1.own_ref.merged_ref, f32[64,4096]{1,0:T(8,128)S(1)} %collective-permute-done.rest_1_.got_ref, f32[64,2048]{1,0:T(8,128)S(1)} %collective-permute-done.2.up_ref, ...), custom_call_target="tpu_custom_call" | custom-call | tf_op jit(solution)/shard_map/left/pallas_call | solution.py:25
  30.0 9.3 %all_to_all.26.packed_ref = f32[8,16,128]{2,1,0:T(8,128)S(1)} all-to-all(f32[8,16,128]{2,1,0:T(8,128)S(1)} %get-tuple-element.22), channel_id=1, replica_groups={{192,224,0,32,64,96,128,160},{193,225,1,33,65,97,129,161},{194,226,2,34..., dimensions={0} | all-to-all | bytes 131072 | tf_op jit(solution)/shard_map/all_to_all | solution.py:50
  39.3 0.5 terms.1
  39.8 11.5 %all_to_all.27.got_ref = f32[16,9,8,128]{3,2,1,0:T(8,128)S(1)} all-to-all(f32[16,9,8,128]{3,2,1,0:T(8,128)S(1)} %get-tuple-element.24), channel_id=1, replica_groups={{10,14,2,6,11,15,3,7,8,12,0,4,9,13,1,5},{26,30,18,22,27,31,19,23,24,28,..., dimensions={0} | all-to-all | bytes 1179648 | tf_op jit(solution)/shard_map/all_to_all | solution.py:50
  51.4 0.7 columns.1
  52.1 6.7 %all-to-all-start.3 = ((f32[8,8,8,128]{3,2,1,0:T(8,128)}), f32[8,8,8,128]{3,2,1,0:T(8,128)S(1)}, u32[]{:S(2)}, u32[]{:S(2)}) async-start(f32[8,8,8,128]{3,2,1,0:T(8,128)} %get-tuple-element.25), calls=%async_computation.3 | async-start | bytes 524288 | tf_op jit(solution)/shard_map/all_to_all | solution.py:50
  58.8 3.5 %factors.1.factors_ref = f32[96,32]{1,0:T(8,128)S(1)} custom-call(f32[8,128]{1,0:T(8,128)S(1)} %get-tuple-element.26.gram_ref, f32[32,64]{1,0:T(8,128)S(1)} %get-tuple-element.27.left_ref), custom_call_target="tpu_custom_call" | custom-call | tf_op jit(solution)/shard_map/factors/pallas_call | solution.py:25
  62.3 1.1 %all-to-all-done.3.got_ref = f32[8,8,8,128]{3,2,1,0:T(8,128)S(1)} async-done(((f32[8,8,8,128]{3,2,1,0:T(8,128)}), f32[8,8,8,128]{3,2,1,0:T(8,128)S(1)}, u32[]{:S(2)}, u32[]{:S(2)}) %all-to-all-start.3) | async-done | bytes 262176 | tf_op jit(solution)/shard_map/all_to_all | solution.py:50
  63.5 0.3 shard.1
  63.8 14.4 %all_to_all.28.right_ref = f32[16,32,512]{2,1,0:T(8,128)S(1)} all-to-all(f32[16,32,512]{2,1,0:T(8,128)S(1)} %get-tuple-element.28), channel_id=1, replica_groups={{10,14,2,6,11,15,3,7,8,12,0,4,9,13,1,5},{26,30,18,22,27,31,19,23,24,28,..., dimensions={0} | all-to-all | bytes 2097152 | tf_op jit(solution)/shard_map/all_to_all | solution.py:50
  78.2 0.0 copy-start.1
  78.2 7.0 %collective-permute-start.5 = (f32[16,32,512]{2,1,0:T(8,128)S(1)}, f32[16,32,512]{2,1,0:T(8,128)S(1)}, u32[]{:S(2)}, u32[]{:S(2)}) collective-permute-start(f32[16,32,512]{2,1,0:T(8,128)S(1)} %all_to_all.28.right_ref), channel_id=1, source_target_pairs={{0,16},{16,0},{1,17},{17,1},{2,18},{18,2},{3,19},{19,3},{4,20},{20... | collective-permute-start | bytes 3145736 | tf_op jit(solution)/shard_map/ppermute | solution.py:36
  85.2 0.0 collective-permute-start.4
  85.2 2.2 %residual_own.1._ = f32[1,2,64,8192]{3,2,1,0:T(8,128)} custom-call(s32[4]{0:T(128)S(1)} %pad_add_fusion.place_ref, f32[64,8192]{1,0:T(8,128)S(1)} %merge_own.1.own_ref.merged_ref, f32[96,32]{1,0:T(8,128)S(1)} %factors.1.factors_ref, f32[16,32,512]{2,1,0:T(8,128)S(1)} %all_to_all.28.right_ref), custom_call_target="tpu_custom_call" | custom-call | tf_op jit(solution)/shard_map/residual_own/pallas_call | solution.py:25
  87.3 0.2 collective-permute-done.4.factors_ref
  87.5 0.0 collective-permute-done.5.right_ref
  87.5 0.0 copy-done.1
  87.5 2.2 %residual_other.1 = (f32[1,2,64,8192]{3,2,1,0:T(8,128)}, f32[2,32,512]{2,1,0:T(8,128)}) custom-call(s32[4]{0:T(128)S(1)} %pad_add_fusion.place_ref, f32[64,8192]{1,0:T(8,128)S(1)} %copy-done.1, f32[96,32]{1,0:T(8,128)S(1)} %collective-permute-done.4.factors_ref, ...), custom_call_target="tpu_custom_call", output_to_operand_aliasing={{0}: (5, {})} | custom-call | tf_op jit(solution)/shard_map/residual_other/pallas_call | solution.py:25
Async XLA Ops:
  3.4 6.0 %copy-start = (f32[64,8192]{1,0:T(8,128)}, f32[64,8192]{1,0:T(8,128)S(1)}, u32[]{:S(2)}) copy-start(f32[64,8192]{1,0:T(8,128)S(1)} %get-tuple-element.17.merged_ref) | copy-start | bytes 6291460
  3.4 6.0 %collective-permute-start.1 = (f32[64,4096]{1,0:T(8,128)S(1)}, f32[64,4096]{1,0:T(8,128)S(1)}, u32[]{:S(2)}, u32[]{:S(2)}) collective-permute-start(f32[64,4096]{1,0:T(8,128)S(1)} %get-tuple-element.19), channel_id=1, source_target_pairs={{0,16},{16,0},{1,17},{17,1},{2,18},{18,2},{3,19},{19,3},{4,20},{20... | collective-permute-start | bytes 3145736 | tf_op jit(solution)/shard_map/ppermute | solution.py:36
  6.7 7.3 %copy-start.2 = (f32[2,32,512]{2,1,0:T(8,128)S(1)}, f32[2,32,512]{2,1,0:T(8,128)}, u32[]{:S(2)}) copy-start(f32[2,32,512]{2,1,0:T(8,128)} %basis_ref.1) | copy-start | bytes 393220
  6.7 7.3 %collective-permute-start = (f32[64,4096]{1,0:T(8,128)S(1)}, f32[64,4096]{1,0:T(8,128)S(1)}, u32[]{:S(2)}, u32[]{:S(2)}) collective-permute-start(f32[64,4096]{1,0:T(8,128)S(1)} %get-tuple-element.18), channel_id=1, source_target_pairs={{0,16},{16,0},{1,17},{17,1},{2,18},{18,2},{3,19},{19,3},{4,20},{20... | collective-permute-start | bytes 3145736 | tf_op jit(solution)/shard_map/ppermute | solution.py:36
  10.1 18.6 %collective-permute-start.3 = (f32[64,2048]{1,0:T(8,128)S(1)}, f32[64,2048]{1,0:T(8,128)S(1)}, u32[]{:S(2)}, u32[]{:S(2)}) collective-permute-start(f32[64,2048]{1,0:T(8,128)S(1)} %get-tuple-element.21), channel_id=1, source_target_pairs={{0,224},{32,0},{64,32},{96,64},{128,96},{160,128},{192,160},{224,1... | collective-permute-start | bytes 1572872 | tf_op jit(solution)/shard_map/ppermute | solution.py:55
  14.0 14.6 %collective-permute-start.2 = (f32[64,2048]{1,0:T(8,128)S(1)}, f32[64,2048]{1,0:T(8,128)S(1)}, u32[]{:S(2)}, u32[]{:S(2)}) collective-permute-start(f32[64,2048]{1,0:T(8,128)S(1)} %get-tuple-element.20.rest_0_), channel_id=1, source_target_pairs={{0,32},{32,64},{64,96},{96,128},{128,160},{160,192},{192,224},{224... | collective-permute-start | bytes 1572872 | tf_op jit(solution)/shard_map/ppermute | solution.py:55
  52.1 11.4 %all-to-all-start.3 = ((f32[8,8,8,128]{3,2,1,0:T(8,128)}), f32[8,8,8,128]{3,2,1,0:T(8,128)S(1)}, u32[]{:S(2)}, u32[]{:S(2)}) async-start(f32[8,8,8,128]{3,2,1,0:T(8,128)} %get-tuple-element.25), calls=%async_computation.3 | async-start | bytes 524288 | tf_op jit(solution)/shard_map/all_to_all | solution.py:50
  78.2 9.3 %copy-start.1 = (f32[64,8192]{1,0:T(8,128)S(1)}, f32[64,8192]{1,0:T(8,128)}, u32[]{:S(2)}) copy-start(f32[64,8192]{1,0:T(8,128)} %copy-done) | copy-start | bytes 6291460
  78.2 9.3 %collective-permute-start.5 = (f32[16,32,512]{2,1,0:T(8,128)S(1)}, f32[16,32,512]{2,1,0:T(8,128)S(1)}, u32[]{:S(2)}, u32[]{:S(2)}) collective-permute-start(f32[16,32,512]{2,1,0:T(8,128)S(1)} %all_to_all.28.right_ref), channel_id=1, source_target_pairs={{0,16},{16,0},{1,17},{17,1},{2,18},{18,2},{3,19},{19,3},{4,20},{20... | collective-permute-start | bytes 3145736 | tf_op jit(solution)/shard_map/ppermute | solution.py:36
  85.2 2.4 %collective-permute-start.4 = (f32[96,32]{1,0:T(8,128)S(1)}, f32[96,32]{1,0:T(8,128)S(1)}, u32[]{:S(2)}, u32[]{:S(2)}) collective-permute-start(f32[96,32]{1,0:T(8,128)S(1)} %factors.1.factors_ref), channel_id=1, source_target_pairs={{0,16},{16,0},{1,17},{17,1},{2,18},{18,2},{3,19},{19,3},{4,20},{20... | collective-permute-start | bytes 36872 | tf_op jit(solution)/shard_map/ppermute | solution.py:36

commit v10 on v9

--- a/solution.py
+++ b/solution.py
@@ -12,7 +12,6 @@
 HIGH = lax.Precision.HIGHEST
 F = ("y", "x")
 LANES = 128
-SMEM = pl.BlockSpec(memory_space=pltpu.SMEM)
 VMEM = pl.BlockSpec(memory_space=pltpu.VMEM)
 ANY = pl.BlockSpec(memory_space=pl.ANY)
 
@@ -46,6 +45,14 @@
     return [int(i) for i in order.ravel()]
 
 
+def position():
+    (slow, fast) = (
+        lax.rem(lax.axis_index(axis) + lax.axis_size(axis) // 2, lax.axis_size(axis))
+        for axis in ("x", "y")
+    )
+    return slow * lax.axis_size("y") + fast
+
+
 def exchange(pieces, axes):
     return lax.all_to_all(pieces, axes, 0, 0, axis_index_groups=[order_of(axes)])
 
@@ -70,12 +77,20 @@
     return jnp.concatenate([high, high, low], axis=axis)
 
 
-def kept(place_ref):
-    return 3 - 2 * place_ref[3], 2 * place_ref[3]
-
-
-def given(place_ref):
-    return 1 + 2 * place_ref[3], 2 - 2 * place_ref[3]
+def own_index():
+    return lax.axis_index("core")
+
+
+def parity():
+    return lax.rem(lax.axis_index("z"), 2)
+
+
+def kept():
+    return 3 - 2 * parity(), 2 * parity()
+
+
+def given():
+    return 1 + 2 * parity(), 2 - 2 * parity()
 
 
 def quarter(ref, chunk, which):
@@ -121,42 +136,42 @@
     ]
 
 
-def other_kernel(place_ref, grad_ref, error_ref, other_ref, give_ref, keep_ref, *scratch):
+def other_kernel(grad_ref, error_ref, other_ref, give_ref, keep_ref, *scratch):
     def sort(chunks):
-        for out_ref, quarters in ((give_ref, given(place_ref)), (keep_ref, kept(place_ref))):
+        for out_ref, quarters in ((give_ref, given()), (keep_ref, kept())):
             for chunk in chunks:
                 for slot, which in enumerate(quarters):
                     start = (2 * chunk + slot) * LANES
                     out_ref[:, start : start + LANES] = quarter(other_ref, chunk, which)
 
-    merge(place_ref[1], sort, grad_ref, error_ref, other_ref, *scratch)
-
-
-def own_kernel(place_ref, grad_ref, error_ref, own_ref, *scratch):
-    merge(place_ref[0], lambda chunks: None, grad_ref, error_ref, own_ref, *scratch)
-
-
-def give_kernel(place_ref, own_ref, got_ref, *out_refs):
+    merge(1 - own_index(), sort, grad_ref, error_ref, other_ref, *scratch)
+
+
+def own_kernel(grad_ref, error_ref, own_ref, *scratch):
+    merge(own_index(), lambda chunks: None, grad_ref, error_ref, own_ref, *scratch)
+
+
+def give_kernel(own_ref, got_ref, *out_refs):
     for chunk in range(own_ref.shape[1] // (4 * LANES)):
-        for slot, (out_ref, which) in enumerate(zip(out_refs, given(place_ref))):
+        for slot, (out_ref, which) in enumerate(zip(out_refs, given())):
             start = chunk * LANES
             out_ref[:, start : start + LANES] = quarter(own_ref, chunk, which) + half(
                 got_ref, chunk, slot
             )
 
 
-def basis_kernel(place_ref, basis_ref, *rest):
+def basis_kernel(basis_ref, *rest):
     copies_ref = rest[-1]
     columns = [
-        basis_ref[place_ref[0], :, pl.ds(pl.multiple_of(which * LANES, LANES), LANES)]
-        for which in kept(place_ref)
+        basis_ref[own_index(), :, pl.ds(pl.multiple_of(which * LANES, LANES), LANES)]
+        for which in kept()
     ]
     chunk = jnp.concatenate(columns, axis=1)
     for copy in range(copies_ref.shape[0]):
         copies_ref[copy] = chunk
 
 
-def left_kernel(turn, place_ref, own_ref, got_ref, up_ref, down_ref, basis_ref, copies_ref, values_ref):
+def left_kernel(turn, own_ref, got_ref, up_ref, down_ref, basis_ref, copies_ref, values_ref):
     parts = []
     for chunk in range(basis_ref.shape[0]):
         start = chunk * LANES
@@ -164,7 +179,7 @@
             quarter(own_ref, chunk, which)
             + half(got_ref, chunk, slot)
             + z_ref[:, start : start + LANES]
-            for slot, (which, z_ref) in enumerate(zip(kept(place_ref), (up_ref, down_ref)))
+            for slot, (which, z_ref) in enumerate(zip(kept(), (up_ref, down_ref)))
         ]
         values = jnp.concatenate(sums, axis=1)
         values_ref[:, 2 * start : 2 * start + 2 * LANES] = values
@@ -286,24 +301,24 @@
     return copies
 
 
-def own_residual_kernel(turn, place_ref, merged_ref, factors_ref, right_ref, out_ref, *scratch):
-    copies = subtract_out(turn, place_ref[0], merged_ref, factors_ref, right_ref, out_ref, *scratch)
+def own_residual_kernel(turn, merged_ref, factors_ref, right_ref, out_ref, *scratch):
+    copies = subtract_out(turn, own_index(), merged_ref, factors_ref, right_ref, out_ref, *scratch)
     for copy in copies:
         copy.wait()
 
 
 def other_residual_kernel(
-    turn, scale, place_ref, merged_ref, factors_ref, right_ref, shard_ref, _,
+    turn, scale, merged_ref, factors_ref, right_ref, shard_ref, _,
     out_ref, basis_ref, buffer, sems, basis_buffer, basis_sem,
 ):
     copies = subtract_out(
-        turn, place_ref[1], merged_ref, factors_ref, right_ref, out_ref, buffer, sems
+        turn, 1 - own_index(), merged_ref, factors_ref, right_ref, out_ref, buffer, sems
     )
     rank = right_ref.shape[1]
-    basis_buffer[place_ref[0]] = shard_ref[...]
-    basis_buffer[place_ref[1]] = scale * jnp.dot(
+    basis_buffer[own_index()] = shard_ref[...]
+    basis_buffer[1 - own_index()] = scale * jnp.dot(
         factors_ref[-rank:, :],
-        right_ref[place_ref[2]],
+        right_ref[position()],
         precision=HIGH,
         preferred_element_type=jnp.float32,
     )
@@ -314,15 +329,12 @@
 
 
 def on_device(grad_pair, error_pair, basis_pair):
-    core = lax.axis_index("core")
     zs = lax.axis_size("z")
     scale = 1.0 / (lax.axis_size("core") * zs)
     pair, rows, width = grad_pair.shape[1:]
     rank, part = basis_pair.shape[1:]
     shards = width // part
     turn = [order_of(F).index(i) for i in range(shards)]
-    position = sum(jnp.where(lax.axis_index(F) == i, turn[i], 0) for i in range(shards))
-    place = jnp.stack([core, 1 - core, position, lax.axis_index("z") % 2])
 
     inputs = [
         pltpu.with_memory_space_constraint(array, pltpu.HBM) for array in (grad_pair, error_pair)
@@ -331,26 +343,26 @@
     by_two, by_four = f32(rows, width // 2), f32(rows, width // 4)
 
     other, give, keep = call(
-        other_kernel, "merge_other", [SMEM, ANY, ANY], (f32(rows, width), by_two, by_two),
-        (place, *inputs), out_specs=(VMEM, VMEM, VMEM), **merging,
+        other_kernel, "merge_other", [ANY, ANY], (f32(rows, width), by_two, by_two),
+        inputs, out_specs=(VMEM, VMEM, VMEM), **merging,
     )
     give, keep = swap(give), swap(keep)
     own = call(
-        own_kernel, "merge_own", [SMEM, ANY, ANY], f32(rows, width),
-        (place, *inputs), out_specs=VMEM, **merging,
+        own_kernel, "merge_own", [ANY, ANY], f32(rows, width),
+        inputs, out_specs=VMEM, **merging,
     )
     up, down = call(
-        give_kernel, "give", [SMEM, VMEM, VMEM], (by_four, by_four), (place, own, give)
+        give_kernel, "give", [VMEM, VMEM], (by_four, by_four), (own, give)
     )
     copies = call(
-        basis_kernel, "basis", [SMEM, VMEM, ANY, ANY], f32(shards, rank, part // 2),
-        (place, basis_pair, up, keep),
+        basis_kernel, "basis", [VMEM, ANY, ANY], f32(shards, rank, part // 2),
+        (basis_pair, up, keep),
     )
     up, down = shift(up, 1), shift(down, -1)
     basis = exchange(copies, F)
     copies, values = call(
-        functools.partial(left_kernel, turn), "left", [SMEM] + [VMEM] * 5, (f32(zs, rank // 2, 2 * rows), by_two),
-        (place, own, keep, up, down, basis),
+        functools.partial(left_kernel, turn), "left", [VMEM] * 5, (f32(zs, rank // 2, 2 * rows), by_two),
+        (own, keep, up, down, basis),
     )
     sent, left = call(
         functools.partial(terms_kernel, turn), "terms", [VMEM, VMEM], (f32(shards, rank // 4 + 1, 8, LANES), f32(rank, rows)),
@@ -375,17 +387,17 @@
     residual_scratch = [pltpu.VMEM((rows, width), jnp.float32), pltpu.SemaphoreType.DMA((4,))]
     residual_shape = f32(1, pair, rows, width)
     residual = call(
-        functools.partial(own_residual_kernel, turn), "residual_own", [SMEM, VMEM, VMEM, VMEM], residual_shape,
-        (place, own, factors, whole), out_specs=ANY, scratch_shapes=residual_scratch,
+        functools.partial(own_residual_kernel, turn), "residual_own", [VMEM] * 3, residual_shape,
+        (own, factors, whole), out_specs=ANY, scratch_shapes=residual_scratch,
     )
     return call(
         functools.partial(other_residual_kernel, turn, scale), "residual_other",
-        [SMEM, VMEM, VMEM, VMEM, VMEM, ANY], (residual_shape, f32(pair, rank, part)),
-        (place, other, other_factors, other_whole, shard, residual),
+        [VMEM] * 4 + [ANY], (residual_shape, f32(pair, rank, part)),
+        (other, other_factors, other_whole, shard, residual),
         out_specs=(ANY, ANY),
         scratch_shapes=residual_scratch
         + [pltpu.VMEM((pair, rank, part), jnp.float32), pltpu.SemaphoreType.DMA],
-        input_output_aliases={5: 0},
+        input_output_aliases={4: 0},
     )
 
 

time: 90.1 us -> 87.2 us (0.968)
  Pallas kernels: 17.2 us -> 13.4 us
    pallas_call x11, Pallas kernels: 17.2 us -> 13.4 us  [call(): pl.pallas_call(kernel, in_specs=in_specs, out_shape=out_shape, compiler_p...]
  transfers between devices with their start and end apart: 7 -> 7, of which waited for: 2 -> 3; matrix products, arithmetic and copies ran while one was open for 0% -> 0% of each run, Pallas kernels for 11% -> 8%
where the time goes in v10:
time: 87.2 us; the launch traced here: 86.9 us
  blocking collectives  49.8 us (57%)
  starting transfers between devices  20.9 us (24%)
  Pallas kernels  13.4 us (15%)
  waiting for transfers between devices  2.07 us (2%)
    all_to_all x4, blocking collectives, exchange(): lax.all_to_all(pieces, axes, 0, 0, axis_index_groups=[order_of(axes)])  49.8 us
    pallas_call x11, Pallas kernels, call(): pl.pallas_call(kernel, in_specs=in_specs, out_shape=out_shape, compiler_p...  13.4 us
    ppermute x4, starting transfers between devices, swap(): return lax.ppermute(value, 'core', [(0, 1), (1, 0)])  10.3 us
    all_to_all x1, starting transfers between devices, exchange(): lax.all_to_all(pieces, axes, 0, 0, axis_index_groups=[order_of(axes)])  6.7 us
    ppermute x2, starting transfers between devices, shift(): lax.ppermute(value, 'z', [(i, (i + step) % count) for i in range(count)])  3.91 us
  transfers between devices with their start and end apart: 7, of which 3 were waited for; matrix products, arithmetic and copies ran while one was open for 0% of the time, Pallas kernels for 8%

profile of v10, /device:TPU:1, one launch (start us, length us, event | category | flops | bytes accessed | tf_op | source)
XLA Modules:
  0.0 86.9 jit_solution(2444699050109674375)
XLA Ops:
  0.6 2.1 %merge_other.1 = (f32[64,8192]{1,0:T(8,128)S(1)}, f32[64,4096]{1,0:T(8,128)S(1)}, f32[64,4096]{1,0:T(8,128)S(1)}) custom-call(bf16[1,2,64,8192]{3,2,1,0:T(8,128)(2,1)} %grad_ref.3, f32[1,2,64,8192]{3,2,1,0:T(8,128)} %error_ref.3), custom_call_target="tpu_custom_call" | custom-call | tf_op jit(solution)/shard_map/merge_other/pallas_call | solution.py:24
  2.7 0.0 copy-start
  2.7 3.3 %collective-permute-start.1 = (f32[64,4096]{1,0:T(8,128)S(1)}, f32[64,4096]{1,0:T(8,128)S(1)}, u32[]{:S(2)}, u32[]{:S(2)}) collective-permute-start(f32[64,4096]{1,0:T(8,128)S(1)} %get-tuple-element.19), channel_id=1, source_target_pairs={{0,16},{16,0},{1,17},{17,1},{2,18},{18,2},{3,19},{19,3},{4,20},{20... | collective-permute-start | bytes 3145736 | tf_op jit(solution)/shard_map/ppermute | solution.py:35
  6.0 0.0 copy-start.2
  6.0 0.1 collective-permute-start
  6.1 1.9 %merge_own.1.own_ref.merged_ref = f32[64,8192]{1,0:T(8,128)S(1)} custom-call(bf16[1,2,64,8192]{3,2,1,0:T(8,128)(2,1)} %grad_ref.3, f32[1,2,64,8192]{3,2,1,0:T(8,128)} %error_ref.3), custom_call_target="tpu_custom_call" | custom-call | tf_op jit(solution)/shard_map/merge_own/pallas_call | solution.py:24
  8.1 0.0 copy-done
  8.1 0.2 collective-permute-done.1.got_ref
  8.3 0.2 give.1
  8.5 3.9 %collective-permute-start.3 = (f32[64,2048]{1,0:T(8,128)S(1)}, f32[64,2048]{1,0:T(8,128)S(1)}, u32[]{:S(2)}, u32[]{:S(2)}) collective-permute-start(f32[64,2048]{1,0:T(8,128)S(1)} %get-tuple-element.21), channel_id=1, source_target_pairs={{0,224},{32,0},{64,32},{96,64},{128,96},{160,128},{192,160},{224,1... | collective-permute-start | bytes 1572872 | tf_op jit(solution)/shard_map/ppermute | solution.py:62
  12.4 0.0 collective-permute-start.2
  12.4 0.0 collective-permute-done.rest_1_.got_ref
  12.4 0.0 copy-done.2
  12.4 0.1 basis.1
  12.5 14.0 %all_to_all.25.basis_ref = f32[16,32,256]{2,1,0:T(8,128)S(1)} all-to-all(f32[16,32,256]{2,1,0:T(8,128)S(1)} %basis.1), channel_id=1, replica_groups={{10,14,2,6,11,15,3,7,8,12,0,4,9,13,1,5},{26,30,18,22,27,31,19,23,24,28,..., dimensions={0} | all-to-all | bytes 1048576 | tf_op jit(solution)/shard_map/all_to_all | solution.py:57
  26.5 0.0 collective-permute-done.3.down_ref
  26.5 0.0 collective-permute-done.2.up_ref
  26.5 0.7 left.1
  27.3 9.3 %all_to_all.26.packed_ref = f32[8,16,128]{2,1,0:T(8,128)S(1)} all-to-all(f32[8,16,128]{2,1,0:T(8,128)S(1)} %get-tuple-element.22), channel_id=1, replica_groups={{192,224,0,32,64,96,128,160},{193,225,1,33,65,97,129,161},{194,226,2,34..., dimensions={0} | all-to-all | bytes 131072 | tf_op jit(solution)/shard_map/all_to_all | solution.py:57
  36.6 0.5 terms.1
  37.1 12.1 %all_to_all.27.got_ref = f32[16,9,8,128]{3,2,1,0:T(8,128)S(1)} all-to-all(f32[16,9,8,128]{3,2,1,0:T(8,128)S(1)} %get-tuple-element.24), channel_id=1, replica_groups={{10,14,2,6,11,15,3,7,8,12,0,4,9,13,1,5},{26,30,18,22,27,31,19,23,24,28,..., dimensions={0} | all-to-all | bytes 1179648 | tf_op jit(solution)/shard_map/all_to_all | solution.py:57
  49.2 0.7 columns.1
  49.9 6.7 %all-to-all-start.3 = ((f32[8,8,8,128]{3,2,1,0:T(8,128)}), f32[8,8,8,128]{3,2,1,0:T(8,128)S(1)}, u32[]{:S(2)}, u32[]{:S(2)}) async-start(f32[8,8,8,128]{3,2,1,0:T(8,128)} %get-tuple-element.25), calls=%async_computation.3 | async-start | bytes 524288 | tf_op jit(solution)/shard_map/all_to_all | solution.py:57
  56.6 3.5 %factors.1.factors_ref = f32[96,32]{1,0:T(8,128)S(1)} custom-call(f32[8,128]{1,0:T(8,128)S(1)} %get-tuple-element.26.gram_ref, f32[32,64]{1,0:T(8,128)S(1)} %get-tuple-element.27.left_ref), custom_call_target="tpu_custom_call" | custom-call | tf_op jit(solution)/shard_map/factors/pallas_call | solution.py:24
  60.2 1.1 %all-to-all-done.3.got_ref = f32[8,8,8,128]{3,2,1,0:T(8,128)S(1)} async-done(((f32[8,8,8,128]{3,2,1,0:T(8,128)}), f32[8,8,8,128]{3,2,1,0:T(8,128)S(1)}, u32[]{:S(2)}, u32[]{:S(2)}) %all-to-all-start.3) | async-done | bytes 262176 | tf_op jit(solution)/shard_map/all_to_all | solution.py:57
  61.3 0.3 shard.1
  61.6 14.4 %all_to_all.28.right_ref = f32[16,32,512]{2,1,0:T(8,128)S(1)} all-to-all(f32[16,32,512]{2,1,0:T(8,128)S(1)} %get-tuple-element.28), channel_id=1, replica_groups={{10,14,2,6,11,15,3,7,8,12,0,4,9,13,1,5},{26,30,18,22,27,31,19,23,24,28,..., dimensions={0} | all-to-all | bytes 2097152 | tf_op jit(solution)/shard_map/all_to_all | solution.py:57
  76.0 0.0 copy-start.1
  76.0 6.9 %collective-permute-start.5 = (f32[16,32,512]{2,1,0:T(8,128)S(1)}, f32[16,32,512]{2,1,0:T(8,128)S(1)}, u32[]{:S(2)}, u32[]{:S(2)}) collective-permute-start(f32[16,32,512]{2,1,0:T(8,128)S(1)} %all_to_all.28.right_ref), channel_id=1, source_target_pairs={{0,16},{16,0},{1,17},{17,1},{2,18},{18,2},{3,19},{19,3},{4,20},{20... | collective-permute-start | bytes 3145736 | tf_op jit(solution)/shard_map/ppermute | solution.py:35
  82.8 0.0 collective-permute-start.4
  82.8 1.6 %residual_own.1._ = f32[1,2,64,8192]{3,2,1,0:T(8,128)} custom-call(f32[64,8192]{1,0:T(8,128)S(1)} %merge_own.1.own_ref.merged_ref, f32[96,32]{1,0:T(8,128)S(1)} %factors.1.factors_ref, f32[16,32,512]{2,1,0:T(8,128)S(1)} %all_to_all.28.right_ref), custom_call_target="tpu_custom_call" | custom-call | tf_op jit(solution)/shard_map/residual_own/pallas_call | solution.py:24
  84.5 0.7 collective-permute-done.4.factors_ref
  85.2 0.0 collective-permute-done.5.right_ref
  85.2 0.0 copy-done.1
  85.2 1.7 %residual_other.1 = (f32[1,2,64,8192]{3,2,1,0:T(8,128)}, f32[2,32,512]{2,1,0:T(8,128)}) custom-call(f32[64,8192]{1,0:T(8,128)S(1)} %copy-done.1, f32[96,32]{1,0:T(8,128)S(1)} %collective-permute-done.4.factors_ref, f32[16,32,512]{2,1,0:T(8,128)S(1)} %collective-permute-done.5.right_ref, ...), custom_call_target="tpu_custom_call", output_to_operand_aliasing={{0}: (4, {})} | custom-call | tf_op jit(solution)/shard_map/residual_other/pallas_call | solution.py:24
Async XLA Ops:
  2.7 5.4 %copy-start = (f32[64,8192]{1,0:T(8,128)}, f32[64,8192]{1,0:T(8,128)S(1)}, u32[]{:S(2)}) copy-start(f32[64,8192]{1,0:T(8,128)S(1)} %get-tuple-element.17.merged_ref) | copy-start | bytes 6291460
  2.7 5.6 %collective-permute-start.1 = (f32[64,4096]{1,0:T(8,128)S(1)}, f32[64,4096]{1,0:T(8,128)S(1)}, u32[]{:S(2)}, u32[]{:S(2)}) collective-permute-start(f32[64,4096]{1,0:T(8,128)S(1)} %get-tuple-element.19), channel_id=1, source_target_pairs={{0,16},{16,0},{1,17},{17,1},{2,18},{18,2},{3,19},{19,3},{4,20},{20... | collective-permute-start | bytes 3145736 | tf_op jit(solution)/shard_map/ppermute | solution.py:35
  6.0 6.4 %copy-start.2 = (f32[2,32,512]{2,1,0:T(8,128)S(1)}, f32[2,32,512]{2,1,0:T(8,128)}, u32[]{:S(2)}) copy-start(f32[2,32,512]{2,1,0:T(8,128)} %basis_ref.1) | copy-start | bytes 393220
  6.0 6.4 %collective-permute-start = (f32[64,4096]{1,0:T(8,128)S(1)}, f32[64,4096]{1,0:T(8,128)S(1)}, u32[]{:S(2)}, u32[]{:S(2)}) collective-permute-start(f32[64,4096]{1,0:T(8,128)S(1)} %get-tuple-element.18), channel_id=1, source_target_pairs={{0,16},{16,0},{1,17},{17,1},{2,18},{18,2},{3,19},{19,3},{4,20},{20... | collective-permute-start | bytes 3145736 | tf_op jit(solution)/shard_map/ppermute | solution.py:35
  8.5 18.0 %collective-permute-start.3 = (f32[64,2048]{1,0:T(8,128)S(1)}, f32[64,2048]{1,0:T(8,128)S(1)}, u32[]{:S(2)}, u32[]{:S(2)}) collective-permute-start(f32[64,2048]{1,0:T(8,128)S(1)} %get-tuple-element.21), channel_id=1, source_target_pairs={{0,224},{32,0},{64,32},{96,64},{128,96},{160,128},{192,160},{224,1... | collective-permute-start | bytes 1572872 | tf_op jit(solution)/shard_map/ppermute | solution.py:62
  12.4 14.1 %collective-permute-start.2 = (f32[64,2048]{1,0:T(8,128)S(1)}, f32[64,2048]{1,0:T(8,128)S(1)}, u32[]{:S(2)}, u32[]{:S(2)}) collective-permute-start(f32[64,2048]{1,0:T(8,128)S(1)} %get-tuple-element.20.rest_0_), channel_id=1, source_target_pairs={{0,32},{32,64},{64,96},{96,128},{128,160},{160,192},{192,224},{224... | collective-permute-start | bytes 1572872 | tf_op jit(solution)/shard_map/ppermute | solution.py:62
  49.9 11.4 %all-to-all-start.3 = ((f32[8,8,8,128]{3,2,1,0:T(8,128)}), f32[8,8,8,128]{3,2,1,0:T(8,128)S(1)}, u32[]{:S(2)}, u32[]{:S(2)}) async-start(f32[8,8,8,128]{3,2,1,0:T(8,128)} %get-tuple-element.25), calls=%async_computation.3 | async-start | bytes 524288 | tf_op jit(solution)/shard_map/all_to_all | solution.py:57
  76.0 9.2 %copy-start.1 = (f32[64,8192]{1,0:T(8,128)S(1)}, f32[64,8192]{1,0:T(8,128)}, u32[]{:S(2)}) copy-start(f32[64,8192]{1,0:T(8,128)} %copy-done) | copy-start | bytes 6291460
  76.0 9.2 %collective-permute-start.5 = (f32[16,32,512]{2,1,0:T(8,128)S(1)}, f32[16,32,512]{2,1,0:T(8,128)S(1)}, u32[]{:S(2)}, u32[]{:S(2)}) collective-permute-start(f32[16,32,512]{2,1,0:T(8,128)S(1)} %all_to_all.28.right_ref), channel_id=1, source_target_pairs={{0,16},{16,0},{1,17},{17,1},{2,18},{18,2},{3,19},{19,3},{4,20},{20... | collective-permute-start | bytes 3145736 | tf_op jit(solution)/shard_map/ppermute | solution.py:35
  82.8 2.4 %collective-permute-start.4 = (f32[96,32]{1,0:T(8,128)S(1)}, f32[96,32]{1,0:T(8,128)S(1)}, u32[]{:S(2)}, u32[]{:S(2)}) collective-permute-start(f32[96,32]{1,0:T(8,128)S(1)} %factors.1.factors_ref), channel_id=1, source_target_pairs={{0,16},{16,0},{1,17},{17,1},{2,18},{18,2},{3,19},{19,3},{4,20},{20... | collective-permute-start | bytes 36872 | tf_op jit(solution)/shard_map/ppermute | solution.py:35
